TPU v7x, 32 devices: a whole 2x2x4 slice. The times are simulated.
32 devices in a mesh: cfg: 2 (over y), ta: 8 (over z, x), sa: 2 (over core).
Axes of the slice: x: 2, y: 2, z: 4, core: 2. Of those that a mesh axis runs over, the one named last changes fastest.
Arguments:
- forward: bfloat16 [32, 2, 256, 2, 256], P(('cfg', 'ta'), 'sa'), parts along dimension 0, may hold values from -6 to 6
- backward: bfloat16 [4, 16, 256, 2, 256], P(('cfg', 'sa'), 'ta'), parts along dimension 0, may hold values from -6 to 6
- sink_bank: bfloat16 [32, 9, 256, 2, 256], P(('cfg', 'ta'), None, 'sa'), parts along dimension 0, may hold values from -0.25 to 0.25
- source_bank: bfloat16 [4, 9, 256, 2, 256], P(('cfg', 'sa'), None, 'ta'), parts along dimension 0, may hold values from -0.25 to 0.25
- op_mom: int32 [4], replicated, may hold values from 0 to 2
- op_disp: int32 [4], replicated, may hold values from 0 to 2
Outputs:
- correlator: float32 [32, 2, 2, 4, 4], P(('cfg', 'ta'), 'sa'), parts along dimension 0
There are 2 independent parts, one for each index of `cfg`. A program takes and returns all parts, laid end to end along the dimension named above; an argument that names none is the same for every part. Nothing has to cross between parts.
All inputs are finite; a program needn't handle non-finite values.
Results may differ from a plain program's by a relative error of at most 0.0029.
Values may be sent and summed in bfloat16 or wider, within the bound.
No kernel may reach another device: no remote copies, remote signals or barrier semaphores. Data moves between devices by JAX's collectives and lax.ppermute only.
A program may use at most 64 MiB of HBM per device.

v0:
```python
import jax
import jax.numpy as jnp
from jax import lax
from jax.sharding import PartitionSpec as P

NDISP = 3
NBANK = 9


def select_ops(bank, op_mom, op_disp):
    wanted = op_mom * NDISP + op_disp
    onehot = (wanted[:, None] == jnp.arange(NBANK, dtype=jnp.int32)[None, :]).astype(jnp.bfloat16)
    chosen = jnp.einsum("ak,tkrcp->tarcp", onehot, bank, preferred_element_type=jnp.float32)
    return chosen.astype(jnp.bfloat16)


def sink_factor(forward_local):
    real_part = forward_local[:, :, 0, :]
    imag_part = forward_local[:, :, 1, :]
    upper = jnp.concatenate([real_part, imag_part], axis=2)
    lower = jnp.concatenate([-imag_part, real_part], axis=2)
    return jnp.concatenate([upper, lower], axis=1)


def sink_product(factor, chosen):
    merged = chosen.reshape(chosen.shape[0], chosen.shape[1], chosen.shape[2], -1)
    result = jnp.einsum("tarv,tvw->tarw", merged, factor, preferred_element_type=jnp.float32)
    return result.astype(jnp.bfloat16)


def source_columns(stacked_back, chosen):
    real_part = chosen[:, :, 0, :]
    imag_part = chosen[:, :, 1, :]
    for_real = jnp.concatenate([real_part, -imag_part], axis=2)
    for_imag = jnp.concatenate([imag_part, real_part], axis=2)
    joined = jnp.stack([for_real, for_imag], axis=0)
    return jnp.einsum("tui,xaju->taxij", stacked_back, joined, preferred_element_type=jnp.float32)


def per_device(forward, backward, sink_bank, source_bank, op_mom, op_disp):
    factor = sink_factor(forward[:, 0])
    back_local = backward[0]
    stacked_back = jnp.concatenate([back_local[:, :, 0, :], back_local[:, :, 1, :]], axis=1)
    sink_local = select_ops(sink_bank, op_mom, op_disp)
    source_local = select_ops(source_bank, op_mom, op_disp)
    product = sink_product(factor, lax.all_gather(sink_local, "sa", axis=2, tiled=True))
    reverse = source_columns(
        stacked_back, lax.all_gather(source_local, "ta", axis=2, tiled=True)[0]
    )
    order = product.shape[2]
    reshaped = product.reshape(product.shape[0], product.shape[1], order, 2, order)
    paired = jnp.einsum(
        "taicj,tbdij->tabcd",
        reshaped,
        reverse,
        preferred_element_type=jnp.float32,
        precision=lax.Precision.HIGHEST,
    )
    real_trace = paired[..., 0, 0] - paired[..., 1, 1]
    imag_trace = paired[..., 0, 1] + paired[..., 1, 0]
    correlator = jnp.stack([real_trace, imag_trace], axis=1) / order
    return correlator[:, None]


def solution(mesh):
    placed = (
        P(("cfg", "ta"), "sa", None, None, None),
        P(("cfg", "sa"), "ta", None, None, None),
        P(("cfg", "ta"), None, "sa", None, None),
        P(("cfg", "sa"), None, "ta", None, None),
        P(),
        P(),
    )
    return jax.shard_map(
        per_device,
        mesh=mesh,
        in_specs=placed,
        out_specs=P(("cfg", "ta"), "sa", None, None, None),
        check_vma=False,
    )
```

profile of v0, /device:TPU:0, one launch (start us, length us, event | category | flops | bytes accessed | tf_op | source)
XLA Modules:
  0.0 118.8 jit_solution(14901242579871128287)
XLA Ops:
  6.5 0.8 multiply_add_fusion
  7.4 1.9 %fusion.12 = bf16[1,4,32,2,256]{4,1,3,0,2:T(4,128)(2,1)} fusion(bf16[9,32,2,256]{3,2,1,0:T(2,128)(2,1)} %bitcast.90, s32[4]{0:T(128)S(1)} %multiply_add_fusion), kind=kOutput, calls=%fused_computation.12 | convolution fusion | flops 1245220 | bytes 426000 | tf_op jit(solution)/shard_map/ak,tkrcp->tarcp/dot_general | solution.py:13
  9.3 0.0 all-gather.5.cloned.1.call-start
  9.4 2.6 %fusion.9 = bf16[2,4,128,2,256]{4,1,3,2,0:T(4,128)(2,1)} fusion(bf16[2,9,128,2,256]{4,3,2,1,0:T(2,128)(2,1)S(1)} %copy-done, s32[4]{0:T(128)S(1)} %multiply_add_fusion), kind=kOutput, calls=%fused_computation.10 | convolution fusion | flops 9961508 | bytes 3407888 | tf_op jit(solution)/shard_map/ak,tkrcp->tarcp/dot_general | solution.py:13
  12.0 0.0 all-gather.5.cloned.1.call-update
  12.0 0.1 copy.66
  12.1 0.9 copy-done.2
  13.0 0.1 copy.65
  13.1 0.8 slice_bitcast_fusion.5
  13.9 38.5 %all-gather.3.cloned.1.call-done = bf16[1,4,256,2,256]{4,1,3,0,2:T(4,128)(2,1)} async-done(((bf16[1,4,32,2,256]{4,1,3,0,2:T(4,128)(2,1)}), bf16[1,4,256,2,256]{4,1,3,0,2:T(4,128)(2,1)}) %all-gather.3.cloned.1.call-update) | async-done | bytes 1048592 | tf_op jit(solution)/shard_map/all_gather | solution.py:48
  52.4 1.4 %copy.64 = bf16[1,4,256,2,256]{4,2,1,3,0:T(8,128)(2,1)S(1)} copy(bf16[1,4,256,2,256]{4,1,3,0,2:T(4,128)(2,1)} %all-gather.3.cloned.1.call-done) | data formatting | bytes 2097152 | tf_op jit(solution)/shard_map/all_gather | solution.py:48
  53.8 0.1 slice_bitcast_fusion
  53.9 0.2 maximum_bitcast_fusion.2
  54.1 0.8 copy-done.3
  54.9 3.2 %convolution_bitcast_fusion = f32[2,4,2,256,256,1]{3,4,0,1,2,5:T(8,128)} fusion(bf16[1,4,256,512]{3,2,1,0:T(8,128)(2,1)S(1)} %get-tuple-element.12, bf16[1,4,256,512]{3,2,1,0:T(8,128)(2,1)S(1)} %get-tuple-element.11, bf16[2,256,256]{2,1,0:T(8,128)(2,1)S(1)} %copy-done.3, bf16[2,256,256]{2,1,0:T(8,128)(2,1)S(1)} %get-tuple-element.9), kind=kOutput, calls=%fused_computation.2 | convolution fusion | flops 1078984704 | bytes 6815744 | tf_op jit(solution)/shard_map/tui,xaju->taxij/dot_general | solution.py:37
  58.1 5.7 %copy.46 = f32[2,4,2,256,256,1]{4,1,3,5,2,0:T(4,128)} copy(f32[2,4,2,256,256,1]{3,4,0,1,2,5:T(8,128)} %convolution_bitcast_fusion) | data formatting | bytes 8388608 | tf_op jit(solution)/shard_map/tui,xaju->taxij/transpose | solution.py:37
  63.8 4.3 %copy.32 = bf16[2,4,256,2,256]{2,4,3,1,0:T(8,128)(2,1)} copy(bf16[2,4,256,2,256]{4,1,3,2,0:T(4,128)(2,1)} %all-gather.5.cloned.1.call-done) | data formatting | bytes 4194304 | tf_op jit(solution)/shard_map/all_gather | solution.py:46
  68.1 4.2 %convolution_convert_fusion = bf16[2,4,256,512]{3,2,1,0:T(8,128)(2,1)} fusion(bf16[2,4,256,512]{2,3,1,0:T(8,128)(2,1)} %bitcast.88, bf16[2,256,256]{2,1,0:T(8,128)(2,1)S(1)} %get-tuple-element.8, bf16[2,256,256]{2,1,0:T(8,128)(2,1)S(1)} %fusion.30, bf16[2,256,256]{2,1,0:T(8,128)(2,1)S(1)} %get-tuple-element.7), kind=kOutput, calls=%fused_computation.8 | convolution fusion | flops 1078984704 | bytes 4980736 | tf_op jit(solution)/shard_map/tarv,tvw->tarw/dot_general | solution.py:27
  72.3 4.0 %reshape.93 = bf16[2,4,256,2,256]{4,3,2,1,0:T(2,128)(2,1)} reshape(bf16[2,4,256,512]{3,2,1,0:T(8,128)(2,1)} %convolution_convert_fusion) | data formatting | bytes 4194304 | tf_op jit(solution)/shard_map/reshape | solution.py:51
  76.3 34.7 %fusion.4 = f32[2,4,2,4,2,1]{1,4,5,3,2,0:T(2,128)S(1)} fusion(f32[2,4,2,256,256,1]{4,1,3,5,2,0:T(4,128)} %copy.46, bf16[2,4,256,2,256]{4,3,2,1,0:T(2,128)(2,1)} %reshape.93), kind=kOutput, calls=%fused_computation.6 | convolution fusion | flops 100663296 | bytes 6291968 | tf_op jit(solution)/shard_map/taicj,tbdij->tabcd/dot_general | solution.py:52
  111.0 0.1 copy.48
  111.2 0.1 copy.38
  111.3 0.1 copy.37
  111.4 0.6 copy.39
  (14 shorter events, 0.1 us)
Async XLA Ops:
  6.5 2.8 %copy-start = (bf16[2,9,128,2,256]{4,3,2,1,0:T(2,128)(2,1)S(1)}, bf16[2,9,128,2,256]{4,3,2,1,0:T(2,128)(2,1)}, u32[]{:S(2)}) copy-start(bf16[2,9,128,2,256]{4,3,2,1,0:T(2,128)(2,1)} %param.8) | copy-start | bytes 7077892
  6.5 45.8 %all-gather.3.cloned.1.call-start = ((), (), s32[]{:S(2)}) async-start(), calls=%async_computation | async-start | bytes 1179648 | tf_op jit(solution)/shard_map/all_gather | solution.py:48
  9.3 2.7 %copy-start.1 = (bf16[1,2,256,2,256]{4,3,2,1,0:T(2,128)(2,1)S(1)}, bf16[1,2,256,2,256]{4,3,2,1,0:T(2,128)(2,1)}, u32[]{:S(2)}) copy-start(bf16[1,2,256,2,256]{4,3,2,1,0:T(2,128)(2,1)} %param.7) | copy-start | bytes 1572868
  9.3 54.4 %all-gather.5.cloned.1.call-start = ((), (), s32[]{:S(2)}) async-start(), calls=%async_computation.1 | async-start | bytes 3145728 | tf_op jit(solution)/shard_map/all_gather | solution.py:46
  12.0 1.0 copy-start.2
  53.9 1.0 copy-start.3
Sparse Core Ops, SparseCore 0:
  9.5 42.8 all-gather.2
  53.9 9.3 all-gather.4
where the time goes:
time: 119 us
  matrix products  46.7 us (39%)
  waiting for transfers between devices  38.5 us (32%)
  local copies, waits for them, and re-layouts  19 us (16%)
  between operations  13.5 us (11%)
    all_gather x1, waiting for transfers between devices, per_device(): lax.all_gather(source_local, 'ta', axis=2, tiled=True)[0]  38.5 us
    dot_general x1, matrix products, per_device(): jnp.einsum('taicj,tbdij->tabcd', reshaped, reverse, preferred_element_typ...  34.7 us
    transpose x1, local copies, waits for them, and re-layouts, source_columns(): jnp.einsum('tui,xaju->taxij', stacked_back, joined, preferred_element_typ...  5.66 us
    dot_general x2, matrix products, select_ops(): jnp.einsum('ak,tkrcp->tarcp', onehot, bank, preferred_element_type=jnp.fl...  4.49 us
    all_gather x1, local copies, waits for them, and re-layouts, per_device(): lax.all_gather(sink_local, 'sa', axis=2, tiled=True)  4.32 us
    dot_general x1, matrix products, sink_product(): jnp.einsum('tarv,tvw->tarw', merged, factor, preferred_element_type=jnp.f...  4.23 us
    reshape x1, local copies, waits for them, and re-layouts, per_device(): product.reshape(product.shape[0], product.shape[1], order, 2, order)  3.98 us
    dot_general x1, matrix products, source_columns(): jnp.einsum('tui,xaju->taxij', stacked_back, joined, preferred_element_typ...  3.22 us
  transfers between devices with their start and end apart: 2, of which 1 were waited for; matrix products, arithmetic and copies ran while one was open for 12% of the time, Pallas kernels for 0%

commit v1 on v0

v1 whole, which is shorter than its diff:
```python
import functools

import jax
import jax.numpy as jnp
from jax import lax
from jax.experimental import pallas as pl
from jax.experimental.pallas import tpu as pltpu
from jax.sharding import PartitionSpec as P

NDISP = 3
VMEM_LIMIT = 40 * 1024 * 1024
WHOLE = pl.BlockSpec(memory_space=pltpu.VMEM)
SCALARS = pl.BlockSpec(memory_space=pltpu.SMEM)


def chosen_entries(bank, wanted):
    picked = [
        lax.dynamic_index_in_dim(bank, wanted[a], axis=1, keepdims=False)
        for a in range(wanted.shape[0])
    ]
    return jnp.stack(picked, axis=1)


def planar(matrices):
    return jnp.swapaxes(matrices, 1, 2)


def snake_hops(count, hop):
    walk = list(range(0, count, 2)) + list(range(1, count, 2))[::-1]
    return [(walk[k], walk[(k + hop) % count]) for k in range(count)]


def sink_kernel(half_ref, forward_ref, own_ref, other_ref, out_ref):
    mine = half_ref[0]
    for t in range(forward_ref.shape[0]):
        real = forward_ref[t, 0].T
        imag = forward_ref[t, 1].T
        for_real = jnp.concatenate([real, -imag], axis=1)
        for_imag = jnp.concatenate([imag, real], axis=1)
        left = jnp.concatenate([for_real, for_imag], axis=0)
        for ops_ref, half in ((own_ref, mine), (other_ref, 1 - mine)):
            out_ref[t, half] = lax.dot_general(
                left, ops_ref[t], (((1,), (1,)), ((), ())), preferred_element_type=jnp.float32
            ).astype(jnp.bfloat16)


def trace_kernel(n_halves, last, nop, rows, *refs):
    place_ref, product_ref, back_ref = refs[:3]
    pieces = []
    at = 3
    for halves in n_halves:
        pieces.append(refs[at : at + halves])
        at += halves
    before_ref = refs[at] if at < len(refs) - 1 else None
    out_ref = refs[-1]
    times = product_ref.shape[0]
    order = back_ref.shape[2]
    totals = [None if before_ref is None else before_ref[t] for t in range(times)]
    for k, parts in enumerate(pieces):
        if len(parts) == 1:
            height = parts[0].shape[0] // 2
            real, imag = parts[0][:height], parts[0][height:]
        else:
            real, imag = parts[0][...], parts[1][...]
        for_real = jnp.concatenate([real, -imag], axis=1)
        for_imag = jnp.concatenate([imag, real], axis=1)
        left = jnp.concatenate([for_real, for_imag], axis=0)
        start = pl.multiple_of(place_ref[k] * rows, rows)
        for t in range(times):
            reverse = jnp.dot(left, back_ref[t], preferred_element_type=jnp.float32)
            high = reverse.astype(jnp.bfloat16)
            low = (reverse - high.astype(jnp.float32)).astype(jnp.bfloat16)
            blocks = []
            for part in range(2):
                two = [
                    product_ref[t, half, pl.ds(pl.multiple_of(part * order + start, rows), rows), :]
                    for half in range(2)
                ]
                width = two[0].shape[1] // nop
                for a in range(nop):
                    blocks.append(
                        jnp.concatenate([x[:, a * width : (a + 1) * width] for x in two], axis=1)
                    )
            sink = jnp.concatenate(blocks, axis=0)
            nt = (((1,), (1,)), ((), ()))
            added = lax.dot_general(sink, high, nt, preferred_element_type=jnp.float32)
            added += lax.dot_general(sink, low, nt, preferred_element_type=jnp.float32)
            totals[t] = added if totals[t] is None else totals[t] + added
    if not last:
        for t in range(times):
            out_ref[t] = totals[t]
        return
    side = totals[0].shape[0]
    row_at = lax.broadcasted_iota(jnp.int32, (side, side), 0)
    column_at = lax.broadcasted_iota(jnp.int32, (side, side), 1)
    same = lax.rem(row_at, rows) == lax.rem(column_at, rows)
    groups = side // rows
    in_group = (
        lax.broadcasted_iota(jnp.int32, (side, groups), 0) // rows
        == lax.broadcasted_iota(jnp.int32, (side, groups), 1)
    ).astype(jnp.float32)
    for t in range(times):
        kept = jnp.where(same, totals[t], 0.0)
        summed = kept.reshape(groups, rows, side).sum(axis=1)
        paired = jnp.dot(
            summed, in_group, preferred_element_type=jnp.float32, precision=lax.Precision.HIGHEST
        )
        out_ref[t, 0] = (paired[:nop, :nop] - paired[nop:, nop:]) / order
        out_ref[t, 1] = (paired[:nop, nop:] + paired[nop:, :nop]) / order


def traces(product, back, pieces, places, nop, rows, before=None, last=False):
    times = product.shape[0]
    side = 2 * nop * rows
    operands = [places, product, back]
    for parts in pieces:
        operands += list(parts)
    if before is not None:
        operands.append(before)
    shape = (times, 2, nop, nop) if last else (times, side, side)
    order = back.shape[2]
    flops = 2 * times * len(pieces) * side * (2 * order * order + 2 * side * order)
    return pl.pallas_call(
        functools.partial(trace_kernel, tuple(len(p) for p in pieces), last, nop, rows),
        out_shape=jax.ShapeDtypeStruct(shape, jnp.float32),
        in_specs=[SCALARS] + [WHOLE] * (len(operands) - 1),
        out_specs=WHOLE,
        compiler_params=pltpu.CompilerParams(vmem_limit_bytes=VMEM_LIMIT),
        cost_estimate=pl.CostEstimate(flops=flops, bytes_accessed=4 * 1024 * 1024, transcendentals=0),
        name="traces_last" if last else "traces",
    )(*operands)


def per_device(forward, backward, sink_bank, source_bank, op_mom, op_disp, n_times):
    wanted = op_mom * NDISP + op_disp
    nop = wanted.shape[0]
    order = forward.shape[2]
    times = forward.shape[0]
    own_rows = source_bank.shape[2]
    me = lax.axis_index("ta")
    half = lax.axis_index("sa")

    source = jnp.transpose(chosen_entries(source_bank, wanted)[0], (2, 0, 1, 3)).reshape(-1, order)

    sink_own = chosen_entries(sink_bank, wanted).reshape(times, -1, 2 * order)
    sink_other = lax.ppermute(sink_own, "sa", [(0, 1), (1, 0)])
    product = pl.pallas_call(
        sink_kernel,
        out_shape=jax.ShapeDtypeStruct((times, 2, 2 * order, sink_own.shape[1]), jnp.bfloat16),
        in_specs=[SCALARS, WHOLE, WHOLE, WHOLE],
        out_specs=WHOLE,
        compiler_params=pltpu.CompilerParams(vmem_limit_bytes=VMEM_LIMIT),
        cost_estimate=pl.CostEstimate(
            flops=2 * times * 2 * order * 2 * order * order * nop,
            bytes_accessed=5 * 1024 * 1024,
            transcendentals=0,
        ),
        name="sink_product",
    )(half.reshape(1).astype(jnp.int32), planar(forward[:, 0]), sink_own, sink_other)
    back = planar(backward[0]).reshape(times, 2 * order, order)

    rows = order // (2 * nop)
    if own_rows == rows:
        def hop(array, k):
            return lax.ppermute(array, "ta", snake_hops(n_times, k))

        walk = jnp.asarray([a for a, _ in snake_hops(n_times, 1)], jnp.int32)
        spot = jnp.argmax(walk == me).astype(jnp.int32)

        def places(*offsets):
            return jnp.stack([walk[(spot + k) % n_times] for k in offsets])

        cut = source.shape[0] // 2
        up1, down1 = hop(source, 1), hop(source, -1)
        up2, down2 = hop(source, 2), hop(source, -2)
        up3, down3 = hop(up2, 1), hop(down2, -1)
        up4, down4 = hop(up2[:cut], 2), hop(down2[cut:], -2)
        first = traces(
            product, back, [(source,), (up1,), (down1,), (up2,), (down2,)], places(0, -1, 1, -2, 2), nop, rows
        )
        result = traces(
            product, back, [(up3,), (down3,), (up4, down4)], places(-3, 3, 4), nop, rows, before=first, last=True
        )
    else:
        whole = lax.all_gather(source.reshape(2, nop, own_rows, order), "ta", axis=2, tiled=True)
        pieces = [
            (whole[:, :, k * rows : (k + 1) * rows].reshape(-1, order),) for k in range(order // rows)
        ]
        result = traces(
            product, back, pieces, jnp.arange(order // rows, dtype=jnp.int32), nop, rows, last=True
        )
    return result[:, None]


def solution(mesh):
    placed = (
        P(("cfg", "ta"), "sa", None, None, None),
        P(("cfg", "sa"), "ta", None, None, None),
        P(("cfg", "ta"), None, "sa", None, None),
        P(("cfg", "sa"), None, "ta", None, None),
        P(),
        P(),
    )
    return jax.shard_map(
        functools.partial(per_device, n_times=mesh.shape["ta"]),
        mesh=mesh,
        in_specs=placed,
        out_specs=P(("cfg", "ta"), "sa", None, None, None),
        check_vma=False,
    )
```

time: 119 us -> 49.5 us (0.42)
  matrix products: 46.7 us -> 0 us
  waiting for transfers between devices: 38.5 us -> 2.79 us
  starting transfers between devices: 0.04 us -> 11.3 us
  local copies, waits for them, and re-layouts: 19 us -> 9.28 us
  Pallas kernels: 0 us -> 6.69 us
  other arithmetic: 1.07 us -> 5.47 us
    dot_general x5 -> x0, matrix products: 46.7 us -> none  [the longest x1 34.7 us: per_device(): jnp.einsum('taicj,tbdij->tabcd', reshaped, reverse, preferred_element_typ...]
    all_gather x2 -> x0, waiting for transfers between devices: 38.5 us -> none  [the longest x1 38.5 us: per_device(): lax.all_gather(source_local, 'ta', axis=2, tiled=True)[0]]
    ppermute x0 -> x9, starting transfers between devices: none -> 11.3 us  [the longest x8 10.8 us: hop(): return lax.ppermute(array, 'ta', snake_hops(n_times, k))]
    pallas_call x0 -> x3, Pallas kernels: none -> 6.69 us  [the longest x2 5.41 us: traces(): pl.pallas_call(functools.partial(trace_kernel, tuple((len(p) for p in pie...]
    all_gather x2 -> x0, local copies, waits for them, and re-layouts: 5.75 us -> none  [the longest x1 4.32 us: per_device(): lax.all_gather(sink_local, 'sa', axis=2, tiled=True)]
    transpose x1 -> x2, local copies, waits for them, and re-layouts: 5.66 us -> 1.13 us  [the longest x1 1.12 us: planar(): return jnp.swapaxes(matrices, 1, 2)]
    another operation x1 -> x3, other arithmetic: 0.17 us -> 4.56 us  [the longest x1 1.96 us: chosen_entries(): return jnp.stack(picked, axis=1)]
    dynamic_slice x0 -> x3, local copies, waits for them, and re-layouts: none -> 3.52 us  [the longest x2 2.83 us: chosen_entries(): lax.dynamic_index_in_dim(bank, wanted[a], axis=1, keepdims=False)]
  transfers between devices with their start and end apart: 2 -> 9, of which waited for: 1 -> 1; matrix products, arithmetic and copies ran while one was open for 12% -> 18% of each run, Pallas kernels for 0% -> 8%
where the time goes in v1:
time: 49.5 us; the launch traced here: 49 us
  between operations  13.4 us (27%)
  starting transfers between devices  11.3 us (23%)
  local copies, waits for them, and re-layouts  9.28 us (19%)
  Pallas kernels  6.69 us (14%)
  other arithmetic  5.47 us (11%)
  waiting for transfers between devices  2.79 us (6%)
    ppermute x8, starting transfers between devices, hop(): return lax.ppermute(array, 'ta', snake_hops(n_times, k))  10.8 us
    pallas_call x2, Pallas kernels, traces(): pl.pallas_call(functools.partial(trace_kernel, tuple((len(p) for p in pie...  5.41 us
    another operation x1, local copies, waits for them, and re-layouts, places(): return jnp.stack([walk[(spot + k) % n_times] for k in offsets])  3.16 us
    dynamic_slice x2, local copies, waits for them, and re-layouts, chosen_entries(): lax.dynamic_index_in_dim(bank, wanted[a], axis=1, keepdims=False)  2.83 us
    ppermute x8, waiting for transfers between devices, hop(): return lax.ppermute(array, 'ta', snake_hops(n_times, k))  2.79 us
    another operation x1, other arithmetic, chosen_entries(): return jnp.stack(picked, axis=1)  1.96 us
    another operation x1, other arithmetic, places(): return jnp.stack([walk[(spot + k) % n_times] for k in offsets])  1.95 us
    pallas_call x1, Pallas kernels, per_device(): pl.pallas_call(sink_kernel, out_shape=jax.ShapeDtypeStruct((times, 2, 2 *...  1.29 us
  transfers between devices with their start and end apart: 9, of which 1 were waited for; matrix products, arithmetic and copies ran while one was open for 18% of the time, Pallas kernels for 8%

profile of v1, /device:TPU:0, one launch (start us, length us, event | category | flops | bytes accessed | tf_op | source)
XLA Modules:
  0.0 49.0 jit_solution(10274420052997859603)
XLA Ops:
  0.0 0.7 %multiply_add_fusion = s32[4]{0:T(128)S(1)} fusion(s32[4]{0:T(128)} %param.12, s32[4]{0:T(128)} %param.11), kind=kLoop, calls=%fused_computation.13 | loop fusion | flops 8 | bytes 48 | tf_op jit(solution)/shard_map/add | solution.py:135
  0.7 0.7 %fusion.1 = (s32[1]{0:T(128)}, s32[1]{0:T(128)}, s32[1]{0:T(128)}, s32[1]{0:T(128)}) fusion(s32[4]{0:T(128)S(1)} %multiply_add_fusion), kind=kLoop, calls=%fused_computation.15 | loop fusion | bytes 32 | tf_op jit(solution)/shard_map/slice | solution.py:18
  8.9 1.9 %constant_dynamic-slice_fusion.7 = (bf16[2,1,128,2,256]{4,3,2,1,0:T(2,128)(2,1)S(1)}, bf16[2,1,128,2,256]{4,3,2,1,0:T(2,128)(2,1)S(1)}, bf16[2,1,128,2,256]{4,3,...) fusion(bf16[2,9,128,2,256]{4,3,2,1,0:T(2,128)(2,1)} %param.9, s32[]{:T(128)S(6)} %select_n.87, s32[]{:T(128)S(6)} %select_n.88, ...), kind=kLoop, calls=%fused_computation.10 | loop fusion | bytes 2097168 | tf_op jit(solution)/shard_map/jit(dynamic_index_in_dim)/dynamic_slice | solution.py:18
  10.8 2.0 %pad_maximum_fusion = bf16[2,4,128,2,256]{4,3,2,1,0:T(2,128)(2,1)S(1)} fusion(bf16[2,1,128,2,256]{4,3,2,1,0:T(2,128)(2,1)S(1)} %get-tuple-element.9, bf16[2,1,128,2,256]{4,3,2,1,0:T(2,128)(2,1)S(1)} %get-tuple-element.10, bf16[2,1,128,2,256]{4,3,2,1,0:T(2,128)(2,1)S(1)} %get-tuple-element.8, bf16[2,1,128,2,256]{4,3,2,1,0:T(2,128)(2,1)S(1)} %get-tuple-element.7), kind=kLoop, calls=%fused_computation | loop fusion | flops 1572864 | bytes 2097152 | tf_op jit(solution)/shard_map/stack | solution.py:21
  12.8 0.7 %reshape.13.own_ref = bf16[2,512,512]{2,1,0:T(8,128)(2,1)S(1)} reshape(bf16[2,4,128,2,256]{4,3,2,1,0:T(2,128)(2,1)S(1)} %pad_maximum_fusion) | data formatting | bytes 2097152 | tf_op jit(solution)/shard_map/reshape | solution.py:145
  13.5 0.5 %collective-permute-start = (bf16[2,512,512]{2,1,0:T(8,128)(2,1)S(1)}, bf16[2,512,512]{2,1,0:T(8,128)(2,1)S(1)}, u32[]{:S(2)}, u32[]{:S(2)}) collective-permute-start(bf16[2,512,512]{2,1,0:T(8,128)(2,1)S(1)} %reshape.13.own_ref), channel_id=1, source_target_pairs={{0,1},{1,0},{2,3},{3,2},{4,5},{5,4},{6,7},{7,6},{8,9},{9,8},{10,11... | collective-permute-start | bytes 3145736 | tf_op jit(solution)/shard_map/ppermute | solution.py:146
  14.0 0.9 %constant_dynamic-slice_fusion.3 = (bf16[1,1,32,2,256]{4,3,2,1,0:T(2,128)(2,1)S(1)}, bf16[1,1,32,2,256]{4,3,2,1,0:T(2,128)(2,1)S(1)}, bf16[1,1,32,2,256]{4,3,2,1,0:T(2,128)(2,1)S(1)}, bf16[1,1,32,2,256]{4,3,2,1,0:T(2,128)(2,1)S(1)}) fusion(bf16[1,9,32,2,256]{4,3,2,1,0:T(2,128)(2,1)} %param.10, s32[]{:T(128)S(6)} %select_n.87, s32[]{:T(128)S(6)} %select_n.88, ...), kind=kLoop, calls=%fused_computation.6 | loop fusion | bytes 262160 | tf_op jit(solution)/shard_map/jit(dynamic_index_in_dim)/dynamic_slice | solution.py:18
  14.9 0.2 maximum_bitcast_fusion
  15.2 3.7 %collective-permute-start.1 = (bf16[256,256]{1,0:T(8,128)(2,1)S(1)}, bf16[256,256]{1,0:T(8,128)(2,1)S(1)}, u32[]{:S(2)}, u32[]{:S(2)}) collective-permute-start(bf16[256,256]{1,0:T(8,128)(2,1)S(1)} %bitcast.25), channel_id=1, source_target_pairs={{0,8},{4,12},{8,14},{12,10},{14,6},{10,2},{6,0},{2,4},{1,9},{5,13}... | collective-permute-start | bytes 393224 | tf_op jit(solution)/shard_map/ppermute | solution.py:165
  18.9 1.9 %collective-permute-start.7 = (bf16[256,256]{1,0:T(8,128)(2,1)S(1)}, bf16[256,256]{1,0:T(8,128)(2,1)}, u32[]{:S(2)}, u32[]{:S(2)}) collective-permute-start(bf16[256,256]{1,0:T(8,128)(2,1)S(1)} %bitcast.27), channel_id=1, source_target_pairs={{0,4},{4,8},{8,12},{12,14},{14,10},{10,6},{6,2},{2,0},{1,5},{5,9},... | collective-permute-start | bytes 393224 | tf_op jit(solution)/shard_map/ppermute | solution.py:165
  20.8 0.1 collective-permute-start.8
  20.9 0.7 %compare_reduce_fusion = (pred[]{:T(512)}, s32[]{:T(128)}) fusion(s32[8]{0:T(128)S(1)} %copy-done.1, s32[]{:T(128)S(6)} %axis_index.23), kind=kLoop, calls=%fused_computation.11 | loop fusion | flops 57 | bytes 41 | tf_op jit(solution)/shard_map/per_device/reduce | solution.py:168
  27.3 0.7 %fusion = (s32[1]{0:T(128)}, s32[1]{0:T(128)}, s32[1]{0:T(128)}, s32[1]{0:T(128)}, s32[1]{0:T(128)}, /*index=5*/s32[1]{0:T(128)}, s32[1]{0:T(128)}, s32[1]{0:T(128)}) fusion(s32[8]{0:T(128)S(1)} %copy-done.1, s32[]{:T(128)S(6)} %select_n.100, s32[]{:T(128)S(6)} %select_n.96, s32[]{:T(128)S(6)} %select_n.94, s32[]{:T(128)S(6)} %select_n.92, s32[]{:T(128)S(6)} %select_n.86, ...), kind=kLoop, calls=%fused_computation.14 | loop fusion | bytes 96 | tf_op jit(solution)/shard_map/dynamic_slice | solution.py:171
  28.0 2.0 %pad_add_fusion.refs_0_ = s32[3]{0:T(128)S(1)} fusion(s32[1]{0:T(128)} %get-tuple-element.19, s32[1]{0:T(128)} %get-tuple-element.20, s32[1]{0:T(128)} %get-tuple-element.21), kind=kLoop, calls=%fused_computation.12 | loop fusion | flops 6 | bytes 24 | tf_op jit(solution)/shard_map/stack | solution.py:171
  29.9 0.1 copy.13
  30.0 1.1 %copy.9 = bf16[2,2,256,256]{3,2,1,0:T(8,128)(2,1)S(1)} copy(bf16[2,2,256,256]{3,1,2,0:T(2,128)(2,1)} %bitcast.30) | data formatting | bytes 1048576 | tf_op jit(solution)/shard_map/transpose | solution.py:25
  31.1 3.2 %stack.11.refs_0_ = s32[5]{0:T(128)S(1)} concatenate(s32[1]{0:T(128)} %get-tuple-element.18, s32[1]{0:T(128)} %get-tuple-element.17, s32[1]{0:T(128)} %get-tuple-element.16, s32[1]{0:T(128)} %get-tuple-element.22, s32[1]{0:T(128)} %get-tuple-element.15), dimensions={0} | concatenate | bytes 40 | tf_op jit(solution)/shard_map/stack | solution.py:171
  34.3 3.0 %collective-permute-start.5 = (bf16[128,256]{1,0:T(8,128)(2,1)S(1)}, bf16[128,256]{1,0:T(8,128)(2,1)S(1)}, u32[]{:S(2)}, u32[]{:S(2)}) collective-permute-start(bf16[128,256]{1,0:T(8,128)(2,1)S(1)} %slice.28), channel_id=1, source_target_pairs={{0,8},{4,12},{8,14},{12,10},{14,6},{10,2},{6,0},{2,4},{1,9},{5,13}... | collective-permute-start | bytes 196616 | tf_op jit(solution)/shard_map/ppermute | solution.py:165
  37.3 1.6 %collective-permute-start.2 = (bf16[256,256]{1,0:T(8,128)(2,1)S(1)}, bf16[256,256]{1,0:T(8,128)(2,1)S(1)}, u32[]{:S(2)}, u32[]{:S(2)}) collective-permute-start(bf16[256,256]{1,0:T(8,128)(2,1)S(1)} %collective-permute-done.1.refs_6_), channel_id=1, source_target_pairs={{0,4},{4,8},{8,12},{12,14},{14,10},{10,6},{6,2},{2,0},{1,5},{5,9},... | collective-permute-start | bytes 393224 | tf_op jit(solution)/shard_map/ppermute | solution.py:165
  38.9 0.5 %collective-permute-start.4 = (bf16[256,256]{1,0:T(8,128)(2,1)S(1)}, bf16[256,256]{1,0:T(8,128)(2,1)S(1)}, u32[]{:S(2)}, u32[]{:S(2)}) collective-permute-start(bf16[256,256]{1,0:T(8,128)(2,1)S(1)} %collective-permute-done.3.refs_7_), channel_id=1, source_target_pairs={{0,2},{4,0},{8,4},{12,8},{14,12},{10,14},{6,10},{2,6},{1,3},{5,1},... | collective-permute-start | bytes 393224 | tf_op jit(solution)/shard_map/ppermute | solution.py:165
  39.4 1.3 %sink_product.1.refs_1_ = bf16[2,2,512,512]{3,2,1,0:T(8,128)(2,1)S(1)} custom-call(s32[1]{0:T(128)} %bitcast.half_ref, bf16[2,2,256,256]{3,2,1,0:T(8,128)(2,1)S(1)} %bitcast.22, bf16[2,512,512]{2,1,0:T(8,128)(2,1)S(1)} %reshape.13.own_ref, bf16[2,512,512]{2,1,0:T(8,128)(2,1)S(1)} %collective-permute-done.other_ref), custom_call_target="tpu_custom_call" | custom-call | flops 1073741824 | bytes 5242880 | tf_op jit(solution)/shard_map/sink_product/pallas_call | solution.py:147
  40.8 2.7 %traces.1.refs_7_ = f32[2,256,256]{2,1,0:T(8,128)S(1)} custom-call(s32[5]{0:T(128)S(1)} %stack.11.refs_0_, bf16[2,2,512,512]{3,2,1,0:T(8,128)(2,1)S(1)} %sink_product.1.refs_1_, bf16[2,512,256]{2,1,0:T(8,128)(2,1)S(1)} %bitcast.23, bf16[256,256]{1,0:T(8,128)(2,1)S(1)} %bitcast.29, bf16[256,256]{1,0:T(8,128)(2,1)} %collective-permute-done.7.refs_4_, ...), custom_call_target="tpu_custom_call" | custom-call | flops 1342177280 | bytes 4194304 | tf_op jit(solution)/shard_map/traces/pallas_call | solution.py:123
  43.5 2.8 %collective-permute-done.6.refs_6_ = bf16[128,256]{1,0:T(8,128)(2,1)S(1)} collective-permute-done((bf16[128,256]{1,0:T(8,128)(2,1)S(1)}, bf16[128,256]{1,0:T(8,128)(2,1)S(1)}, u32[]{:S(2)}, u32[]{:S(2)}) %collective-permute-start.6) | collective-permute-done | bytes 65568 | tf_op jit(solution)/shard_map/ppermute | solution.py:165
  46.3 2.7 %traces_last.1 = f32[2,2,4,4]{3,2,1,0:T(4,128)} custom-call(s32[3]{0:T(128)S(1)} %pad_add_fusion.refs_0_, bf16[2,2,512,512]{3,2,1,0:T(8,128)(2,1)S(1)} %sink_product.1.refs_1_, bf16[2,512,256]{2,1,0:T(8,128)(2,1)S(1)} %bitcast.24, bf16[256,256]{1,0:T(8,128)(2,1)S(1)} %collective-permute-done.2.refs_3_, bf16[256,256]{1,0:T(8,128)(2,1)S(1)} %collective-permute-done.4.refs_4_, ...), custom_call_target="tpu_custom_call" | custom-call | flops 805306368 | bytes 4194304 | tf_op jit(solution)/shard_map/traces_last/pallas_call | solution.py:123
  (17 shorter events, 0.1 us)
Async XLA Ops:
  10.8 10.1 %copy-start.1 = (s32[8]{0:T(128)S(1)}, s32[8]{0:T(128)}, u32[]{:S(2)}) copy-start(s32[8]{0:T(128)} %constant.93.clone) | copy-start | bytes 100
  10.8 19.1 %copy-start = (bf16[2,1,256,2,256]{4,3,2,1,0:T(2,128)(2,1)S(1)}, bf16[2,1,256,2,256]{4,3,2,1,0:T(2,128)(2,1)}, u32[]{:S(2)}) copy-start(bf16[2,1,256,2,256]{4,3,2,1,0:T(2,128)(2,1)} %param.7) | copy-start | bytes 1572868
  13.5 25.4 %collective-permute-start = (bf16[2,512,512]{2,1,0:T(8,128)(2,1)S(1)}, bf16[2,512,512]{2,1,0:T(8,128)(2,1)S(1)}, u32[]{:S(2)}, u32[]{:S(2)}) collective-permute-start(bf16[2,512,512]{2,1,0:T(8,128)(2,1)S(1)} %reshape.13.own_ref), channel_id=1, source_target_pairs={{0,1},{1,0},{2,3},{3,2},{4,5},{5,4},{6,7},{7,6},{8,9},{9,8},{10,11... | collective-permute-start | bytes 3145736 | tf_op jit(solution)/shard_map/ppermute | solution.py:146
  15.2 19.1 %collective-permute-start.1 = (bf16[256,256]{1,0:T(8,128)(2,1)S(1)}, bf16[256,256]{1,0:T(8,128)(2,1)S(1)}, u32[]{:S(2)}, u32[]{:S(2)}) collective-permute-start(bf16[256,256]{1,0:T(8,128)(2,1)S(1)} %bitcast.25), channel_id=1, source_target_pairs={{0,8},{4,12},{8,14},{12,10},{14,6},{10,2},{6,0},{2,4},{1,9},{5,13}... | collective-permute-start | bytes 393224 | tf_op jit(solution)/shard_map/ppermute | solution.py:165
  18.9 18.4 %collective-permute-start.3 = (bf16[256,256]{1,0:T(8,128)(2,1)S(1)}, bf16[256,256]{1,0:T(8,128)(2,1)S(1)}, u32[]{:S(2)}, u32[]{:S(2)}) collective-permute-start(bf16[256,256]{1,0:T(8,128)(2,1)S(1)} %bitcast.26), channel_id=1, source_target_pairs={{0,6},{4,2},{8,0},{12,4},{14,8},{10,12},{6,14},{2,10},{1,7},{5,3},... | collective-permute-start | bytes 393224 | tf_op jit(solution)/shard_map/ppermute | solution.py:165
  18.9 21.8 %collective-permute-start.7 = (bf16[256,256]{1,0:T(8,128)(2,1)S(1)}, bf16[256,256]{1,0:T(8,128)(2,1)}, u32[]{:S(2)}, u32[]{:S(2)}) collective-permute-start(bf16[256,256]{1,0:T(8,128)(2,1)S(1)} %bitcast.27), channel_id=1, source_target_pairs={{0,4},{4,8},{8,12},{12,14},{14,10},{10,6},{6,2},{2,0},{1,5},{5,9},... | collective-permute-start | bytes 393224 | tf_op jit(solution)/shard_map/ppermute | solution.py:165
  20.8 20.0 %collective-permute-start.8 = (bf16[256,256]{1,0:T(8,128)(2,1)S(1)}, bf16[256,256]{1,0:T(8,128)(2,1)}, u32[]{:S(2)}, u32[]{:S(2)}) collective-permute-start(bf16[256,256]{1,0:T(8,128)(2,1)S(1)} %bitcast.28), channel_id=1, source_target_pairs={{0,2},{4,0},{8,4},{12,8},{14,12},{10,14},{6,10},{2,6},{1,3},{5,1},... | collective-permute-start | bytes 393224 | tf_op jit(solution)/shard_map/ppermute | solution.py:165
  34.3 9.2 %collective-permute-start.5 = (bf16[128,256]{1,0:T(8,128)(2,1)S(1)}, bf16[128,256]{1,0:T(8,128)(2,1)S(1)}, u32[]{:S(2)}, u32[]{:S(2)}) collective-permute-start(bf16[128,256]{1,0:T(8,128)(2,1)S(1)} %slice.28), channel_id=1, source_target_pairs={{0,8},{4,12},{8,14},{12,10},{14,6},{10,2},{6,0},{2,4},{1,9},{5,13}... | collective-permute-start | bytes 196616 | tf_op jit(solution)/shard_map/ppermute | solution.py:165
  37.3 9.0 %collective-permute-start.2 = (bf16[256,256]{1,0:T(8,128)(2,1)S(1)}, bf16[256,256]{1,0:T(8,128)(2,1)S(1)}, u32[]{:S(2)}, u32[]{:S(2)}) collective-permute-start(bf16[256,256]{1,0:T(8,128)(2,1)S(1)} %collective-permute-done.1.refs_6_), channel_id=1, source_target_pairs={{0,4},{4,8},{8,12},{12,14},{14,10},{10,6},{6,2},{2,0},{1,5},{5,9},... | collective-permute-start | bytes 393224 | tf_op jit(solution)/shard_map/ppermute | solution.py:165
  38.9 7.4 %collective-permute-start.4 = (bf16[256,256]{1,0:T(8,128)(2,1)S(1)}, bf16[256,256]{1,0:T(8,128)(2,1)S(1)}, u32[]{:S(2)}, u32[]{:S(2)}) collective-permute-start(bf16[256,256]{1,0:T(8,128)(2,1)S(1)} %collective-permute-done.3.refs_7_), channel_id=1, source_target_pairs={{0,2},{4,0},{8,4},{12,8},{14,12},{10,14},{6,10},{2,6},{1,3},{5,1},... | collective-permute-start | bytes 393224 | tf_op jit(solution)/shard_map/ppermute | solution.py:165
  40.7 5.6 %collective-permute-start.6 = (bf16[128,256]{1,0:T(8,128)(2,1)S(1)}, bf16[128,256]{1,0:T(8,128)(2,1)S(1)}, u32[]{:S(2)}, u32[]{:S(2)}) collective-permute-start(bf16[128,256]{1,0:T(8,128)(2,1)S(1)} %slice.29), channel_id=1, source_target_pairs={{0,6},{4,2},{8,0},{12,4},{14,8},{10,12},{6,14},{2,10},{1,7},{5,3},... | collective-permute-start | bytes 196616 | tf_op jit(solution)/shard_map/ppermute | solution.py:165

commit v2 on v1

--- a/solution.py
+++ b/solution.py
@@ -13,16 +13,40 @@
 SCALARS = pl.BlockSpec(memory_space=pltpu.SMEM)
 
 
-def chosen_entries(bank, wanted):
-    picked = [
-        lax.dynamic_index_in_dim(bank, wanted[a], axis=1, keepdims=False)
-        for a in range(wanted.shape[0])
-    ]
-    return jnp.stack(picked, axis=1)
+def select_kernel(mom_ref, disp_ref, bank_ref, out_ref, arrived):
+    copies = []
+    for a in range(out_ref.shape[1]):
+        entry = mom_ref[a] * NDISP + disp_ref[a]
+        copies.append(pltpu.make_async_copy(bank_ref.at[:, entry], out_ref.at[:, a], arrived.at[a]))
+        copies[-1].start()
+    for copy in copies:
+        copy.wait()
+
+
+def chosen_entries(bank, op_mom, op_disp, name):
+    nop = op_mom.shape[0]
+    shape = (bank.shape[0], nop) + bank.shape[2:]
+    return pl.pallas_call(
+        select_kernel,
+        out_shape=jax.ShapeDtypeStruct(shape, bank.dtype),
+        in_specs=[SCALARS, SCALARS, pl.BlockSpec(memory_space=pl.ANY)],
+        out_specs=WHOLE,
+        scratch_shapes=[pltpu.SemaphoreType.DMA((nop,))],
+        compiler_params=pltpu.CompilerParams(vmem_limit_bytes=VMEM_LIMIT),
+        name=name,
+    )(op_mom, op_disp, bank)
 
 
 def planar(matrices):
     return jnp.swapaxes(matrices, 1, 2)
+
+
+def snake_at(spot, count):
+    return jnp.where(2 * spot < count, 2 * spot, 2 * (count - 1 - spot) + 1)
+
+
+def snake_spot(index, count):
+    return jnp.where(lax.rem(index, 2) == 0, index // 2, count - 1 - index // 2)
 
 
 def snake_hops(count, hop):
@@ -30,8 +54,8 @@
     return [(walk[k], walk[(k + hop) % count]) for k in range(count)]
 
 
-def sink_kernel(half_ref, forward_ref, own_ref, other_ref, out_ref):
-    mine = half_ref[0]
+def sink_kernel(forward_ref, own_ref, other_ref, out_ref):
+    mine = lax.axis_index("sa")
     for t in range(forward_ref.shape[0]):
         real = forward_ref[t, 0].T
         imag = forward_ref[t, 1].T
@@ -44,10 +68,11 @@
             ).astype(jnp.bfloat16)
 
 
-def trace_kernel(n_halves, last, nop, rows, *refs):
-    place_ref, product_ref, back_ref = refs[:3]
+def trace_kernel(n_halves, spots, count, last, nop, rows, *refs):
+    product_ref, back_ref = refs[:2]
+    own_spot = None if count is None else snake_spot(lax.axis_index("ta"), count)
     pieces = []
-    at = 3
+    at = 2
     for halves in n_halves:
         pieces.append(refs[at : at + halves])
         at += halves
@@ -65,7 +90,11 @@
         for_real = jnp.concatenate([real, -imag], axis=1)
         for_imag = jnp.concatenate([imag, real], axis=1)
         left = jnp.concatenate([for_real, for_imag], axis=0)
-        start = pl.multiple_of(place_ref[k] * rows, rows)
+        if own_spot is None:
+            start = spots[k] * rows
+        else:
+            spot = lax.rem(own_spot + (spots[k] + count), count)
+            start = pl.multiple_of(snake_at(spot, count) * rows, rows)
         for t in range(times):
             reverse = jnp.dot(left, back_ref[t], preferred_element_type=jnp.float32)
             high = reverse.astype(jnp.bfloat16)
@@ -73,7 +102,7 @@
             blocks = []
             for part in range(2):
                 two = [
-                    product_ref[t, half, pl.ds(pl.multiple_of(part * order + start, rows), rows), :]
+                    product_ref[t, half, pl.ds(part * order + start, rows), :]
                     for half in range(2)
                 ]
                 width = two[0].shape[1] // nop
@@ -109,10 +138,10 @@
         out_ref[t, 1] = (paired[:nop, nop:] + paired[nop:, :nop]) / order
 
 
-def traces(product, back, pieces, places, nop, rows, before=None, last=False):
+def traces(product, back, pieces, spots, count, nop, rows, before=None, last=False):
     times = product.shape[0]
     side = 2 * nop * rows
-    operands = [places, product, back]
+    operands = [product, back]
     for parts in pieces:
         operands += list(parts)
     if before is not None:
@@ -121,9 +150,9 @@
     order = back.shape[2]
     flops = 2 * times * len(pieces) * side * (2 * order * order + 2 * side * order)
     return pl.pallas_call(
-        functools.partial(trace_kernel, tuple(len(p) for p in pieces), last, nop, rows),
+        functools.partial(trace_kernel, tuple(len(p) for p in pieces), spots, count, last, nop, rows),
         out_shape=jax.ShapeDtypeStruct(shape, jnp.float32),
-        in_specs=[SCALARS] + [WHOLE] * (len(operands) - 1),
+        in_specs=[WHOLE] * len(operands),
         out_specs=WHOLE,
         compiler_params=pltpu.CompilerParams(vmem_limit_bytes=VMEM_LIMIT),
         cost_estimate=pl.CostEstimate(flops=flops, bytes_accessed=4 * 1024 * 1024, transcendentals=0),
@@ -132,22 +161,19 @@
 
 
 def per_device(forward, backward, sink_bank, source_bank, op_mom, op_disp, n_times):
-    wanted = op_mom * NDISP + op_disp
-    nop = wanted.shape[0]
+    nop = op_mom.shape[0]
     order = forward.shape[2]
     times = forward.shape[0]
     own_rows = source_bank.shape[2]
-    me = lax.axis_index("ta")
-    half = lax.axis_index("sa")
-
-    source = jnp.transpose(chosen_entries(source_bank, wanted)[0], (2, 0, 1, 3)).reshape(-1, order)
-
-    sink_own = chosen_entries(sink_bank, wanted).reshape(times, -1, 2 * order)
+
+    source = jnp.transpose(chosen_entries(source_bank, op_mom, op_disp, "source_rows")[0], (2, 0, 1, 3)).reshape(-1, order)
+
+    sink_own = chosen_entries(sink_bank, op_mom, op_disp, "sink_rows").reshape(times, -1, 2 * order)
     sink_other = lax.ppermute(sink_own, "sa", [(0, 1), (1, 0)])
     product = pl.pallas_call(
         sink_kernel,
         out_shape=jax.ShapeDtypeStruct((times, 2, 2 * order, sink_own.shape[1]), jnp.bfloat16),
-        in_specs=[SCALARS, WHOLE, WHOLE, WHOLE],
+        in_specs=[WHOLE, WHOLE, WHOLE],
         out_specs=WHOLE,
         compiler_params=pltpu.CompilerParams(vmem_limit_bytes=VMEM_LIMIT),
         cost_estimate=pl.CostEstimate(
@@ -156,19 +182,13 @@
             transcendentals=0,
         ),
         name="sink_product",
-    )(half.reshape(1).astype(jnp.int32), planar(forward[:, 0]), sink_own, sink_other)
+    )(planar(forward[:, 0]), sink_own, sink_other)
     back = planar(backward[0]).reshape(times, 2 * order, order)
 
     rows = order // (2 * nop)
     if own_rows == rows:
         def hop(array, k):
             return lax.ppermute(array, "ta", snake_hops(n_times, k))
-
-        walk = jnp.asarray([a for a, _ in snake_hops(n_times, 1)], jnp.int32)
-        spot = jnp.argmax(walk == me).astype(jnp.int32)
-
-        def places(*offsets):
-            return jnp.stack([walk[(spot + k) % n_times] for k in offsets])
 
         cut = source.shape[0] // 2
         up1, down1 = hop(source, 1), hop(source, -1)
@@ -176,10 +196,10 @@
         up3, down3 = hop(up2, 1), hop(down2, -1)
         up4, down4 = hop(up2[:cut], 2), hop(down2[cut:], -2)
         first = traces(
-            product, back, [(source,), (up1,), (down1,), (up2,), (down2,)], places(0, -1, 1, -2, 2), nop, rows
+            product, back, [(source,), (up1,), (down1,), (up2,), (down2,)], (0, -1, 1, -2, 2), n_times, nop, rows
         )
         result = traces(
-            product, back, [(up3,), (down3,), (up4, down4)], places(-3, 3, 4), nop, rows, before=first, last=True
+            product, back, [(up3,), (down3,), (up4, down4)], (-3, 3, 4), n_times, nop, rows, before=first, last=True
         )
     else:
         whole = lax.all_gather(source.reshape(2, nop, own_rows, order), "ta", axis=2, tiled=True)
@@ -187,7 +207,7 @@
             (whole[:, :, k * rows : (k + 1) * rows].reshape(-1, order),) for k in range(order // rows)
         ]
         result = traces(
-            product, back, pieces, jnp.arange(order // rows, dtype=jnp.int32), nop, rows, last=True
+            product, back, pieces, tuple(range(order // rows)), None, nop, rows, last=True
         )
     return result[:, None]
 

time: 49.5 us -> 31.5 us (0.64)
  between operations: 13.4 us -> 0.12 us
  waiting for transfers between devices: 2.79 us -> 8.77 us
  other arithmetic: 5.47 us -> 0 us
  local copies, waits for them, and re-layouts: 9.28 us -> 3.88 us
  starting transfers between devices: 11.3 us -> 11.9 us
    ppermute x8, waiting for transfers between devices: 2.79 us -> 8.77 us  [hop(): return lax.ppermute(array, 'ta', snake_hops(n_times, k))]
    another operation x3 -> x0, other arithmetic: 4.56 us -> none  [the longest x1 1.96 us: chosen_entries(): return jnp.stack(picked, axis=1)]
    dynamic_slice x3 -> x0, local copies, waits for them, and re-layouts: 3.52 us -> none  [the longest x2 2.83 us: chosen_entries(): lax.dynamic_index_in_dim(bank, wanted[a], axis=1, keepdims=False)]
    another operation x1 -> x0, local copies, waits for them, and re-layouts: 3.16 us -> none  [places(): return jnp.stack([walk[(spot + k) % n_times] for k in offsets])]
    unnamed x5 -> x17, local copies, waits for them, and re-layouts: 0.09 us -> 3.07 us
    pallas_call x2, Pallas kernels: 5.41 us -> 3.89 us  [traces(): pl.pallas_call(functools.partial(trace_kernel, tuple((len(p) for p in pie...]
    pallas_call x0 -> x2, Pallas kernels: none -> 1.46 us  [chosen_entries(): pl.pallas_call(select_kernel, out_shape=jax.ShapeDtypeStruct(shape, bank....]
    transpose x1, local copies, waits for them, and re-layouts: 1.12 us -> 0.08 us  [planar(): return jnp.swapaxes(matrices, 1, 2)]
  transfers between devices with their start and end apart: 9 -> 9, of which waited for: 1 -> 3; matrix products, arithmetic and copies ran while one was open for 18% -> 1% of each run, Pallas kernels for 8% -> 12%
where the time goes in v2:
time: 31.5 us; the launch traced here: 31.3 us
  starting transfers between devices  11.9 us (38%)
  waiting for transfers between devices  8.77 us (28%)
  Pallas kernels  6.64 us (21%)
  local copies, waits for them, and re-layouts  3.88 us (12%)
    ppermute x8, starting transfers between devices, hop(): return lax.ppermute(array, 'ta', snake_hops(n_times, k))  11.4 us
    ppermute x8, waiting for transfers between devices, hop(): return lax.ppermute(array, 'ta', snake_hops(n_times, k))  8.77 us
    pallas_call x2, Pallas kernels, traces(): pl.pallas_call(functools.partial(trace_kernel, tuple((len(p) for p in pie...  3.89 us
    unnamed x17, local copies, waits for them, and re-layouts  3.07 us
    pallas_call x2, Pallas kernels, chosen_entries(): pl.pallas_call(select_kernel, out_shape=jax.ShapeDtypeStruct(shape, bank....  1.46 us
    pallas_call x1, Pallas kernels, per_device(): pl.pallas_call(sink_kernel, out_shape=jax.ShapeDtypeStruct((times, 2, 2 *...  1.29 us
    reshape x1, local copies, waits for them, and re-layouts, per_device(): chosen_entries(sink_bank, op_mom, op_disp, 'sink_rows')  0.71 us
  transfers between devices with their start and end apart: 9, of which 3 were waited for; matrix products, arithmetic and copies ran while one was open for 1% of the time, Pallas kernels for 12%

profile of v2, /device:TPU:0, one launch (start us, length us, event | category | flops | bytes accessed | tf_op | source)
XLA Modules:
  0.0 31.3 jit_solution(14448623526689394594)
XLA Ops:
  0.0 1.7 %copy-done = bf16[2,9,128,2,256]{4,3,2,1,0:T(2,128)(2,1)S(1)} copy-done((bf16[2,9,128,2,256]{4,3,2,1,0:T(2,128)(2,1)S(1)}, bf16[2,9,128,2,256]{4,3,2,1,0:T(2,128)(2,1)}, u32[]{:S(2)}) %copy-start) | copy-done | bytes 2359320
  1.7 0.7 %copy-done.2 = s32[4]{0:T(128)S(1)} copy-done((s32[4]{0:T(128)S(1)}, s32[4]{0:T(128)}, u32[]{:S(2)}) %copy-start.2) | copy-done | bytes 40
  2.3 0.7 %copy-done.4 = s32[4]{0:T(128)S(1)} copy-done((s32[4]{0:T(128)S(1)}, s32[4]{0:T(128)}, u32[]{:S(2)}) %copy-start.4) | copy-done | bytes 40
  3.0 0.7 %sink_rows.1 = bf16[2,4,128,2,256]{4,3,2,1,0:T(2,128)(2,1)S(1)} custom-call(s32[4]{0:T(128)S(1)} %copy-done.2, s32[4]{0:T(128)S(1)} %copy-done.4, bf16[2,9,128,2,256]{4,3,2,1,0:T(2,128)(2,1)S(1)} %copy-done), custom_call_target="tpu_custom_call" | custom-call | tf_op jit(solution)/shard_map/sink_rows/pallas_call | solution.py:29
  3.7 0.0 copy-start.7
  3.7 0.7 %reshape.9.own_ref = bf16[2,512,512]{2,1,0:T(8,128)(2,1)S(1)} reshape(bf16[2,4,128,2,256]{4,3,2,1,0:T(2,128)(2,1)S(1)} %sink_rows.1) | data formatting | bytes 2097152 | tf_op jit(solution)/shard_map/reshape | solution.py:171
  4.4 0.5 %collective-permute-start = (bf16[2,512,512]{2,1,0:T(8,128)(2,1)S(1)}, bf16[2,512,512]{2,1,0:T(8,128)(2,1)S(1)}, u32[]{:S(2)}, u32[]{:S(2)}) collective-permute-start(bf16[2,512,512]{2,1,0:T(8,128)(2,1)S(1)} %reshape.9.own_ref), channel_id=1, source_target_pairs={{0,1},{1,0},{2,3},{3,2},{4,5},{5,4},{6,7},{7,6},{8,9},{9,8},{10,11... | collective-permute-start | bytes 3145736 | tf_op jit(solution)/shard_map/ppermute | solution.py:172
  4.9 0.8 %source_rows.1 = bf16[1,4,32,2,256]{4,3,2,1,0:T(2,128)(2,1)S(1)} custom-call(s32[4]{0:T(128)S(1)} %copy-done.3, s32[4]{0:T(128)S(1)} %copy-done.5, bf16[1,9,32,2,256]{4,3,2,1,0:T(2,128)(2,1)S(1)} %copy-done.1), custom_call_target="tpu_custom_call" | custom-call | tf_op jit(solution)/shard_map/source_rows/pallas_call | solution.py:29
  5.7 3.7 %collective-permute-start.1 = (bf16[256,256]{1,0:T(8,128)(2,1)S(1)}, bf16[256,256]{1,0:T(8,128)(2,1)S(1)}, u32[]{:S(2)}, u32[]{:S(2)}) collective-permute-start(bf16[256,256]{1,0:T(8,128)(2,1)S(1)} %bitcast.20), channel_id=1, source_target_pairs={{0,8},{4,12},{8,14},{12,10},{14,6},{10,2},{6,0},{2,4},{1,9},{5,13}... | collective-permute-start | bytes 393224 | tf_op jit(solution)/shard_map/ppermute | solution.py:191
  9.4 0.0 collective-permute-start.3
  9.4 1.9 %collective-permute-start.7 = (bf16[256,256]{1,0:T(8,128)(2,1)S(1)}, bf16[256,256]{1,0:T(8,128)(2,1)S(1)}, u32[]{:S(2)}, u32[]{:S(2)}) collective-permute-start(bf16[256,256]{1,0:T(8,128)(2,1)S(1)} %bitcast.22), channel_id=1, source_target_pairs={{0,4},{4,8},{8,12},{12,14},{14,10},{10,6},{6,2},{2,0},{1,5},{5,9},... | collective-permute-start | bytes 393224 | tf_op jit(solution)/shard_map/ppermute | solution.py:191
  11.3 0.1 collective-permute-start.8
  11.4 0.1 copy.12
  11.5 0.1 copy.8
  11.6 3.2 %collective-permute-done.1.refs_5_ = bf16[256,256]{1,0:T(8,128)(2,1)S(1)} collective-permute-done((bf16[256,256]{1,0:T(8,128)(2,1)S(1)}, bf16[256,256]{1,0:T(8,128)(2,1)S(1)}, u32[]{:S(2)}, u32[]{:S(2)}) %collective-permute-start.1) | collective-permute-done | bytes 131104 | tf_op jit(solution)/shard_map/ppermute | solution.py:191
  14.8 3.6 %collective-permute-start.5 = (bf16[128,256]{1,0:T(8,128)(2,1)S(1)}, bf16[128,256]{1,0:T(8,128)(2,1)S(1)}, u32[]{:S(2)}, u32[]{:S(2)}) collective-permute-start(bf16[128,256]{1,0:T(8,128)(2,1)S(1)} %slice.8), channel_id=1, source_target_pairs={{0,8},{4,12},{8,14},{12,10},{14,6},{10,2},{6,0},{2,4},{1,9},{5,13}... | collective-permute-start | bytes 196616 | tf_op jit(solution)/shard_map/ppermute | solution.py:191
  18.4 1.1 %collective-permute-done.3.refs_6_ = bf16[256,256]{1,0:T(8,128)(2,1)S(1)} collective-permute-done((bf16[256,256]{1,0:T(8,128)(2,1)S(1)}, bf16[256,256]{1,0:T(8,128)(2,1)S(1)}, u32[]{:S(2)}, u32[]{:S(2)}) %collective-permute-start.3) | collective-permute-done | bytes 131104 | tf_op jit(solution)/shard_map/ppermute | solution.py:191
  19.5 1.1 %collective-permute-start.2 = (bf16[256,256]{1,0:T(8,128)(2,1)S(1)}, bf16[256,256]{1,0:T(8,128)(2,1)S(1)}, u32[]{:S(2)}, u32[]{:S(2)}) collective-permute-start(bf16[256,256]{1,0:T(8,128)(2,1)S(1)} %collective-permute-done.1.refs_5_), channel_id=1, source_target_pairs={{0,4},{4,8},{8,12},{12,14},{14,10},{10,6},{6,2},{2,0},{1,5},{5,9},... | collective-permute-start | bytes 393224 | tf_op jit(solution)/shard_map/ppermute | solution.py:191
  20.6 1.0 %collective-permute-start.4 = (bf16[256,256]{1,0:T(8,128)(2,1)S(1)}, bf16[256,256]{1,0:T(8,128)(2,1)S(1)}, u32[]{:S(2)}, u32[]{:S(2)}) collective-permute-start(bf16[256,256]{1,0:T(8,128)(2,1)S(1)} %collective-permute-done.3.refs_6_), channel_id=1, source_target_pairs={{0,2},{4,0},{8,4},{12,8},{14,12},{10,14},{6,10},{2,6},{1,3},{5,1},... | collective-permute-start | bytes 393224 | tf_op jit(solution)/shard_map/ppermute | solution.py:191
  21.6 1.3 %sink_product.1.refs_0_ = bf16[2,2,512,512]{3,2,1,0:T(8,128)(2,1)S(1)} custom-call(bf16[2,2,256,256]{3,2,1,0:T(8,128)(2,1)S(1)} %bitcast.18, bf16[2,512,512]{2,1,0:T(8,128)(2,1)S(1)} %reshape.9.own_ref, bf16[2,512,512]{2,1,0:T(8,128)(2,1)S(1)} %collective-permute-done.other_ref), custom_call_target="tpu_custom_call" | custom-call | flops 1073741824 | bytes 5242880 | tf_op jit(solution)/shard_map/sink_product/pallas_call | solution.py:173
  22.9 0.1 collective-permute-start.6
  23.0 1.8 %traces.1.refs_6_ = f32[2,256,256]{2,1,0:T(8,128)S(1)} custom-call(bf16[2,2,512,512]{3,2,1,0:T(8,128)(2,1)S(1)} %sink_product.1.refs_0_, bf16[2,512,256]{2,1,0:T(8,128)(2,1)S(1)} %bitcast.16, bf16[256,256]{1,0:T(8,128)(2,1)S(1)} %bitcast.24, bf16[256,256]{1,0:T(8,128)(2,1)S(1)} %collective-permute-done.7.refs_3_, ...), custom_call_target="tpu_custom_call" | custom-call | flops 1342177280 | bytes 4194304 | tf_op jit(solution)/shard_map/traces/pallas_call | solution.py:152
  24.7 4.4 %collective-permute-done.6.refs_5_ = bf16[128,256]{1,0:T(8,128)(2,1)S(1)} collective-permute-done((bf16[128,256]{1,0:T(8,128)(2,1)S(1)}, bf16[128,256]{1,0:T(8,128)(2,1)S(1)}, u32[]{:S(2)}, u32[]{:S(2)}) %collective-permute-start.6) | collective-permute-done | bytes 65568 | tf_op jit(solution)/shard_map/ppermute | solution.py:191
  29.2 2.1 %traces_last.1 = f32[2,2,4,4]{3,2,1,0:T(4,128)} custom-call(bf16[2,2,512,512]{3,2,1,0:T(8,128)(2,1)S(1)} %sink_product.1.refs_0_, bf16[2,512,256]{2,1,0:T(8,128)(2,1)S(1)} %bitcast.17, bf16[256,256]{1,0:T(8,128)(2,1)S(1)} %collective-permute-done.2.refs_2_, bf16[256,256]{1,0:T(8,128)(2,1)S(1)} %collective-permute-done.4.refs_3_, ...), custom_call_target="tpu_custom_call" | custom-call | flops 805306368 | bytes 4194304 | tf_op jit(solution)/shard_map/traces_last/pallas_call | solution.py:152
  (21 shorter events, 0.1 us)
Async XLA Ops:
  0.0 1.7 %copy-start = (bf16[2,9,128,2,256]{4,3,2,1,0:T(2,128)(2,1)S(1)}, bf16[2,9,128,2,256]{4,3,2,1,0:T(2,128)(2,1)}, u32[]{:S(2)}) copy-start(bf16[2,9,128,2,256]{4,3,2,1,0:T(2,128)(2,1)} %bank_ref.2) | copy-start | bytes 7077892
  1.7 0.7 %copy-start.2 = (s32[4]{0:T(128)S(1)}, s32[4]{0:T(128)}, u32[]{:S(2)}) copy-start(s32[4]{0:T(128)} %mom_ref.3) | copy-start | bytes 52
  2.3 0.7 %copy-start.4 = (s32[4]{0:T(128)S(1)}, s32[4]{0:T(128)}, u32[]{:S(2)}) copy-start(s32[4]{0:T(128)} %disp_ref.3) | copy-start | bytes 52
  3.0 2.0 %copy-start.1 = (bf16[1,9,32,2,256]{4,3,2,1,0:T(2,128)(2,1)S(1)}, bf16[1,9,32,2,256]{4,3,2,1,0:T(2,128)(2,1)}, u32[]{:S(2)}) copy-start(bf16[1,9,32,2,256]{4,3,2,1,0:T(2,128)(2,1)} %bank_ref.3) | copy-start | bytes 884740
  3.0 2.0 %copy-start.3 = (s32[4]{0:T(128)S(1)}, s32[4]{0:T(128)}, u32[]{:S(2)}) copy-start(s32[4]{0:T(128)} %mom_ref.3) | copy-start | bytes 52
  3.0 2.0 %copy-start.5 = (s32[4]{0:T(128)S(1)}, s32[4]{0:T(128)}, u32[]{:S(2)}) copy-start(s32[4]{0:T(128)} %disp_ref.3) | copy-start | bytes 52
  3.0 8.5 %copy-start.6 = (bf16[2,1,256,2,256]{4,3,2,1,0:T(2,128)(2,1)S(1)}, bf16[2,1,256,2,256]{4,3,2,1,0:T(2,128)(2,1)}, u32[]{:S(2)}) copy-start(bf16[2,1,256,2,256]{4,3,2,1,0:T(2,128)(2,1)} %param.6) | copy-start | bytes 1572868
  3.7 7.8 %copy-start.7 = (bf16[1,2,256,2,256]{4,3,2,1,0:T(2,128)(2,1)S(1)}, bf16[1,2,256,2,256]{4,3,2,1,0:T(2,128)(2,1)}, u32[]{:S(2)}) copy-start(bf16[1,2,256,2,256]{4,3,2,1,0:T(2,128)(2,1)} %param.7) | copy-start | bytes 1572868
  4.4 16.2 %collective-permute-start = (bf16[2,512,512]{2,1,0:T(8,128)(2,1)S(1)}, bf16[2,512,512]{2,1,0:T(8,128)(2,1)S(1)}, u32[]{:S(2)}, u32[]{:S(2)}) collective-permute-start(bf16[2,512,512]{2,1,0:T(8,128)(2,1)S(1)} %reshape.9.own_ref), channel_id=1, source_target_pairs={{0,1},{1,0},{2,3},{3,2},{4,5},{5,4},{6,7},{7,6},{8,9},{9,8},{10,11... | collective-permute-start | bytes 3145736 | tf_op jit(solution)/shard_map/ppermute | solution.py:172
  5.7 9.1 %collective-permute-start.1 = (bf16[256,256]{1,0:T(8,128)(2,1)S(1)}, bf16[256,256]{1,0:T(8,128)(2,1)S(1)}, u32[]{:S(2)}, u32[]{:S(2)}) collective-permute-start(bf16[256,256]{1,0:T(8,128)(2,1)S(1)} %bitcast.20), channel_id=1, source_target_pairs={{0,8},{4,12},{8,14},{12,10},{14,6},{10,2},{6,0},{2,4},{1,9},{5,13}... | collective-permute-start | bytes 393224 | tf_op jit(solution)/shard_map/ppermute | solution.py:191
  9.4 10.1 %collective-permute-start.3 = (bf16[256,256]{1,0:T(8,128)(2,1)S(1)}, bf16[256,256]{1,0:T(8,128)(2,1)S(1)}, u32[]{:S(2)}, u32[]{:S(2)}) collective-permute-start(bf16[256,256]{1,0:T(8,128)(2,1)S(1)} %bitcast.21), channel_id=1, source_target_pairs={{0,6},{4,2},{8,0},{12,4},{14,8},{10,12},{6,14},{2,10},{1,7},{5,3},... | collective-permute-start | bytes 393224 | tf_op jit(solution)/shard_map/ppermute | solution.py:191
  9.4 13.5 %collective-permute-start.7 = (bf16[256,256]{1,0:T(8,128)(2,1)S(1)}, bf16[256,256]{1,0:T(8,128)(2,1)S(1)}, u32[]{:S(2)}, u32[]{:S(2)}) collective-permute-start(bf16[256,256]{1,0:T(8,128)(2,1)S(1)} %bitcast.22), channel_id=1, source_target_pairs={{0,4},{4,8},{8,12},{12,14},{14,10},{10,6},{6,2},{2,0},{1,5},{5,9},... | collective-permute-start | bytes 393224 | tf_op jit(solution)/shard_map/ppermute | solution.py:191
  11.3 11.6 %collective-permute-start.8 = (bf16[256,256]{1,0:T(8,128)(2,1)S(1)}, bf16[256,256]{1,0:T(8,128)(2,1)S(1)}, u32[]{:S(2)}, u32[]{:S(2)}) collective-permute-start(bf16[256,256]{1,0:T(8,128)(2,1)S(1)} %bitcast.23), channel_id=1, source_target_pairs={{0,2},{4,0},{8,4},{12,8},{14,12},{10,14},{6,10},{2,6},{1,3},{5,1},... | collective-permute-start | bytes 393224 | tf_op jit(solution)/shard_map/ppermute | solution.py:191
  14.8 9.9 %collective-permute-start.5 = (bf16[128,256]{1,0:T(8,128)(2,1)S(1)}, bf16[128,256]{1,0:T(8,128)(2,1)S(1)}, u32[]{:S(2)}, u32[]{:S(2)}) collective-permute-start(bf16[128,256]{1,0:T(8,128)(2,1)S(1)} %slice.8), channel_id=1, source_target_pairs={{0,8},{4,12},{8,14},{12,10},{14,6},{10,2},{6,0},{2,4},{1,9},{5,13}... | collective-permute-start | bytes 196616 | tf_op jit(solution)/shard_map/ppermute | solution.py:191
  19.5 9.7 %collective-permute-start.2 = (bf16[256,256]{1,0:T(8,128)(2,1)S(1)}, bf16[256,256]{1,0:T(8,128)(2,1)S(1)}, u32[]{:S(2)}, u32[]{:S(2)}) collective-permute-start(bf16[256,256]{1,0:T(8,128)(2,1)S(1)} %collective-permute-done.1.refs_5_), channel_id=1, source_target_pairs={{0,4},{4,8},{8,12},{12,14},{14,10},{10,6},{6,2},{2,0},{1,5},{5,9},... | collective-permute-start | bytes 393224 | tf_op jit(solution)/shard_map/ppermute | solution.py:191
  20.6 8.6 %collective-permute-start.4 = (bf16[256,256]{1,0:T(8,128)(2,1)S(1)}, bf16[256,256]{1,0:T(8,128)(2,1)S(1)}, u32[]{:S(2)}, u32[]{:S(2)}) collective-permute-start(bf16[256,256]{1,0:T(8,128)(2,1)S(1)} %collective-permute-done.3.refs_6_), channel_id=1, source_target_pairs={{0,2},{4,0},{8,4},{12,8},{14,12},{10,14},{6,10},{2,6},{1,3},{5,1},... | collective-permute-start | bytes 393224 | tf_op jit(solution)/shard_map/ppermute | solution.py:191
  22.9 6.3 %collective-permute-start.6 = (bf16[128,256]{1,0:T(8,128)(2,1)S(1)}, bf16[128,256]{1,0:T(8,128)(2,1)S(1)}, u32[]{:S(2)}, u32[]{:S(2)}) collective-permute-start(bf16[128,256]{1,0:T(8,128)(2,1)S(1)} %slice.9), channel_id=1, source_target_pairs={{0,6},{4,2},{8,0},{12,4},{14,8},{10,12},{6,14},{2,10},{1,7},{5,3},... | collective-permute-start | bytes 196616 | tf_op jit(solution)/shard_map/ppermute | solution.py:191

commit v3 on v1

v3 whole, which is shorter than its diff:
```python
import functools

import jax
import jax.numpy as jnp
from jax import lax
from jax.experimental import pallas as pl
from jax.experimental.pallas import tpu as pltpu
from jax.sharding import PartitionSpec as P

NDISP = 3
VMEM_LIMIT = 40 * 1024 * 1024
WHOLE = pl.BlockSpec(memory_space=pltpu.VMEM)
IN_HBM = pl.BlockSpec(memory_space=pltpu.HBM)


def source_kernel(mom_ref, disp_ref, bank_ref, out_ref, mom, disp, bank, arrived):
    copies = [
        pltpu.make_async_copy(mom_ref, mom, arrived.at[0]),
        pltpu.make_async_copy(disp_ref, disp, arrived.at[1]),
        pltpu.make_async_copy(bank_ref, bank, arrived.at[2]),
    ]
    for copy in copies:
        copy.start()
    for copy in copies:
        copy.wait()
    for a in range(out_ref.shape[1]):
        out_ref[:, a] = bank[:, mom[a] * NDISP + disp[a]]


def chosen_source_rows(bank, op_mom, op_disp):
    nop = op_mom.shape[0]
    return pl.pallas_call(
        source_kernel,
        out_shape=pltpu.VMEM((bank.shape[0], nop) + bank.shape[2:], bank.dtype),
        in_specs=[IN_HBM] * 3,
        out_specs=WHOLE,
        scratch_shapes=[
            pltpu.SMEM((nop,), jnp.int32),
            pltpu.SMEM((nop,), jnp.int32),
            pltpu.VMEM(bank.shape, bank.dtype),
            pltpu.SemaphoreType.DMA((3,)),
        ],
        compiler_params=pltpu.CompilerParams(vmem_limit_bytes=VMEM_LIMIT),
        name="source_rows",
    )(*(pltpu.with_memory_space_constraint(x, pltpu.HBM) for x in (op_mom, op_disp, bank)))


def planar(matrices):
    return jnp.swapaxes(matrices, 1, 2)


def swap(array, mask, count):
    return lax.ppermute(array, "ta", [(k, k ^ mask) for k in range(count)])


def sink_kernel(mom_ref, disp_ref, forward_ref, own_ref, other_ref, out_ref, mom, disp, forward, rows, arrived):
    times, nop = rows.shape[:2]
    numbers = [
        pltpu.make_async_copy(mom_ref, mom, arrived.at[nop]),
        pltpu.make_async_copy(disp_ref, disp, arrived.at[nop + 1]),
    ]
    whole = pltpu.make_async_copy(forward_ref, forward, arrived.at[nop + 2])
    for copy in numbers + [whole]:
        copy.start()
    for copy in numbers:
        copy.wait()
    entries = [mom[a] * NDISP + disp[a] for a in range(nop)]
    copies = [
        pltpu.make_async_copy(own_ref.at[:, e], rows.at[:, a], arrived.at[a]) for a, e in enumerate(entries)
    ]
    for copy in copies:
        copy.start()
    whole.wait()
    lefts = []
    for t in range(times):
        parts = jnp.swapaxes(forward[t, 0], 0, 1)
        real, imag = parts[0].T, parts[1].T
        for_real = jnp.concatenate([real, -imag], axis=1)
        for_imag = jnp.concatenate([imag, real], axis=1)
        lefts.append(jnp.concatenate([for_real, for_imag], axis=0))
    mine = lax.axis_index("sa")

    def multiply(half, pick):
        for t in range(times):
            chosen = [jnp.swapaxes(pick(t, a), 0, 1) for a in range(nop)]
            right = jnp.concatenate([jnp.concatenate([x[0], x[1]], axis=1) for x in chosen], axis=0)
            out_ref[t, half] = lax.dot_general(
                lefts[t], right, (((1,), (1,)), ((), ())), preferred_element_type=jnp.float32
            ).astype(jnp.bfloat16)

    multiply(1 - mine, lambda t, a: other_ref[t, entries[a]])
    for copy in copies:
        copy.wait()
    multiply(mine, lambda t, a: rows[t, a])


def sink_products(forward, own_bank, other_bank, op_mom, op_disp):
    nop = op_mom.shape[0]
    times, order = forward.shape[0], forward.shape[2]
    return pl.pallas_call(
        sink_kernel,
        out_shape=jax.ShapeDtypeStruct((times, 2, 2 * order, nop * own_bank.shape[2]), jnp.bfloat16),
        in_specs=[IN_HBM] * 4 + [WHOLE],
        out_specs=WHOLE,
        scratch_shapes=[
            pltpu.SMEM((nop,), jnp.int32),
            pltpu.SMEM((nop,), jnp.int32),
            pltpu.VMEM(forward.shape, forward.dtype),
            pltpu.VMEM((times, nop) + own_bank.shape[2:], own_bank.dtype),
            pltpu.SemaphoreType.DMA((nop + 3,)),
        ],
        compiler_params=pltpu.CompilerParams(vmem_limit_bytes=VMEM_LIMIT),
        cost_estimate=pl.CostEstimate(
            flops=2 * times * 2 * order * 2 * order * order * nop,
            bytes_accessed=5 * 1024 * 1024,
            transcendentals=0,
        ),
        name="sink_product",
    )(
        *(pltpu.with_memory_space_constraint(x, pltpu.HBM) for x in (op_mom, op_disp, forward, own_bank)),
        other_bank,
    )


def trace_kernel(masks, known, last, nop, rows, *refs):
    product_ref, back_ref = refs[:2]
    me = 0 if known else lax.axis_index("ta")
    piece_refs = refs[2 : 2 + len(masks)]
    before_ref = refs[2 + len(masks)] if len(refs) == 4 + len(masks) else None
    out_ref = refs[-1]
    times = product_ref.shape[0]
    order = back_ref.shape[2]
    totals = [None if before_ref is None else before_ref[t] for t in range(times)]
    for mask, piece_ref in zip(masks, piece_refs):
        height = piece_ref.shape[0] // 2
        real, imag = piece_ref[:height], piece_ref[height:]
        for_real = jnp.concatenate([real, -imag], axis=1)
        for_imag = jnp.concatenate([imag, real], axis=1)
        left = jnp.concatenate([for_real, for_imag], axis=0)
        start = pl.multiple_of((me ^ mask) * rows, rows)
        for t in range(times):
            reverse = jnp.dot(left, back_ref[t], preferred_element_type=jnp.float32)
            high = reverse.astype(jnp.bfloat16)
            low = (reverse - high.astype(jnp.float32)).astype(jnp.bfloat16)
            blocks = []
            for part in range(2):
                two = [
                    product_ref[t, half, pl.ds(part * order + start, rows), :]
                    for half in range(2)
                ]
                width = two[0].shape[1] // nop
                for a in range(nop):
                    blocks.append(
                        jnp.concatenate([x[:, a * width : (a + 1) * width] for x in two], axis=1)
                    )
            sink = jnp.concatenate(blocks, axis=0)
            nt = (((1,), (1,)), ((), ()))
            added = lax.dot_general(sink, high, nt, preferred_element_type=jnp.float32)
            added += lax.dot_general(sink, low, nt, preferred_element_type=jnp.float32)
            totals[t] = added if totals[t] is None else totals[t] + added
    if not last:
        for t in range(times):
            out_ref[t] = totals[t]
        return
    side = totals[0].shape[0]
    shape = (2, nop, rows, 2 * nop * rows)
    row_part = lax.broadcasted_iota(jnp.int32, shape, 0)
    row_at = lax.broadcasted_iota(jnp.int32, shape, 2)
    column_at = lax.broadcasted_iota(jnp.int32, shape, 3)
    column_part = (column_at >= nop * rows).astype(jnp.int32)
    same = row_at == lax.rem(column_at, rows)
    sign = jnp.where(row_part == 0, 1.0, -1.0)
    weights = (
        jnp.where(same & (row_part == column_part), sign, 0.0),
        jnp.where(same & (row_part != column_part), 1.0, 0.0),
    )
    sums = []
    for t in range(times):
        table = totals[t].reshape(shape)
        for weight in weights:
            sums.append((table * weight).sum(axis=(0, 2)))
    left_over = jnp.concatenate(sums, axis=0)
    height = left_over.shape[0]
    terms = []
    for _ in range(3):
        terms.append(left_over.astype(jnp.bfloat16))
        left_over = left_over - terms[-1].astype(jnp.float32)
    of_operator = (
        lax.rem(lax.broadcasted_iota(jnp.int32, (side, nop), 0) // rows, nop)
        == lax.broadcasted_iota(jnp.int32, (side, nop), 1)
    ).astype(jnp.bfloat16)
    paired = jnp.dot(jnp.concatenate(terms, axis=0), of_operator, preferred_element_type=jnp.float32)
    paired = (paired[:height] + (paired[height : 2 * height] + paired[2 * height :])) / order
    for t in range(times):
        for part in range(2):
            at = (2 * t + part) * nop
            out_ref[t, part] = paired[at : at + nop]


def traces(product, back, pieces, nop, rows, known=False, before=None, last=False):
    times, order = product.shape[0], back.shape[2]
    side = 2 * nop * rows
    operands = [product, back, *pieces.values()] + ([] if before is None else [before])
    shape = (times, 2, nop, nop) if last else (times, side, side)
    flops = 2 * times * len(pieces) * side * (2 * order * order + 2 * side * order)
    return pl.pallas_call(
        functools.partial(trace_kernel, tuple(pieces), known, last, nop, rows),
        out_shape=jax.ShapeDtypeStruct(shape, jnp.float32),
        in_specs=[WHOLE] * len(operands),
        out_specs=WHOLE,
        compiler_params=pltpu.CompilerParams(vmem_limit_bytes=VMEM_LIMIT),
        cost_estimate=pl.CostEstimate(flops=flops, bytes_accessed=4 * 1024 * 1024, transcendentals=0),
        name="traces_last" if last else "traces",
    )(*operands)


def per_device(forward, backward, sink_bank, source_bank, op_mom, op_disp, n_times):
    nop = op_mom.shape[0]
    order = forward.shape[2]
    times = forward.shape[0]
    own_rows = source_bank.shape[2]

    source_raw = chosen_source_rows(source_bank, op_mom, op_disp)
    source = jnp.transpose(source_raw[0], (2, 0, 1, 3)).reshape(-1, order)
    other_bank = lax.ppermute(sink_bank, "sa", [(0, 1), (1, 0)])
    product = sink_products(
        forward,
        sink_bank,
        other_bank,
        op_mom,
        op_disp,
    )
    back = planar(backward[0]).reshape(times, 2 * order, order)

    rows = order // (2 * nop)
    far_mask = n_times // 2
    if own_rows == rows and n_times == 2 * far_mask and far_mask & (far_mask - 1) == 0:
        near = range(1, far_mask)
        far = swap(source, far_mask, n_times)
        early = {0: source} | {m: swap(source, m, n_times) for m in near}
        early[far_mask] = far
        far, product = lax.optimization_barrier((far, product))
        late = {far_mask ^ m: swap(far, m, n_times) for m in near}
        first = traces(product, back, early, nop, rows)
        result = traces(product, back, late, nop, rows, before=first, last=True)
    else:
        whole = lax.all_gather(source.reshape(2, nop, own_rows, order), "ta", axis=2, tiled=True)
        pieces = {
            k: whole[:, :, k * rows : (k + 1) * rows].reshape(-1, order) for k in range(order // rows)
        }
        result = traces(product, back, pieces, nop, rows, known=True, last=True)
    return result[:, None]


def solution(mesh):
    placed = (
        P(("cfg", "ta"), "sa", None, None, None),
        P(("cfg", "sa"), "ta", None, None, None),
        P(("cfg", "ta"), None, "sa", None, None),
        P(("cfg", "sa"), None, "ta", None, None),
        P(),
        P(),
    )
    return jax.shard_map(
        functools.partial(per_device, n_times=mesh.shape["ta"]),
        mesh=mesh,
        in_specs=placed,
        out_specs=P(("cfg", "ta"), "sa", None, None, None),
        check_vma=False,
    )
```

time: 49.5 us -> 24.2 us (0.49)
  between operations: 13.4 us -> 0.05 us
  local copies, waits for them, and re-layouts: 9.28 us -> 0.1 us
  other arithmetic: 5.47 us -> 0 us
  waiting for transfers between devices: 2.79 us -> 4.69 us
  Pallas kernels: 6.69 us -> 8.12 us
    another operation x3 -> x0, other arithmetic: 4.56 us -> none  [the longest x1 1.96 us: chosen_entries(): return jnp.stack(picked, axis=1)]
    dynamic_slice x3 -> x0, local copies, waits for them, and re-layouts: 3.52 us -> none  [the longest x2 2.83 us: chosen_entries(): lax.dynamic_index_in_dim(bank, wanted[a], axis=1, keepdims=False)]
    another operation x1 -> x0, local copies, waits for them, and re-layouts: 3.16 us -> none  [places(): return jnp.stack([walk[(spot + k) % n_times] for k in offsets])]
    ppermute x9 -> x8, waiting for transfers between devices: 2.79 us -> 4.69 us  [the longest x7 4.69 us: swap(): return lax.ppermute(array, 'ta', [(k, k ^ mask) for k in range(count)])]
    pallas_call x3 -> x4, Pallas kernels: 6.69 us -> 8.12 us  [the longest x2 3.71 us: traces(): pl.pallas_call(functools.partial(trace_kernel, tuple(pieces), known, last...]
    transpose x1, local copies, waits for them, and re-layouts: 1.12 us -> 0.07 us  [planar(): return jnp.swapaxes(matrices, 1, 2)]
    reshape x1 -> x0, local copies, waits for them, and re-layouts: 0.71 us -> none  [per_device(): sink_own = chosen_entries(sink_bank, wanted).reshape(times, -1, 2 * order)]
    slice x3 -> x0, local copies, waits for them, and re-layouts: 0.68 us -> none  [the longest x1 0.67 us: chosen_entries(): wanted[a]]
  transfers between devices with their start and end apart: 9 -> 8, of which waited for: 1 -> 5; matrix products, arithmetic and copies ran while one was open for 18% -> 0% of each run, Pallas kernels for 8% -> 26%
where the time goes in v3:
time: 24.2 us; the launch traced here: 24 us
  starting transfers between devices  11.1 us (46%)
  Pallas kernels  8.12 us (34%)
  waiting for transfers between devices  4.69 us (19%)
    ppermute x7, starting transfers between devices, swap(): return lax.ppermute(array, 'ta', [(k, k ^ mask) for k in range(count)])  10.6 us
    ppermute x7, waiting for transfers between devices, swap(): return lax.ppermute(array, 'ta', [(k, k ^ mask) for k in range(count)])  4.69 us
    pallas_call x2, Pallas kernels, traces(): pl.pallas_call(functools.partial(trace_kernel, tuple(pieces), known, last...  3.71 us
    pallas_call x1, Pallas kernels, sink_products(): pl.pallas_call(sink_kernel, out_shape=jax.ShapeDtypeStruct((times, 2, 2 *...  3.41 us
    pallas_call x1, Pallas kernels, chosen_source_rows(): pl.pallas_call(source_kernel, out_shape=pltpu.VMEM((bank.shape[0], nop) +...  1 us
  transfers between devices with their start and end apart: 8, of which 5 were waited for; matrix products, arithmetic and copies ran while one was open for 0% of the time, Pallas kernels for 26%

profile of v3, /device:TPU:0, one launch (start us, length us, event | category | flops | bytes accessed | tf_op | source)
XLA Modules:
  0.0 24.0 jit_solution(10602808621209563413)
XLA Ops:
  0.0 0.5 %collective-permute-start.1 = (bf16[2,9,128,2,256]{4,3,2,1,0:T(2,128)(2,1)}, bf16[2,9,128,2,256]{4,3,2,1,0:T(2,128)(2,1)S(1)}, u32[]{:S(2)}, u32[]{:S(2)}) collective-permute-start(bf16[2,9,128,2,256]{4,3,2,1,0:T(2,128)(2,1)} %own_ref.1), channel_id=1, source_target_pairs={{0,1},{1,0},{2,3},{3,2},{4,5},{5,4},{6,7},{7,6},{8,9},{9,8},{10,11... | collective-permute-start | bytes 7077896 | tf_op jit(solution)/shard_map/ppermute | solution.py:225
  0.5 1.0 %source_rows.1 = bf16[1,4,32,2,256]{4,3,2,1,0:T(2,128)(2,1)S(1)} custom-call(s32[4]{0:T(128)} %mom_ref.3, s32[4]{0:T(128)} %disp_ref.3, bf16[1,9,32,2,256]{4,3,2,1,0:T(2,128)(2,1)} %bank_ref.1), custom_call_target="tpu_custom_call" | custom-call | tf_op jit(solution)/shard_map/source_rows/pallas_call | solution.py:32
  1.5 0.0 copy-start
  1.5 3.7 %collective-permute-start = (bf16[256,256]{1,0:T(8,128)(2,1)S(1)}, bf16[256,256]{1,0:T(8,128)(2,1)S(1)}, u32[]{:S(2)}, u32[]{:S(2)}) collective-permute-start(bf16[256,256]{1,0:T(8,128)(2,1)S(1)} %bitcast.14), channel_id=1, source_target_pairs={{0,8},{2,10},{4,12},{6,14},{8,0},{10,2},{12,4},{14,6},{1,9},{3,11}... | collective-permute-start | bytes 393224 | tf_op jit(solution)/shard_map/ppermute | solution.py:53
  5.1 1.5 %collective-permute-start.5 = (bf16[256,256]{1,0:T(8,128)(2,1)S(1)}, bf16[256,256]{1,0:T(8,128)(2,1)S(1)}, u32[]{:S(2)}, u32[]{:S(2)}) collective-permute-start(bf16[256,256]{1,0:T(8,128)(2,1)S(1)} %bitcast.15), channel_id=1, source_target_pairs={{0,2},{2,0},{4,6},{6,4},{8,10},{10,8},{12,14},{14,12},{1,3},{3,1},... | collective-permute-start | bytes 393224 | tf_op jit(solution)/shard_map/ppermute | solution.py:53
  6.6 1.6 %collective-permute-start.6 = (bf16[256,256]{1,0:T(8,128)(2,1)S(1)}, bf16[256,256]{1,0:T(8,128)(2,1)S(1)}, u32[]{:S(2)}, u32[]{:S(2)}) collective-permute-start(bf16[256,256]{1,0:T(8,128)(2,1)S(1)} %bitcast.16), channel_id=1, source_target_pairs={{0,4},{2,6},{4,0},{6,2},{8,12},{10,14},{12,8},{14,10},{1,5},{3,7},... | collective-permute-start | bytes 393224 | tf_op jit(solution)/shard_map/ppermute | solution.py:53
  8.2 0.4 %collective-permute-start.7 = (bf16[256,256]{1,0:T(8,128)(2,1)S(1)}, bf16[256,256]{1,0:T(8,128)(2,1)S(1)}, u32[]{:S(2)}, u32[]{:S(2)}) collective-permute-start(bf16[256,256]{1,0:T(8,128)(2,1)S(1)} %bitcast.17), channel_id=1, source_target_pairs={{0,6},{2,4},{4,2},{6,0},{8,14},{10,12},{12,10},{14,8},{1,7},{3,5},... | collective-permute-start | bytes 393224 | tf_op jit(solution)/shard_map/ppermute | solution.py:53
  8.6 0.0 collective-permute-done.1.other_ref
  8.6 3.4 %sink_product.1.refs_0_ = bf16[2,2,512,512]{3,2,1,0:T(8,128)(2,1)S(1)} custom-call(s32[4]{0:T(128)} %mom_ref.3, s32[4]{0:T(128)} %disp_ref.3, bf16[2,1,256,2,256]{4,3,2,1,0:T(2,128)(2,1)} %forward_ref.1, bf16[2,9,128,2,256]{4,3,2,1,0:T(2,128)(2,1)} %own_ref.1, bf16[2,9,128,2,256]{4,3,2,1,0:T(2,128)(2,1)S(1)} %collective-permute-done.1.other_ref), custom_call_target="tpu_custom_call" | custom-call | flops 1073741824 | bytes 5242880 | tf_op jit(solution)/shard_map/sink_product/pallas_call | solution.py:100
  12.1 0.2 collective-permute-done.refs_6_
  12.2 1.5 %collective-permute-start.2 = (bf16[256,256]{1,0:T(8,128)(2,1)S(1)}, bf16[256,256]{1,0:T(8,128)(2,1)S(1)}, u32[]{:S(2)}, u32[]{:S(2)}) collective-permute-start(bf16[256,256]{1,0:T(8,128)(2,1)S(1)} %collective-permute-done.refs_6_), channel_id=1, source_target_pairs={{0,2},{2,0},{4,6},{6,4},{8,10},{10,8},{12,14},{14,12},{1,3},{3,1},... | collective-permute-start | bytes 393224 | tf_op jit(solution)/shard_map/ppermute | solution.py:53
  13.8 1.4 %collective-permute-start.3 = (bf16[256,256]{1,0:T(8,128)(2,1)S(1)}, bf16[256,256]{1,0:T(8,128)(2,1)S(1)}, u32[]{:S(2)}, u32[]{:S(2)}) collective-permute-start(bf16[256,256]{1,0:T(8,128)(2,1)S(1)} %collective-permute-done.refs_6_), channel_id=1, source_target_pairs={{0,4},{2,6},{4,0},{6,2},{8,12},{10,14},{12,8},{14,10},{1,5},{3,7},... | collective-permute-start | bytes 393224 | tf_op jit(solution)/shard_map/ppermute | solution.py:53
  15.2 0.0 collective-permute-done.5.refs_3_
  15.2 0.5 %collective-permute-start.4 = (bf16[256,256]{1,0:T(8,128)(2,1)S(1)}, bf16[256,256]{1,0:T(8,128)(2,1)S(1)}, u32[]{:S(2)}, u32[]{:S(2)}) collective-permute-start(bf16[256,256]{1,0:T(8,128)(2,1)S(1)} %collective-permute-done.refs_6_), channel_id=1, source_target_pairs={{0,6},{2,4},{4,2},{6,0},{8,14},{10,12},{12,10},{14,8},{1,7},{3,5},... | collective-permute-start | bytes 393224 | tf_op jit(solution)/shard_map/ppermute | solution.py:53
  15.7 0.0 copy-done
  15.7 0.1 copy.8
  15.8 0.0 collective-permute-done.6.refs_4_
  15.8 1.2 %collective-permute-done.7.refs_5_ = bf16[256,256]{1,0:T(8,128)(2,1)S(1)} collective-permute-done((bf16[256,256]{1,0:T(8,128)(2,1)S(1)}, bf16[256,256]{1,0:T(8,128)(2,1)S(1)}, u32[]{:S(2)}, u32[]{:S(2)}) %collective-permute-start.7) | collective-permute-done | bytes 131104 | tf_op jit(solution)/shard_map/ppermute | solution.py:53
  17.0 1.7 %traces.1.refs_5_ = f32[2,256,256]{2,1,0:T(8,128)S(1)} custom-call(bf16[2,2,512,512]{3,2,1,0:T(8,128)(2,1)S(1)} %sink_product.1.refs_0_, bf16[2,512,256]{2,1,0:T(8,128)(2,1)S(1)} %bitcast.11, bf16[256,256]{1,0:T(8,128)(2,1)S(1)} %bitcast.18, bf16[256,256]{1,0:T(8,128)(2,1)S(1)} %collective-permute-done.5.refs_3_, ...), custom_call_target="tpu_custom_call" | custom-call | flops 1342177280 | bytes 4194304 | tf_op jit(solution)/shard_map/traces/pallas_call | solution.py:206
  18.7 1.4 %collective-permute-done.2.refs_2_ = bf16[256,256]{1,0:T(8,128)(2,1)S(1)} collective-permute-done((bf16[256,256]{1,0:T(8,128)(2,1)S(1)}, bf16[256,256]{1,0:T(8,128)(2,1)S(1)}, u32[]{:S(2)}, u32[]{:S(2)}) %collective-permute-start.2) | collective-permute-done | bytes 131104 | tf_op jit(solution)/shard_map/ppermute | solution.py:53
  20.1 0.1 collective-permute-done.3.refs_3_
  20.2 1.9 %collective-permute-done.4.refs_4_ = bf16[256,256]{1,0:T(8,128)(2,1)S(1)} collective-permute-done((bf16[256,256]{1,0:T(8,128)(2,1)S(1)}, bf16[256,256]{1,0:T(8,128)(2,1)S(1)}, u32[]{:S(2)}, u32[]{:S(2)}) %collective-permute-start.4) | collective-permute-done | bytes 131104 | tf_op jit(solution)/shard_map/ppermute | solution.py:53
  22.1 2.0 %traces_last.1 = f32[2,2,4,4]{3,2,1,0:T(4,128)} custom-call(bf16[2,2,512,512]{3,2,1,0:T(8,128)(2,1)S(1)} %sink_product.1.refs_0_, bf16[2,512,256]{2,1,0:T(8,128)(2,1)S(1)} %bitcast.12, bf16[256,256]{1,0:T(8,128)(2,1)S(1)} %collective-permute-done.2.refs_2_, bf16[256,256]{1,0:T(8,128)(2,1)S(1)} %collective-permute-done.3.refs_3_, ...), custom_call_target="tpu_custom_call" | custom-call | flops 805306368 | bytes 4194304 | tf_op jit(solution)/shard_map/traces_last/pallas_call | solution.py:206
  (1 shorter events, 0.0 us)
Async XLA Ops:
  0.0 8.6 %collective-permute-start.1 = (bf16[2,9,128,2,256]{4,3,2,1,0:T(2,128)(2,1)}, bf16[2,9,128,2,256]{4,3,2,1,0:T(2,128)(2,1)S(1)}, u32[]{:S(2)}, u32[]{:S(2)}) collective-permute-start(bf16[2,9,128,2,256]{4,3,2,1,0:T(2,128)(2,1)} %own_ref.1), channel_id=1, source_target_pairs={{0,1},{1,0},{2,3},{3,2},{4,5},{5,4},{6,7},{7,6},{8,9},{9,8},{10,11... | collective-permute-start | bytes 7077896 | tf_op jit(solution)/shard_map/ppermute | solution.py:225
  1.5 14.2 %copy-start = (bf16[1,2,256,2,256]{4,3,2,1,0:T(2,128)(2,1)S(1)}, bf16[1,2,256,2,256]{4,3,2,1,0:T(2,128)(2,1)}, u32[]{:S(2)}) copy-start(bf16[1,2,256,2,256]{4,3,2,1,0:T(2,128)(2,1)} %param.7) | copy-start | bytes 1572868
  1.5 10.7 %collective-permute-start = (bf16[256,256]{1,0:T(8,128)(2,1)S(1)}, bf16[256,256]{1,0:T(8,128)(2,1)S(1)}, u32[]{:S(2)}, u32[]{:S(2)}) collective-permute-start(bf16[256,256]{1,0:T(8,128)(2,1)S(1)} %bitcast.14), channel_id=1, source_target_pairs={{0,8},{2,10},{4,12},{6,14},{8,0},{10,2},{12,4},{14,6},{1,9},{3,11}... | collective-permute-start | bytes 393224 | tf_op jit(solution)/shard_map/ppermute | solution.py:53
  5.1 10.1 %collective-permute-start.5 = (bf16[256,256]{1,0:T(8,128)(2,1)S(1)}, bf16[256,256]{1,0:T(8,128)(2,1)S(1)}, u32[]{:S(2)}, u32[]{:S(2)}) collective-permute-start(bf16[256,256]{1,0:T(8,128)(2,1)S(1)} %bitcast.15), channel_id=1, source_target_pairs={{0,2},{2,0},{4,6},{6,4},{8,10},{10,8},{12,14},{14,12},{1,3},{3,1},... | collective-permute-start | bytes 393224 | tf_op jit(solution)/shard_map/ppermute | solution.py:53
  6.6 9.2 %collective-permute-start.6 = (bf16[256,256]{1,0:T(8,128)(2,1)S(1)}, bf16[256,256]{1,0:T(8,128)(2,1)S(1)}, u32[]{:S(2)}, u32[]{:S(2)}) collective-permute-start(bf16[256,256]{1,0:T(8,128)(2,1)S(1)} %bitcast.16), channel_id=1, source_target_pairs={{0,4},{2,6},{4,0},{6,2},{8,12},{10,14},{12,8},{14,10},{1,5},{3,7},... | collective-permute-start | bytes 393224 | tf_op jit(solution)/shard_map/ppermute | solution.py:53
  8.2 8.8 %collective-permute-start.7 = (bf16[256,256]{1,0:T(8,128)(2,1)S(1)}, bf16[256,256]{1,0:T(8,128)(2,1)S(1)}, u32[]{:S(2)}, u32[]{:S(2)}) collective-permute-start(bf16[256,256]{1,0:T(8,128)(2,1)S(1)} %bitcast.17), channel_id=1, source_target_pairs={{0,6},{2,4},{4,2},{6,0},{8,14},{10,12},{12,10},{14,8},{1,7},{3,5},... | collective-permute-start | bytes 393224 | tf_op jit(solution)/shard_map/ppermute | solution.py:53
  12.2 7.9 %collective-permute-start.2 = (bf16[256,256]{1,0:T(8,128)(2,1)S(1)}, bf16[256,256]{1,0:T(8,128)(2,1)S(1)}, u32[]{:S(2)}, u32[]{:S(2)}) collective-permute-start(bf16[256,256]{1,0:T(8,128)(2,1)S(1)} %collective-permute-done.refs_6_), channel_id=1, source_target_pairs={{0,2},{2,0},{4,6},{6,4},{8,10},{10,8},{12,14},{14,12},{1,3},{3,1},... | collective-permute-start | bytes 393224 | tf_op jit(solution)/shard_map/ppermute | solution.py:53
  13.8 6.4 %collective-permute-start.3 = (bf16[256,256]{1,0:T(8,128)(2,1)S(1)}, bf16[256,256]{1,0:T(8,128)(2,1)S(1)}, u32[]{:S(2)}, u32[]{:S(2)}) collective-permute-start(bf16[256,256]{1,0:T(8,128)(2,1)S(1)} %collective-permute-done.refs_6_), channel_id=1, source_target_pairs={{0,4},{2,6},{4,0},{6,2},{8,12},{10,14},{12,8},{14,10},{1,5},{3,7},... | collective-permute-start | bytes 393224 | tf_op jit(solution)/shard_map/ppermute | solution.py:53
  15.2 6.9 %collective-permute-start.4 = (bf16[256,256]{1,0:T(8,128)(2,1)S(1)}, bf16[256,256]{1,0:T(8,128)(2,1)S(1)}, u32[]{:S(2)}, u32[]{:S(2)}) collective-permute-start(bf16[256,256]{1,0:T(8,128)(2,1)S(1)} %collective-permute-done.refs_6_), channel_id=1, source_target_pairs={{0,6},{2,4},{4,2},{6,0},{8,14},{10,12},{12,10},{14,8},{1,7},{3,5},... | collective-permute-start | bytes 393224 | tf_op jit(solution)/shard_map/ppermute | solution.py:53

commit v4 on v3

--- a/solution.py
+++ b/solution.py
@@ -11,9 +11,10 @@
 VMEM_LIMIT = 40 * 1024 * 1024
 WHOLE = pl.BlockSpec(memory_space=pltpu.VMEM)
 IN_HBM = pl.BlockSpec(memory_space=pltpu.HBM)
-
-
-def source_kernel(mom_ref, disp_ref, bank_ref, out_ref, mom, disp, bank, arrived):
+IN_SMEM = pl.BlockSpec(memory_space=pltpu.SMEM)
+
+
+def source_kernel(mom_ref, disp_ref, bank_ref, out_ref, entry_ref, mom, disp, bank, arrived):
     copies = [
         pltpu.make_async_copy(mom_ref, mom, arrived.at[0]),
         pltpu.make_async_copy(disp_ref, disp, arrived.at[1]),
@@ -24,16 +25,20 @@
     for copy in copies:
         copy.wait()
     for a in range(out_ref.shape[1]):
-        out_ref[:, a] = bank[:, mom[a] * NDISP + disp[a]]
+        entry_ref[a] = mom[a] * NDISP + disp[a]
+        out_ref[:, a] = bank[:, entry_ref[a]]
 
 
 def chosen_source_rows(bank, op_mom, op_disp):
     nop = op_mom.shape[0]
     return pl.pallas_call(
         source_kernel,
-        out_shape=pltpu.VMEM((bank.shape[0], nop) + bank.shape[2:], bank.dtype),
+        out_shape=[
+            pltpu.VMEM((bank.shape[0], nop) + bank.shape[2:], bank.dtype),
+            pltpu.SMEM((nop,), jnp.int32),
+        ],
         in_specs=[IN_HBM] * 3,
-        out_specs=WHOLE,
+        out_specs=[WHOLE, IN_SMEM],
         scratch_shapes=[
             pltpu.SMEM((nop,), jnp.int32),
             pltpu.SMEM((nop,), jnp.int32),
@@ -53,61 +58,54 @@
     return lax.ppermute(array, "ta", [(k, k ^ mask) for k in range(count)])
 
 
-def sink_kernel(mom_ref, disp_ref, forward_ref, own_ref, other_ref, out_ref, mom, disp, forward, rows, arrived):
+def sink_kernel(entry_ref, forward_ref, own_ref, other_ref, out_ref, forward, rows, arrived):
     times, nop = rows.shape[:2]
-    numbers = [
-        pltpu.make_async_copy(mom_ref, mom, arrived.at[nop]),
-        pltpu.make_async_copy(disp_ref, disp, arrived.at[nop + 1]),
-    ]
-    whole = pltpu.make_async_copy(forward_ref, forward, arrived.at[nop + 2])
-    for copy in numbers + [whole]:
-        copy.start()
-    for copy in numbers:
-        copy.wait()
-    entries = [mom[a] * NDISP + disp[a] for a in range(nop)]
+    entries = [entry_ref[a] for a in range(nop)]
+    whole = pltpu.make_async_copy(forward_ref, forward, arrived.at[nop])
+    whole.start()
     copies = [
         pltpu.make_async_copy(own_ref.at[:, e], rows.at[:, a], arrived.at[a]) for a, e in enumerate(entries)
     ]
     for copy in copies:
         copy.start()
+    mine = lax.axis_index("sa")
+
+    def joined(matrices):
+        split = [jnp.swapaxes(x, 0, 1) for x in matrices]
+        return jnp.concatenate([jnp.concatenate([x[0], x[1]], axis=1) for x in split], axis=0)
+
+    def multiply(half, lefts, rights):
+        for t in range(times):
+            out_ref[t, half] = lax.dot_general(
+                lefts[t], rights[t], (((0,), (1,)), ((), ())), preferred_element_type=jnp.float32
+            ).astype(jnp.bfloat16)
+
+    rights = [joined([other_ref[t, e] for e in entries]) for t in range(times)]
     whole.wait()
     lefts = []
     for t in range(times):
         parts = jnp.swapaxes(forward[t, 0], 0, 1)
-        real, imag = parts[0].T, parts[1].T
-        for_real = jnp.concatenate([real, -imag], axis=1)
-        for_imag = jnp.concatenate([imag, real], axis=1)
-        lefts.append(jnp.concatenate([for_real, for_imag], axis=0))
-    mine = lax.axis_index("sa")
-
-    def multiply(half, pick):
-        for t in range(times):
-            chosen = [jnp.swapaxes(pick(t, a), 0, 1) for a in range(nop)]
-            right = jnp.concatenate([jnp.concatenate([x[0], x[1]], axis=1) for x in chosen], axis=0)
-            out_ref[t, half] = lax.dot_general(
-                lefts[t], right, (((1,), (1,)), ((), ())), preferred_element_type=jnp.float32
-            ).astype(jnp.bfloat16)
-
-    multiply(1 - mine, lambda t, a: other_ref[t, entries[a]])
+        for_real = jnp.concatenate([parts[0], -parts[1]], axis=0)
+        for_imag = jnp.concatenate([parts[1], parts[0]], axis=0)
+        lefts.append(jnp.concatenate([for_real, for_imag], axis=1))
+    multiply(1 - mine, lefts, rights)
     for copy in copies:
         copy.wait()
-    multiply(mine, lambda t, a: rows[t, a])
-
-
-def sink_products(forward, own_bank, other_bank, op_mom, op_disp):
-    nop = op_mom.shape[0]
+    multiply(mine, lefts, [joined([rows[t, a] for a in range(nop)]) for t in range(times)])
+
+
+def sink_products(forward, own_bank, other_bank, entries):
+    nop = entries.shape[0]
     times, order = forward.shape[0], forward.shape[2]
     return pl.pallas_call(
         sink_kernel,
         out_shape=jax.ShapeDtypeStruct((times, 2, 2 * order, nop * own_bank.shape[2]), jnp.bfloat16),
-        in_specs=[IN_HBM] * 4 + [WHOLE],
+        in_specs=[IN_SMEM, IN_HBM, IN_HBM, WHOLE],
         out_specs=WHOLE,
         scratch_shapes=[
-            pltpu.SMEM((nop,), jnp.int32),
-            pltpu.SMEM((nop,), jnp.int32),
             pltpu.VMEM(forward.shape, forward.dtype),
             pltpu.VMEM((times, nop) + own_bank.shape[2:], own_bank.dtype),
-            pltpu.SemaphoreType.DMA((nop + 3,)),
+            pltpu.SemaphoreType.DMA((nop + 1,)),
         ],
         compiler_params=pltpu.CompilerParams(vmem_limit_bytes=VMEM_LIMIT),
         cost_estimate=pl.CostEstimate(
@@ -117,7 +115,9 @@
         ),
         name="sink_product",
     )(
-        *(pltpu.with_memory_space_constraint(x, pltpu.HBM) for x in (op_mom, op_disp, forward, own_bank)),
+        pltpu.with_memory_space_constraint(entries, pltpu.SMEM),
+        pltpu.with_memory_space_constraint(forward, pltpu.HBM),
+        pltpu.with_memory_space_constraint(own_bank, pltpu.HBM),
         other_bank,
     )
 
@@ -162,32 +162,27 @@
         for t in range(times):
             out_ref[t] = totals[t]
         return
-    side = totals[0].shape[0]
-    shape = (2, nop, rows, 2 * nop * rows)
-    row_part = lax.broadcasted_iota(jnp.int32, shape, 0)
-    row_at = lax.broadcasted_iota(jnp.int32, shape, 2)
-    column_at = lax.broadcasted_iota(jnp.int32, shape, 3)
-    column_part = (column_at >= nop * rows).astype(jnp.int32)
-    same = row_at == lax.rem(column_at, rows)
-    sign = jnp.where(row_part == 0, 1.0, -1.0)
-    weights = (
-        jnp.where(same & (row_part == column_part), sign, 0.0),
-        jnp.where(same & (row_part != column_part), 1.0, 0.0),
+    width = nop * rows
+    same = lax.broadcasted_iota(jnp.int32, (rows, width), 0) == lax.rem(
+        lax.broadcasted_iota(jnp.int32, (rows, width), 1), rows
     )
     sums = []
     for t in range(times):
-        table = totals[t].reshape(shape)
-        for weight in weights:
-            sums.append((table * weight).sum(axis=(0, 2)))
-    left_over = jnp.concatenate(sums, axis=0)
+        kept = [
+            jnp.where(same, totals[t][:, d * width : (d + 1) * width].reshape(2, nop, rows, width), 0.0)
+            for d in range(2)
+        ]
+        sums.append(kept[0][0] - kept[1][1])
+        sums.append(kept[1][0] + kept[0][1])
+    left_over = jnp.concatenate(sums, axis=0).sum(axis=1)
     height = left_over.shape[0]
     terms = []
     for _ in range(3):
         terms.append(left_over.astype(jnp.bfloat16))
         left_over = left_over - terms[-1].astype(jnp.float32)
     of_operator = (
-        lax.rem(lax.broadcasted_iota(jnp.int32, (side, nop), 0) // rows, nop)
-        == lax.broadcasted_iota(jnp.int32, (side, nop), 1)
+        lax.broadcasted_iota(jnp.int32, (width, nop), 0) // rows
+        == lax.broadcasted_iota(jnp.int32, (width, nop), 1)
     ).astype(jnp.bfloat16)
     paired = jnp.dot(jnp.concatenate(terms, axis=0), of_operator, preferred_element_type=jnp.float32)
     paired = (paired[:height] + (paired[height : 2 * height] + paired[2 * height :])) / order
@@ -220,15 +215,14 @@
     times = forward.shape[0]
     own_rows = source_bank.shape[2]
 
-    source_raw = chosen_source_rows(source_bank, op_mom, op_disp)
+    source_raw, entries = chosen_source_rows(source_bank, op_mom, op_disp)
     source = jnp.transpose(source_raw[0], (2, 0, 1, 3)).reshape(-1, order)
     other_bank = lax.ppermute(sink_bank, "sa", [(0, 1), (1, 0)])
     product = sink_products(
         forward,
         sink_bank,
         other_bank,
-        op_mom,
-        op_disp,
+        entries,
     )
     back = planar(backward[0]).reshape(times, 2 * order, order)
 
@@ -237,12 +231,14 @@
     if own_rows == rows and n_times == 2 * far_mask and far_mask & (far_mask - 1) == 0:
         near = range(1, far_mask)
         far = swap(source, far_mask, n_times)
-        early = {0: source} | {m: swap(source, m, n_times) for m in near}
+        early = {0: source} | {m: swap(source, m, n_times) for m in reversed(near)}
         early[far_mask] = far
         far, product = lax.optimization_barrier((far, product))
         late = {far_mask ^ m: swap(far, m, n_times) for m in near}
         first = traces(product, back, early, nop, rows)
-        result = traces(product, back, late, nop, rows, before=first, last=True)
+        end = {far_mask ^ near[-1]: late.pop(far_mask ^ near[-1])}
+        first = traces(product, back, late, nop, rows, before=first)
+        result = traces(product, back, end, nop, rows, before=first, last=True)
     else:
         whole = lax.all_gather(source.reshape(2, nop, own_rows, order), "ta", axis=2, tiled=True)
         pieces = {

time: 24.2 us -> 23.4 us (0.967)
  waiting for transfers between devices: 4.69 us -> 3.84 us
    ppermute x7, waiting for transfers between devices: 4.69 us -> 3.84 us  [swap(): return lax.ppermute(array, 'ta', [(k, k ^ mask) for k in range(count)])]
    pallas_call x1, Pallas kernels: 3.41 us -> 2.97 us  [sink_products(): pl.pallas_call(sink_kernel, out_shape=jax.ShapeDtypeStruct((times, 2, 2 *...]
    pallas_call x2 -> x3, Pallas kernels: 3.71 us -> 4.1 us  [traces(): pl.pallas_call(functools.partial(trace_kernel, tuple(pieces), known, last...]
  transfers between devices with their start and end apart: 8 -> 8, of which waited for: 5 -> 4; matrix products, arithmetic and copies ran while one was open for 0% -> 0% of each run, Pallas kernels for 26% -> 29%
where the time goes in v4:
time: 23.4 us; the launch traced here: 23.2 us
  starting transfers between devices  11.1 us (47%)
  Pallas kernels  8.07 us (34%)
  waiting for transfers between devices  3.84 us (16%)
    ppermute x7, starting transfers between devices, swap(): return lax.ppermute(array, 'ta', [(k, k ^ mask) for k in range(count)])  10.7 us
    pallas_call x3, Pallas kernels, traces(): pl.pallas_call(functools.partial(trace_kernel, tuple(pieces), known, last...  4.1 us
    ppermute x7, waiting for transfers between devices, swap(): return lax.ppermute(array, 'ta', [(k, k ^ mask) for k in range(count)])  3.84 us
    pallas_call x1, Pallas kernels, sink_products(): pl.pallas_call(sink_kernel, out_shape=jax.ShapeDtypeStruct((times, 2, 2 *...  2.97 us
    pallas_call x1, Pallas kernels, chosen_source_rows(): pl.pallas_call(source_kernel, out_shape=[pltpu.VMEM((bank.shape[0], nop)...  1 us
  transfers between devices with their start and end apart: 8, of which 4 were waited for; matrix products, arithmetic and copies ran while one was open for 0% of the time, Pallas kernels for 29%

profile of v4, /device:TPU:0, one launch (start us, length us, event | category | flops | bytes accessed | tf_op | source)
XLA Modules:
  0.0 23.2 jit_solution(6002268776560014494)
XLA Ops:
  0.0 0.5 %collective-permute-start.1 = (bf16[2,9,128,2,256]{4,3,2,1,0:T(2,128)(2,1)}, bf16[2,9,128,2,256]{4,3,2,1,0:T(2,128)(2,1)S(1)}, u32[]{:S(2)}, u32[]{:S(2)}) collective-permute-start(bf16[2,9,128,2,256]{4,3,2,1,0:T(2,128)(2,1)} %own_ref.1), channel_id=1, source_target_pairs={{0,1},{1,0},{2,3},{3,2},{4,5},{5,4},{6,7},{7,6},{8,9},{9,8},{10,11... | collective-permute-start | bytes 7077896 | tf_op jit(solution)/shard_map/ppermute | solution.py:220
  0.5 1.0 %source_rows.1 = (bf16[1,4,32,2,256]{4,3,2,1,0:T(2,128)(2,1)S(1)}, s32[4]{0:T(128)S(4)}) custom-call(s32[4]{0:T(128)} %mom_ref.1, s32[4]{0:T(128)} %disp_ref.1, bf16[1,9,32,2,256]{4,3,2,1,0:T(2,128)(2,1)} %bank_ref.1), custom_call_target="tpu_custom_call" | custom-call | tf_op jit(solution)/shard_map/source_rows/pallas_call | solution.py:34
  1.5 3.7 %collective-permute-start = (bf16[256,256]{1,0:T(8,128)(2,1)S(1)}, bf16[256,256]{1,0:T(8,128)(2,1)S(1)}, u32[]{:S(2)}, u32[]{:S(2)}) collective-permute-start(bf16[256,256]{1,0:T(8,128)(2,1)S(1)} %bitcast.14), channel_id=1, source_target_pairs={{0,8},{2,10},{4,12},{6,14},{8,0},{10,2},{12,4},{14,6},{1,9},{3,11}... | collective-permute-start | bytes 393224 | tf_op jit(solution)/shard_map/ppermute | solution.py:58
  5.1 2.5 %collective-permute-start.5 = (bf16[256,256]{1,0:T(8,128)(2,1)S(1)}, bf16[256,256]{1,0:T(8,128)(2,1)S(1)}, u32[]{:S(2)}, u32[]{:S(2)}) collective-permute-start(bf16[256,256]{1,0:T(8,128)(2,1)S(1)} %bitcast.15), channel_id=1, source_target_pairs={{0,6},{2,4},{4,2},{6,0},{8,14},{10,12},{12,10},{14,8},{1,7},{3,5},... | collective-permute-start | bytes 393224 | tf_op jit(solution)/shard_map/ppermute | solution.py:58
  7.6 0.4 %collective-permute-start.6 = (bf16[256,256]{1,0:T(8,128)(2,1)S(1)}, bf16[256,256]{1,0:T(8,128)(2,1)S(1)}, u32[]{:S(2)}, u32[]{:S(2)}) collective-permute-start(bf16[256,256]{1,0:T(8,128)(2,1)S(1)} %bitcast.16), channel_id=1, source_target_pairs={{0,4},{2,6},{4,0},{6,2},{8,12},{10,14},{12,8},{14,10},{1,5},{3,7},... | collective-permute-start | bytes 393224 | tf_op jit(solution)/shard_map/ppermute | solution.py:58
  8.1 0.5 %collective-permute-start.7 = (bf16[256,256]{1,0:T(8,128)(2,1)S(1)}, bf16[256,256]{1,0:T(8,128)(2,1)S(1)}, u32[]{:S(2)}, u32[]{:S(2)}) collective-permute-start(bf16[256,256]{1,0:T(8,128)(2,1)S(1)} %bitcast.17), channel_id=1, source_target_pairs={{0,2},{2,0},{4,6},{6,4},{8,10},{10,8},{12,14},{14,12},{1,3},{3,1},... | collective-permute-start | bytes 393224 | tf_op jit(solution)/shard_map/ppermute | solution.py:58
  8.6 0.0 collective-permute-done.1.other_ref
  8.6 0.0 copy-start
  8.6 3.0 %sink_product.1.refs_0_ = bf16[2,2,512,512]{3,2,1,0:T(8,128)(2,1)S(1)} custom-call(s32[4]{0:T(128)S(4)} %get-tuple-element.10.entry_ref, bf16[2,1,256,2,256]{4,3,2,1,0:T(2,128)(2,1)} %forward_ref.1, bf16[2,9,128,2,256]{4,3,2,1,0:T(2,128)(2,1)} %own_ref.1, bf16[2,9,128,2,256]{4,3,2,1,0:T(2,128)(2,1)S(1)} %collective-permute-done.1.other_ref), custom_call_target="tpu_custom_call" | custom-call | flops 1073741824 | bytes 5242880 | tf_op jit(solution)/shard_map/sink_product/pallas_call | solution.py:100
  11.6 0.6 %collective-permute-done.refs_6_ = bf16[256,256]{1,0:T(8,128)(2,1)S(1)} collective-permute-done((bf16[256,256]{1,0:T(8,128)(2,1)S(1)}, bf16[256,256]{1,0:T(8,128)(2,1)S(1)}, u32[]{:S(2)}, u32[]{:S(2)}) %collective-permute-start) | collective-permute-done | bytes 131104 | tf_op jit(solution)/shard_map/ppermute | solution.py:58
  12.2 1.5 %collective-permute-start.3 = (bf16[256,256]{1,0:T(8,128)(2,1)S(1)}, bf16[256,256]{1,0:T(8,128)(2,1)S(1)}, u32[]{:S(2)}, u32[]{:S(2)}) collective-permute-start(bf16[256,256]{1,0:T(8,128)(2,1)S(1)} %collective-permute-done.refs_6_), channel_id=1, source_target_pairs={{0,2},{2,0},{4,6},{6,4},{8,10},{10,8},{12,14},{14,12},{1,3},{3,1},... | collective-permute-start | bytes 393224 | tf_op jit(solution)/shard_map/ppermute | solution.py:58
  13.8 1.0 %collective-permute-start.4 = (bf16[256,256]{1,0:T(8,128)(2,1)S(1)}, bf16[256,256]{1,0:T(8,128)(2,1)S(1)}, u32[]{:S(2)}, u32[]{:S(2)}) collective-permute-start(bf16[256,256]{1,0:T(8,128)(2,1)S(1)} %collective-permute-done.refs_6_), channel_id=1, source_target_pairs={{0,4},{2,6},{4,0},{6,2},{8,12},{10,14},{12,8},{14,10},{1,5},{3,7},... | collective-permute-start | bytes 393224 | tf_op jit(solution)/shard_map/ppermute | solution.py:58
  14.8 0.0 copy-done
  14.8 0.1 copy.8
  14.8 0.0 collective-permute-done.5.refs_3_
  14.8 1.0 %collective-permute-start.2 = (bf16[256,256]{1,0:T(8,128)(2,1)S(1)}, bf16[256,256]{1,0:T(8,128)(2,1)S(1)}, u32[]{:S(2)}, u32[]{:S(2)}) collective-permute-start(bf16[256,256]{1,0:T(8,128)(2,1)S(1)} %collective-permute-done.refs_6_), channel_id=1, source_target_pairs={{0,6},{2,4},{4,2},{6,0},{8,14},{10,12},{12,10},{14,8},{1,7},{3,5},... | collective-permute-start | bytes 393224 | tf_op jit(solution)/shard_map/ppermute | solution.py:58
  15.9 0.6 %collective-permute-done.6.refs_4_ = bf16[256,256]{1,0:T(8,128)(2,1)S(1)} collective-permute-done((bf16[256,256]{1,0:T(8,128)(2,1)S(1)}, bf16[256,256]{1,0:T(8,128)(2,1)S(1)}, u32[]{:S(2)}, u32[]{:S(2)}) %collective-permute-start.6) | collective-permute-done | bytes 131104 | tf_op jit(solution)/shard_map/ppermute | solution.py:58
  16.5 0.0 collective-permute-done.7.refs_5_
  16.5 1.8 %traces.2.refs_4_ = f32[2,256,256]{2,1,0:T(8,128)S(1)} custom-call(bf16[2,2,512,512]{3,2,1,0:T(8,128)(2,1)S(1)} %sink_product.1.refs_0_, bf16[2,512,256]{2,1,0:T(8,128)(2,1)S(1)} %bitcast.11, bf16[256,256]{1,0:T(8,128)(2,1)S(1)} %bitcast.18, bf16[256,256]{1,0:T(8,128)(2,1)S(1)} %collective-permute-done.5.refs_3_, ...), custom_call_target="tpu_custom_call" | custom-call | flops 1342177280 | bytes 4194304 | tf_op jit(solution)/shard_map/traces/pallas_call | solution.py:201
  18.2 0.0 collective-permute-done.3.refs_2_
  18.2 1.9 %collective-permute-done.4.refs_3_ = bf16[256,256]{1,0:T(8,128)(2,1)S(1)} collective-permute-done((bf16[256,256]{1,0:T(8,128)(2,1)S(1)}, bf16[256,256]{1,0:T(8,128)(2,1)S(1)}, u32[]{:S(2)}, u32[]{:S(2)}) %collective-permute-start.4) | collective-permute-done | bytes 131104 | tf_op jit(solution)/shard_map/ppermute | solution.py:58
  20.2 0.9 %traces.3.refs_3_ = f32[2,256,256]{2,1,0:T(8,128)S(1)} custom-call(bf16[2,2,512,512]{3,2,1,0:T(8,128)(2,1)S(1)} %sink_product.1.refs_0_, bf16[2,512,256]{2,1,0:T(8,128)(2,1)S(1)} %bitcast.12, bf16[256,256]{1,0:T(8,128)(2,1)S(1)} %collective-permute-done.3.refs_2_, bf16[256,256]{1,0:T(8,128)(2,1)S(1)} %collective-permute-done.4.refs_3_, ...), custom_call_target="tpu_custom_call" | custom-call | flops 536870912 | bytes 4194304 | tf_op jit(solution)/shard_map/traces/pallas_call | solution.py:201
  21.1 0.7 %collective-permute-done.2.refs_2_ = bf16[256,256]{1,0:T(8,128)(2,1)S(1)} collective-permute-done((bf16[256,256]{1,0:T(8,128)(2,1)S(1)}, bf16[256,256]{1,0:T(8,128)(2,1)S(1)}, u32[]{:S(2)}, u32[]{:S(2)}) %collective-permute-start.2) | collective-permute-done | bytes 131104 | tf_op jit(solution)/shard_map/ppermute | solution.py:58
  21.8 1.4 %traces_last.1 = f32[2,2,4,4]{3,2,1,0:T(4,128)} custom-call(bf16[2,2,512,512]{3,2,1,0:T(8,128)(2,1)S(1)} %sink_product.1.refs_0_, bf16[2,512,256]{2,1,0:T(8,128)(2,1)S(1)} %bitcast.13, bf16[256,256]{1,0:T(8,128)(2,1)S(1)} %collective-permute-done.2.refs_2_, f32[2,256,256]{2,1,0:T(8,128)S(1)} %traces.3.refs_3_), custom_call_target="tpu_custom_call" | custom-call | flops 268435456 | bytes 4194304 | tf_op jit(solution)/shard_map/traces_last/pallas_call | solution.py:201
  (1 shorter events, 0.0 us)
Async XLA Ops:
  0.0 8.6 %collective-permute-start.1 = (bf16[2,9,128,2,256]{4,3,2,1,0:T(2,128)(2,1)}, bf16[2,9,128,2,256]{4,3,2,1,0:T(2,128)(2,1)S(1)}, u32[]{:S(2)}, u32[]{:S(2)}) collective-permute-start(bf16[2,9,128,2,256]{4,3,2,1,0:T(2,128)(2,1)} %own_ref.1), channel_id=1, source_target_pairs={{0,1},{1,0},{2,3},{3,2},{4,5},{5,4},{6,7},{7,6},{8,9},{9,8},{10,11... | collective-permute-start | bytes 7077896 | tf_op jit(solution)/shard_map/ppermute | solution.py:220
  1.5 10.7 %collective-permute-start = (bf16[256,256]{1,0:T(8,128)(2,1)S(1)}, bf16[256,256]{1,0:T(8,128)(2,1)S(1)}, u32[]{:S(2)}, u32[]{:S(2)}) collective-permute-start(bf16[256,256]{1,0:T(8,128)(2,1)S(1)} %bitcast.14), channel_id=1, source_target_pairs={{0,8},{2,10},{4,12},{6,14},{8,0},{10,2},{12,4},{14,6},{1,9},{3,11}... | collective-permute-start | bytes 393224 | tf_op jit(solution)/shard_map/ppermute | solution.py:58
  5.1 9.7 %collective-permute-start.5 = (bf16[256,256]{1,0:T(8,128)(2,1)S(1)}, bf16[256,256]{1,0:T(8,128)(2,1)S(1)}, u32[]{:S(2)}, u32[]{:S(2)}) collective-permute-start(bf16[256,256]{1,0:T(8,128)(2,1)S(1)} %bitcast.15), channel_id=1, source_target_pairs={{0,6},{2,4},{4,2},{6,0},{8,14},{10,12},{12,10},{14,8},{1,7},{3,5},... | collective-permute-start | bytes 393224 | tf_op jit(solution)/shard_map/ppermute | solution.py:58
  7.6 8.8 %collective-permute-start.6 = (bf16[256,256]{1,0:T(8,128)(2,1)S(1)}, bf16[256,256]{1,0:T(8,128)(2,1)S(1)}, u32[]{:S(2)}, u32[]{:S(2)}) collective-permute-start(bf16[256,256]{1,0:T(8,128)(2,1)S(1)} %bitcast.16), channel_id=1, source_target_pairs={{0,4},{2,6},{4,0},{6,2},{8,12},{10,14},{12,8},{14,10},{1,5},{3,7},... | collective-permute-start | bytes 393224 | tf_op jit(solution)/shard_map/ppermute | solution.py:58
  8.1 8.4 %collective-permute-start.7 = (bf16[256,256]{1,0:T(8,128)(2,1)S(1)}, bf16[256,256]{1,0:T(8,128)(2,1)S(1)}, u32[]{:S(2)}, u32[]{:S(2)}) collective-permute-start(bf16[256,256]{1,0:T(8,128)(2,1)S(1)} %bitcast.17), channel_id=1, source_target_pairs={{0,2},{2,0},{4,6},{6,4},{8,10},{10,8},{12,14},{14,12},{1,3},{3,1},... | collective-permute-start | bytes 393224 | tf_op jit(solution)/shard_map/ppermute | solution.py:58
  8.6 6.1 %copy-start = (bf16[1,2,256,2,256]{4,3,2,1,0:T(2,128)(2,1)S(1)}, bf16[1,2,256,2,256]{4,3,2,1,0:T(2,128)(2,1)}, u32[]{:S(2)}) copy-start(bf16[1,2,256,2,256]{4,3,2,1,0:T(2,128)(2,1)} %param.7) | copy-start | bytes 1572868
  12.2 6.0 %collective-permute-start.3 = (bf16[256,256]{1,0:T(8,128)(2,1)S(1)}, bf16[256,256]{1,0:T(8,128)(2,1)S(1)}, u32[]{:S(2)}, u32[]{:S(2)}) collective-permute-start(bf16[256,256]{1,0:T(8,128)(2,1)S(1)} %collective-permute-done.refs_6_), channel_id=1, source_target_pairs={{0,2},{2,0},{4,6},{6,4},{8,10},{10,8},{12,14},{14,12},{1,3},{3,1},... | collective-permute-start | bytes 393224 | tf_op jit(solution)/shard_map/ppermute | solution.py:58
  13.8 6.4 %collective-permute-start.4 = (bf16[256,256]{1,0:T(8,128)(2,1)S(1)}, bf16[256,256]{1,0:T(8,128)(2,1)S(1)}, u32[]{:S(2)}, u32[]{:S(2)}) collective-permute-start(bf16[256,256]{1,0:T(8,128)(2,1)S(1)} %collective-permute-done.refs_6_), channel_id=1, source_target_pairs={{0,4},{2,6},{4,0},{6,2},{8,12},{10,14},{12,8},{14,10},{1,5},{3,7},... | collective-permute-start | bytes 393224 | tf_op jit(solution)/shard_map/ppermute | solution.py:58
  14.8 6.9 %collective-permute-start.2 = (bf16[256,256]{1,0:T(8,128)(2,1)S(1)}, bf16[256,256]{1,0:T(8,128)(2,1)S(1)}, u32[]{:S(2)}, u32[]{:S(2)}) collective-permute-start(bf16[256,256]{1,0:T(8,128)(2,1)S(1)} %collective-permute-done.refs_6_), channel_id=1, source_target_pairs={{0,6},{2,4},{4,2},{6,0},{8,14},{10,12},{12,10},{14,8},{1,7},{3,5},... | collective-permute-start | bytes 393224 | tf_op jit(solution)/shard_map/ppermute | solution.py:58

commit v5 on v4

--- a/solution.py
+++ b/solution.py
@@ -24,9 +24,10 @@
         copy.start()
     for copy in copies:
         copy.wait()
-    for a in range(out_ref.shape[1]):
-        entry_ref[a] = mom[a] * NDISP + disp[a]
-        out_ref[:, a] = bank[:, entry_ref[a]]
+    for a in range(out_ref.shape[0]):
+        entry = mom[a] * NDISP + disp[a]
+        entry_ref[a] = entry
+        out_ref[a] = jnp.swapaxes(bank[0, entry], 0, 1)
 
 
 def chosen_source_rows(bank, op_mom, op_disp):
@@ -34,7 +35,7 @@
     return pl.pallas_call(
         source_kernel,
         out_shape=[
-            pltpu.VMEM((bank.shape[0], nop) + bank.shape[2:], bank.dtype),
+            pltpu.VMEM((nop, bank.shape[3], bank.shape[2], bank.shape[4]), bank.dtype),
             pltpu.SMEM((nop,), jnp.int32),
         ],
         in_specs=[IN_HBM] * 3,
@@ -54,8 +55,10 @@
     return jnp.swapaxes(matrices, 1, 2)
 
 
-def swap(array, mask, count):
-    return lax.ppermute(array, "ta", [(k, k ^ mask) for k in range(count)])
+def swap(array, masks, count):
+    cores = len(masks)
+    pairs = [(k * cores + c, (k ^ m) * cores + c) for k in range(count) for c, m in enumerate(masks)]
+    return lax.ppermute(array, ("ta", "sa"), pairs)
 
 
 def sink_kernel(entry_ref, forward_ref, own_ref, other_ref, out_ref, forward, rows, arrived):
@@ -122,59 +125,131 @@
     )
 
 
-def trace_kernel(masks, known, last, nop, rows, *refs):
+def own_mask(masks, core):
+    mask = masks[0]
+    for c, m in enumerate(masks[1:], 1):
+        mask = jnp.where(core == c, m, mask) if m != masks[0] else mask
+    return mask
+
+
+def sink_block(product_ref, t, start, nop, rows):
+    order = product_ref.shape[2] // 2
+    width = product_ref.shape[3] // nop
+    parts = []
+    for part in range(2):
+        two = [product_ref[t, half, pl.ds(part * order + start, rows), :] for half in range(2)]
+        parts.append(
+            jnp.concatenate(
+                [
+                    jnp.concatenate([x[:, a * width : (a + 1) * width] for x in two], axis=1)
+                    for a in range(nop)
+                ],
+                axis=0,
+            )
+        )
+    return parts
+
+
+def block_start(masks, rows, known):
+    if known:
+        return masks[0] * rows
+    return pl.multiple_of((lax.axis_index("ta") ^ own_mask(masks, lax.axis_index("sa"))) * rows, rows)
+
+
+def diagonal_sums(tables, nop, rows):
+    width = nop * rows
+    same = lax.broadcasted_iota(jnp.int32, (rows, width), 0) == lax.rem(
+        lax.broadcasted_iota(jnp.int32, (rows, width), 1), rows
+    )
+    return jnp.concatenate(
+        [jnp.where(same, x.reshape(nop, rows, width), 0.0) for x in tables], axis=0
+    ).sum(axis=1)
+
+
+def trace_kernel(masks, known, sums, nop, rows, *refs):
     product_ref, back_ref = refs[:2]
-    me = 0 if known else lax.axis_index("ta")
     piece_refs = refs[2 : 2 + len(masks)]
     before_ref = refs[2 + len(masks)] if len(refs) == 4 + len(masks) else None
     out_ref = refs[-1]
     times = product_ref.shape[0]
     order = back_ref.shape[2]
     totals = [None if before_ref is None else before_ref[t] for t in range(times)]
+    nt = (((1,), (1,)), ((), ()))
     for mask, piece_ref in zip(masks, piece_refs):
-        height = piece_ref.shape[0] // 2
-        real, imag = piece_ref[:height], piece_ref[height:]
+        real, imag = (piece_ref[:, part].reshape(nop * rows, order) for part in range(2))
         for_real = jnp.concatenate([real, -imag], axis=1)
         for_imag = jnp.concatenate([imag, real], axis=1)
         left = jnp.concatenate([for_real, for_imag], axis=0)
-        start = pl.multiple_of((me ^ mask) * rows, rows)
+        start = block_start(mask, rows, known)
         for t in range(times):
             reverse = jnp.dot(left, back_ref[t], preferred_element_type=jnp.float32)
             high = reverse.astype(jnp.bfloat16)
             low = (reverse - high.astype(jnp.float32)).astype(jnp.bfloat16)
-            blocks = []
-            for part in range(2):
-                two = [
-                    product_ref[t, half, pl.ds(part * order + start, rows), :]
-                    for half in range(2)
-                ]
-                width = two[0].shape[1] // nop
-                for a in range(nop):
-                    blocks.append(
-                        jnp.concatenate([x[:, a * width : (a + 1) * width] for x in two], axis=1)
-                    )
-            sink = jnp.concatenate(blocks, axis=0)
-            nt = (((1,), (1,)), ((), ()))
+            sink = jnp.concatenate(sink_block(product_ref, t, start, nop, rows), axis=0)
             added = lax.dot_general(sink, high, nt, preferred_element_type=jnp.float32)
             added += lax.dot_general(sink, low, nt, preferred_element_type=jnp.float32)
             totals[t] = added if totals[t] is None else totals[t] + added
-    if not last:
+    if not sums:
         for t in range(times):
             out_ref[t] = totals[t]
         return
     width = nop * rows
-    same = lax.broadcasted_iota(jnp.int32, (rows, width), 0) == lax.rem(
-        lax.broadcasted_iota(jnp.int32, (rows, width), 1), rows
-    )
-    sums = []
-    for t in range(times):
-        kept = [
-            jnp.where(same, totals[t][:, d * width : (d + 1) * width].reshape(2, nop, rows, width), 0.0)
-            for d in range(2)
+    tables = []
+    for total in totals:
+        (rr, ri), (ir, ii) = (
+            [total[c * width : (c + 1) * width, d * width : (d + 1) * width] for d in range(2)] for c in range(2)
+        )
+        tables += [rr - ii, ri + ir]
+    out_ref[...] = diagonal_sums(tables, nop, rows)
+
+
+def traces(product, back, pieces, nop, rows, known=False, before=None, sums=False):
+    times, order = product.shape[0], back.shape[2]
+    side = 2 * nop * rows
+    operands = [product, back, *pieces.values()] + ([] if before is None else [before])
+    shape = (times * 2 * nop, nop * rows) if sums else (times, side, side)
+    flops = 2 * times * len(pieces) * side * (2 * order * order + 2 * side * order)
+    return pl.pallas_call(
+        functools.partial(trace_kernel, tuple(pieces), known, sums, nop, rows),
+        out_shape=jax.ShapeDtypeStruct(shape, jnp.float32),
+        in_specs=[WHOLE] * len(operands),
+        out_specs=WHOLE,
+        compiler_params=pltpu.CompilerParams(vmem_limit_bytes=VMEM_LIMIT),
+        cost_estimate=pl.CostEstimate(flops=flops, bytes_accessed=4 * 1024 * 1024, transcendentals=0),
+        name="trace_sums" if sums else "traces",
+    )(*operands)
+
+
+def loop_kernel(masks, nop, rows, product_ref, back_ref, after_ref, out_ref):
+    order = back_ref.shape[2]
+    start = block_start(masks, rows, False)
+    for t in range(product_ref.shape[0]):
+        back = jnp.concatenate([back_ref[t, :order], back_ref[t, order:]], axis=1)
+        real, imag = sink_block(product_ref, t, start, nop, rows)
+        value = [
+            lax.dot_general(x, back, (((1,), (1,)), ((), ())), preferred_element_type=jnp.float32)
+            for x in (jnp.concatenate([real, -imag], axis=1), jnp.concatenate([imag, real], axis=1))
         ]
-        sums.append(kept[0][0] - kept[1][1])
-        sums.append(kept[1][0] + kept[0][1])
-    left_over = jnp.concatenate(sums, axis=0).sum(axis=1)
+        for term in range(2):
+            now = [x.astype(jnp.bfloat16) for x in value]
+            value = [x - y.astype(jnp.float32) for x, y in zip(value, now)]
+            out_ref[t, term, 0] = jnp.concatenate([now[0], -now[1]], axis=1)
+            out_ref[t, term, 1] = jnp.concatenate([now[1], now[0]], axis=1)
+
+
+def last_kernel(nop, rows, order, *refs):
+    left_over = refs[0][...]
+    out_ref = refs[-1]
+    times = out_ref.shape[0]
+    width = nop * rows
+    if len(refs) > 2:
+        piece_ref, loop_ref = refs[1:3]
+        piece = jnp.concatenate([piece_ref[:, part].reshape(width, order) for part in range(2)], axis=1)
+        met = loop_ref[...].reshape(-1, 2 * order)
+        found = lax.dot_general(met, piece, (((1,), (1,)), ((), ())), preferred_element_type=jnp.float32)
+        found = found.reshape(times, 2, 2, width, width)
+        tables = [found[t, 0, part] + found[t, 1, part] for t in range(times) for part in range(2)]
+        left_over = left_over + diagonal_sums(tables, nop, rows)
     height = left_over.shape[0]
     terms = []
     for _ in range(3):
@@ -192,21 +267,27 @@
             out_ref[t, part] = paired[at : at + nop]
 
 
-def traces(product, back, pieces, nop, rows, known=False, before=None, last=False):
+def finish(sums, nop, rows, order, *more):
+    return pl.pallas_call(
+        functools.partial(last_kernel, nop, rows, order),
+        out_shape=jax.ShapeDtypeStruct((sums.shape[0] // (2 * nop), 2, nop, nop), jnp.float32),
+        in_specs=[WHOLE] * (1 + len(more)),
+        out_specs=WHOLE,
+        compiler_params=pltpu.CompilerParams(vmem_limit_bytes=VMEM_LIMIT),
+        name="traces_last",
+    )(sums, *more)
+
+
+def loops(product, back, after, masks, nop, rows):
     times, order = product.shape[0], back.shape[2]
-    side = 2 * nop * rows
-    operands = [product, back, *pieces.values()] + ([] if before is None else [before])
-    shape = (times, 2, nop, nop) if last else (times, side, side)
-    flops = 2 * times * len(pieces) * side * (2 * order * order + 2 * side * order)
-    return pl.pallas_call(
-        functools.partial(trace_kernel, tuple(pieces), known, last, nop, rows),
-        out_shape=jax.ShapeDtypeStruct(shape, jnp.float32),
-        in_specs=[WHOLE] * len(operands),
+    return pl.pallas_call(
+        functools.partial(loop_kernel, masks, nop, rows),
+        out_shape=jax.ShapeDtypeStruct((times, 2, 2, nop * rows, 2 * order), jnp.bfloat16),
+        in_specs=[WHOLE, WHOLE, pl.BlockSpec(memory_space=pl.ANY)],
         out_specs=WHOLE,
         compiler_params=pltpu.CompilerParams(vmem_limit_bytes=VMEM_LIMIT),
-        cost_estimate=pl.CostEstimate(flops=flops, bytes_accessed=4 * 1024 * 1024, transcendentals=0),
-        name="traces_last" if last else "traces",
-    )(*operands)
+        name="loops",
+    )(product, back, after)
 
 
 def per_device(forward, backward, sink_bank, source_bank, op_mom, op_disp, n_times):
@@ -215,8 +296,7 @@
     times = forward.shape[0]
     own_rows = source_bank.shape[2]
 
-    source_raw, entries = chosen_source_rows(source_bank, op_mom, op_disp)
-    source = jnp.transpose(source_raw[0], (2, 0, 1, 3)).reshape(-1, order)
+    source, entries = chosen_source_rows(source_bank, op_mom, op_disp)
     other_bank = lax.ppermute(sink_bank, "sa", [(0, 1), (1, 0)])
     product = sink_products(
         forward,
@@ -229,22 +309,24 @@
     rows = order // (2 * nop)
     far_mask = n_times // 2
     if own_rows == rows and n_times == 2 * far_mask and far_mask & (far_mask - 1) == 0:
-        near = range(1, far_mask)
-        far = swap(source, far_mask, n_times)
-        early = {0: source} | {m: swap(source, m, n_times) for m in reversed(near)}
-        early[far_mask] = far
+        near = tuple(range(1, far_mask))
+        orders = (near[::-1], (near[1:-1] + near[:1] + near[-1:]))
+        far = swap(source, (far_mask, far_mask), n_times)
+        early = {(0, 0): source} | {m: swap(source, m, n_times) for m in zip(*orders)}
+        early[far_mask, far_mask] = far
         far, product = lax.optimization_barrier((far, product))
-        late = {far_mask ^ m: swap(far, m, n_times) for m in near}
+        late = {(far_mask ^ m[0], far_mask ^ m[1]): swap(far, m, n_times) for m in zip(near, near)}
         first = traces(product, back, early, nop, rows)
-        end = {far_mask ^ near[-1]: late.pop(far_mask ^ near[-1])}
-        first = traces(product, back, late, nop, rows, before=first)
-        result = traces(product, back, end, nop, rows, before=first, last=True)
+        last_masks = list(late)[-1]
+        end = late.pop(last_masks)
+        loop = loops(product, back, first, last_masks, nop, rows)
+        sums = traces(product, back, late, nop, rows, before=first, sums=True)
+        result = finish(sums, nop, rows, order, end, loop)
     else:
-        whole = lax.all_gather(source.reshape(2, nop, own_rows, order), "ta", axis=2, tiled=True)
-        pieces = {
-            k: whole[:, :, k * rows : (k + 1) * rows].reshape(-1, order) for k in range(order // rows)
-        }
-        result = traces(product, back, pieces, nop, rows, known=True, last=True)
+        whole = lax.all_gather(source, "ta", axis=2, tiled=True)
+        pieces = {(k,): whole[:, :, k * rows : (k + 1) * rows] for k in range(order // rows)}
+        sums = traces(product, back, pieces, nop, rows, known=True, sums=True)
+        result = finish(sums, nop, rows, order)
     return result[:, None]
 
 

time: 23.4 us -> 23.2 us (level)
  waiting for transfers between devices: 3.84 us -> 3.36 us
  Pallas kernels: 8.07 us -> 8.39 us
    ppermute x7, waiting for transfers between devices: 3.84 us -> 3.36 us  [swap(): return lax.ppermute(array, ('ta', 'sa'), pairs)]
    pallas_call x4 -> x5, Pallas kernels: 5.1 us -> 5.42 us  [the longest x2 2.71 us: traces(): pl.pallas_call(functools.partial(trace_kernel, tuple(pieces), known, sums...]
  transfers between devices with their start and end apart: 8 -> 8, of which waited for: 4 -> 4; matrix products, arithmetic and copies ran while one was open for 0% -> 0% of each run, Pallas kernels for 29% -> 31%
where the time goes in v5:
time: 23.2 us; the launch traced here: 23 us
  starting transfers between devices  11.1 us (48%)
  Pallas kernels  8.39 us (36%)
  waiting for transfers between devices  3.36 us (14%)
    ppermute x7, starting transfers between devices, swap(): return lax.ppermute(array, ('ta', 'sa'), pairs)  10.7 us
    ppermute x7, waiting for transfers between devices, swap(): return lax.ppermute(array, ('ta', 'sa'), pairs)  3.36 us
    pallas_call x1, Pallas kernels, sink_products(): pl.pallas_call(sink_kernel, out_shape=jax.ShapeDtypeStruct((times, 2, 2 *...  2.97 us
    pallas_call x2, Pallas kernels, traces(): pl.pallas_call(functools.partial(trace_kernel, tuple(pieces), known, sums...  2.71 us
    pallas_call x1, Pallas kernels, finish(): pl.pallas_call(functools.partial(last_kernel, nop, rows, order), out_shap...  1.18 us
    pallas_call x1, Pallas kernels, chosen_source_rows(): pl.pallas_call(source_kernel, out_shape=[pltpu.VMEM((nop, bank.shape[3],...  1.05 us
    pallas_call x1, Pallas kernels, loops(): pl.pallas_call(functools.partial(loop_kernel, masks, nop, rows), out_shap...  0.48 us
  transfers between devices with their start and end apart: 8, of which 4 were waited for; matrix products, arithmetic and copies ran while one was open for 0% of the time, Pallas kernels for 31%

profile of v5, /device:TPU:0, one launch (start us, length us, event | category | flops | bytes accessed | tf_op | source)
XLA Modules:
  0.0 23.0 jit_solution(16886226148702698524)
XLA Ops:
  0.0 0.5 %collective-permute-start.1 = (bf16[2,9,128,2,256]{4,3,2,1,0:T(2,128)(2,1)}, bf16[2,9,128,2,256]{4,3,2,1,0:T(2,128)(2,1)S(1)}, u32[]{:S(2)}, u32[]{:S(2)}) collective-permute-start(bf16[2,9,128,2,256]{4,3,2,1,0:T(2,128)(2,1)} %own_ref.1), channel_id=1, source_target_pairs={{0,1},{1,0},{2,3},{3,2},{4,5},{5,4},{6,7},{7,6},{8,9},{9,8},{10,11... | collective-permute-start | bytes 7077896 | tf_op jit(solution)/shard_map/ppermute | solution.py:300
  0.5 1.1 %source_rows.1 = (bf16[4,2,32,256]{3,2,1,0:T(8,128)(2,1)S(1)}, s32[4]{0:T(128)S(4)}) custom-call(s32[4]{0:T(128)} %mom_ref.1, s32[4]{0:T(128)} %disp_ref.1, bf16[1,9,32,2,256]{4,3,2,1,0:T(2,128)(2,1)} %bank_ref.1), custom_call_target="tpu_custom_call" | custom-call | tf_op jit(solution)/shard_map/source_rows/pallas_call | solution.py:35
  1.5 3.7 %collective-permute-start = (bf16[4,2,32,256]{3,2,1,0:T(8,128)(2,1)S(1)}, bf16[4,2,32,256]{3,2,1,0:T(8,128)(2,1)S(1)}, u32[]{:S(2)}, u32[]{:S(2)}) collective-permute-start(bf16[4,2,32,256]{3,2,1,0:T(8,128)(2,1)S(1)} %get-tuple-element.9.refs_2_), channel_id=1, source_target_pairs={{0,8},{1,9},{2,10},{3,11},{4,12},{5,13},{6,14},{7,15},{8,0},{9,1},... | collective-permute-start | bytes 393224 | tf_op jit(solution)/shard_map/ppermute | solution.py:61
  5.2 2.5 %collective-permute-start.4 = (bf16[4,2,32,256]{3,2,1,0:T(8,128)(2,1)S(1)}, bf16[4,2,32,256]{3,2,1,0:T(8,128)(2,1)S(1)}, u32[]{:S(2)}, u32[]{:S(2)}) collective-permute-start(bf16[4,2,32,256]{3,2,1,0:T(8,128)(2,1)S(1)} %get-tuple-element.9.refs_2_), channel_id=1, source_target_pairs={{0,6},{1,5},{2,4},{3,7},{4,2},{5,1},{6,0},{7,3},{8,14},{9,13},{10,... | collective-permute-start | bytes 393224 | tf_op jit(solution)/shard_map/ppermute | solution.py:61
  7.7 0.4 %collective-permute-start.5 = (bf16[4,2,32,256]{3,2,1,0:T(8,128)(2,1)S(1)}, bf16[4,2,32,256]{3,2,1,0:T(8,128)(2,1)S(1)}, u32[]{:S(2)}, u32[]{:S(2)}) collective-permute-start(bf16[4,2,32,256]{3,2,1,0:T(8,128)(2,1)S(1)} %get-tuple-element.9.refs_2_), channel_id=1, source_target_pairs={{0,4},{1,3},{2,6},{3,1},{4,0},{5,7},{6,2},{7,5},{8,12},{9,11},{10,... | collective-permute-start | bytes 393224 | tf_op jit(solution)/shard_map/ppermute | solution.py:61
  8.1 0.5 %collective-permute-start.6 = (bf16[4,2,32,256]{3,2,1,0:T(8,128)(2,1)S(1)}, bf16[4,2,32,256]{3,2,1,0:T(8,128)(2,1)S(1)}, u32[]{:S(2)}, u32[]{:S(2)}) collective-permute-start(bf16[4,2,32,256]{3,2,1,0:T(8,128)(2,1)S(1)} %get-tuple-element.9.refs_2_), channel_id=1, source_target_pairs={{0,2},{1,7},{2,0},{3,5},{4,6},{5,3},{6,4},{7,1},{8,10},{9,15},{10,... | collective-permute-start | bytes 393224 | tf_op jit(solution)/shard_map/ppermute | solution.py:61
  8.7 0.0 collective-permute-done.1.other_ref
  8.7 3.0 %sink_product.1.refs_0_.product_ref = bf16[2,2,512,512]{3,2,1,0:T(8,128)(2,1)S(1)} custom-call(s32[4]{0:T(128)S(4)} %get-tuple-element.10.entry_ref, bf16[2,1,256,2,256]{4,3,2,1,0:T(2,128)(2,1)} %forward_ref.1, bf16[2,9,128,2,256]{4,3,2,1,0:T(2,128)(2,1)} %own_ref.1, bf16[2,9,128,2,256]{4,3,2,1,0:T(2,128)(2,1)S(1)} %collective-permute-done.1.other_ref), custom_call_target="tpu_custom_call" | custom-call | flops 1073741824 | bytes 5242880 | tf_op jit(solution)/shard_map/sink_product/pallas_call | solution.py:103
  11.6 0.6 %collective-permute-done.refs_6_ = bf16[4,2,32,256]{3,2,1,0:T(8,128)(2,1)S(1)} collective-permute-done((bf16[4,2,32,256]{3,2,1,0:T(8,128)(2,1)S(1)}, bf16[4,2,32,256]{3,2,1,0:T(8,128)(2,1)S(1)}, u32[]{:S(2)}, u32[]{:S(2)}) %collective-permute-start) | collective-permute-done | bytes 131104 | tf_op jit(solution)/shard_map/ppermute | solution.py:61
  12.2 1.5 %collective-permute-start.2 = (bf16[4,2,32,256]{3,2,1,0:T(8,128)(2,1)S(1)}, bf16[4,2,32,256]{3,2,1,0:T(8,128)(2,1)S(1)}, u32[]{:S(2)}, u32[]{:S(2)}) collective-permute-start(bf16[4,2,32,256]{3,2,1,0:T(8,128)(2,1)S(1)} %collective-permute-done.refs_6_), channel_id=1, source_target_pairs={{0,2},{1,3},{2,0},{3,1},{4,6},{5,7},{6,4},{7,5},{8,10},{9,11},{10,... | collective-permute-start | bytes 393224 | tf_op jit(solution)/shard_map/ppermute | solution.py:61
  13.8 1.0 %collective-permute-start.3 = (bf16[4,2,32,256]{3,2,1,0:T(8,128)(2,1)S(1)}, bf16[4,2,32,256]{3,2,1,0:T(8,128)(2,1)S(1)}, u32[]{:S(2)}, u32[]{:S(2)}) collective-permute-start(bf16[4,2,32,256]{3,2,1,0:T(8,128)(2,1)S(1)} %collective-permute-done.refs_6_), channel_id=1, source_target_pairs={{0,4},{1,5},{2,6},{3,7},{4,0},{5,1},{6,2},{7,3},{8,12},{9,13},{10,... | collective-permute-start | bytes 393224 | tf_op jit(solution)/shard_map/ppermute | solution.py:61
  14.8 0.0 copy-done
  14.8 0.1 copy.7
  14.9 0.0 collective-permute-done.4.refs_3_
  14.9 1.0 %collective-permute-start.7 = (bf16[4,2,32,256]{3,2,1,0:T(8,128)(2,1)S(1)}, bf16[4,2,32,256]{3,2,1,0:T(8,128)(2,1)S(1)}, u32[]{:S(2)}, u32[]{:S(2)}) collective-permute-start(bf16[4,2,32,256]{3,2,1,0:T(8,128)(2,1)S(1)} %collective-permute-done.refs_6_), channel_id=1, source_target_pairs={{0,6},{1,7},{2,4},{3,5},{4,2},{5,3},{6,0},{7,1},{8,14},{9,15},{10,... | collective-permute-start | bytes 393224 | tf_op jit(solution)/shard_map/ppermute | solution.py:61
  15.9 0.0 collective-permute-done.5.refs_4_
  15.9 0.0 collective-permute-done.6.refs_5_
  15.9 1.8 %traces.1.refs_4_.after_ref = f32[2,256,256]{2,1,0:T(8,128)S(1)} custom-call(bf16[2,2,512,512]{3,2,1,0:T(8,128)(2,1)S(1)} %sink_product.1.refs_0_.product_ref, bf16[2,512,256]{2,1,0:T(8,128)(2,1)S(1)} %bitcast.7, bf16[4,2,32,256]{3,2,1,0:T(8,128)(2,1)S(1)} %get-tuple-element.9.refs_2_, bf16[4,2,32,256]{3,2,1,0:T(8,128)(2,1)S(1)} %collective-permute-done.4.refs_3_, ...), custom_call_target="tpu_custom_call" | custom-call | flops 1342177280 | bytes 4194304 | tf_op jit(solution)/shard_map/traces/pallas_call | solution.py:212
  17.7 0.5 %loops.1.refs_2_ = bf16[2,2,2,128,512]{4,3,2,1,0:T(8,128)(2,1)S(1)} custom-call(bf16[2,2,512,512]{3,2,1,0:T(8,128)(2,1)S(1)} %sink_product.1.refs_0_.product_ref, bf16[2,512,256]{2,1,0:T(8,128)(2,1)S(1)} %bitcast.8, f32[2,256,256]{2,1,0:T(8,128)S(1)} %traces.1.refs_4_.after_ref), custom_call_target="tpu_custom_call" | custom-call | tf_op jit(solution)/shard_map/loops/pallas_call | solution.py:283
  18.1 0.1 collective-permute-done.2.refs_2_
  18.2 1.8 %collective-permute-done.3.refs_3_ = bf16[4,2,32,256]{3,2,1,0:T(8,128)(2,1)S(1)} collective-permute-done((bf16[4,2,32,256]{3,2,1,0:T(8,128)(2,1)S(1)}, bf16[4,2,32,256]{3,2,1,0:T(8,128)(2,1)S(1)}, u32[]{:S(2)}, u32[]{:S(2)}) %collective-permute-start.3) | collective-permute-done | bytes 131104 | tf_op jit(solution)/shard_map/ppermute | solution.py:61
  20.0 1.0 %trace_sums.1.refs_0_ = f32[16,128]{1,0:T(8,128)S(1)} custom-call(bf16[2,2,512,512]{3,2,1,0:T(8,128)(2,1)S(1)} %sink_product.1.refs_0_.product_ref, bf16[2,512,256]{2,1,0:T(8,128)(2,1)S(1)} %bitcast.9, bf16[4,2,32,256]{3,2,1,0:T(8,128)(2,1)S(1)} %collective-permute-done.2.refs_2_, bf16[4,2,32,256]{3,2,1,0:T(8,128)(2,1)S(1)} %collective-permute-done.3.refs_3_, ...), custom_call_target="tpu_custom_call" | custom-call | flops 536870912 | bytes 4194304 | tf_op jit(solution)/shard_map/trace_sums/pallas_call | solution.py:212
  20.9 0.9 %collective-permute-done.7.refs_1_ = bf16[4,2,32,256]{3,2,1,0:T(8,128)(2,1)S(1)} collective-permute-done((bf16[4,2,32,256]{3,2,1,0:T(8,128)(2,1)S(1)}, bf16[4,2,32,256]{3,2,1,0:T(8,128)(2,1)S(1)}, u32[]{:S(2)}, u32[]{:S(2)}) %collective-permute-start.7) | collective-permute-done | bytes 131104 | tf_op jit(solution)/shard_map/ppermute | solution.py:61
  21.8 1.2 %traces_last.1 = f32[2,2,4,4]{3,2,1,0:T(4,128)} custom-call(f32[16,128]{1,0:T(8,128)S(1)} %trace_sums.1.refs_0_, bf16[4,2,32,256]{3,2,1,0:T(8,128)(2,1)S(1)} %collective-permute-done.7.refs_1_, bf16[2,2,2,128,512]{4,3,2,1,0:T(8,128)(2,1)S(1)} %loops.1.refs_2_), custom_call_target="tpu_custom_call" | custom-call | tf_op jit(solution)/shard_map/traces_last/pallas_call | solution.py:271
  (1 shorter events, 0.0 us)
Async XLA Ops:
  0.0 8.7 %collective-permute-start.1 = (bf16[2,9,128,2,256]{4,3,2,1,0:T(2,128)(2,1)}, bf16[2,9,128,2,256]{4,3,2,1,0:T(2,128)(2,1)S(1)}, u32[]{:S(2)}, u32[]{:S(2)}) collective-permute-start(bf16[2,9,128,2,256]{4,3,2,1,0:T(2,128)(2,1)} %own_ref.1), channel_id=1, source_target_pairs={{0,1},{1,0},{2,3},{3,2},{4,5},{5,4},{6,7},{7,6},{8,9},{9,8},{10,11... | collective-permute-start | bytes 7077896 | tf_op jit(solution)/shard_map/ppermute | solution.py:300
  1.5 10.7 %collective-permute-start = (bf16[4,2,32,256]{3,2,1,0:T(8,128)(2,1)S(1)}, bf16[4,2,32,256]{3,2,1,0:T(8,128)(2,1)S(1)}, u32[]{:S(2)}, u32[]{:S(2)}) collective-permute-start(bf16[4,2,32,256]{3,2,1,0:T(8,128)(2,1)S(1)} %get-tuple-element.9.refs_2_), channel_id=1, source_target_pairs={{0,8},{1,9},{2,10},{3,11},{4,12},{5,13},{6,14},{7,15},{8,0},{9,1},... | collective-permute-start | bytes 393224 | tf_op jit(solution)/shard_map/ppermute | solution.py:61
  5.2 9.7 %collective-permute-start.4 = (bf16[4,2,32,256]{3,2,1,0:T(8,128)(2,1)S(1)}, bf16[4,2,32,256]{3,2,1,0:T(8,128)(2,1)S(1)}, u32[]{:S(2)}, u32[]{:S(2)}) collective-permute-start(bf16[4,2,32,256]{3,2,1,0:T(8,128)(2,1)S(1)} %get-tuple-element.9.refs_2_), channel_id=1, source_target_pairs={{0,6},{1,5},{2,4},{3,7},{4,2},{5,1},{6,0},{7,3},{8,14},{9,13},{10,... | collective-permute-start | bytes 393224 | tf_op jit(solution)/shard_map/ppermute | solution.py:61
  7.7 8.2 %collective-permute-start.5 = (bf16[4,2,32,256]{3,2,1,0:T(8,128)(2,1)S(1)}, bf16[4,2,32,256]{3,2,1,0:T(8,128)(2,1)S(1)}, u32[]{:S(2)}, u32[]{:S(2)}) collective-permute-start(bf16[4,2,32,256]{3,2,1,0:T(8,128)(2,1)S(1)} %get-tuple-element.9.refs_2_), channel_id=1, source_target_pairs={{0,4},{1,3},{2,6},{3,1},{4,0},{5,7},{6,2},{7,5},{8,12},{9,11},{10,... | collective-permute-start | bytes 393224 | tf_op jit(solution)/shard_map/ppermute | solution.py:61
  8.1 7.8 %collective-permute-start.6 = (bf16[4,2,32,256]{3,2,1,0:T(8,128)(2,1)S(1)}, bf16[4,2,32,256]{3,2,1,0:T(8,128)(2,1)S(1)}, u32[]{:S(2)}, u32[]{:S(2)}) collective-permute-start(bf16[4,2,32,256]{3,2,1,0:T(8,128)(2,1)S(1)} %get-tuple-element.9.refs_2_), channel_id=1, source_target_pairs={{0,2},{1,7},{2,0},{3,5},{4,6},{5,3},{6,4},{7,1},{8,10},{9,15},{10,... | collective-permute-start | bytes 393224 | tf_op jit(solution)/shard_map/ppermute | solution.py:61
  8.7 6.1 %copy-start = (bf16[1,2,256,2,256]{4,3,2,1,0:T(2,128)(2,1)S(1)}, bf16[1,2,256,2,256]{4,3,2,1,0:T(2,128)(2,1)}, u32[]{:S(2)}) copy-start(bf16[1,2,256,2,256]{4,3,2,1,0:T(2,128)(2,1)} %param.7) | copy-start | bytes 1572868
  12.2 6.0 %collective-permute-start.2 = (bf16[4,2,32,256]{3,2,1,0:T(8,128)(2,1)S(1)}, bf16[4,2,32,256]{3,2,1,0:T(8,128)(2,1)S(1)}, u32[]{:S(2)}, u32[]{:S(2)}) collective-permute-start(bf16[4,2,32,256]{3,2,1,0:T(8,128)(2,1)S(1)} %collective-permute-done.refs_6_), channel_id=1, source_target_pairs={{0,2},{1,3},{2,0},{3,1},{4,6},{5,7},{6,4},{7,5},{8,10},{9,11},{10,... | collective-permute-start | bytes 393224 | tf_op jit(solution)/shard_map/ppermute | solution.py:61
  13.8 6.2 %collective-permute-start.3 = (bf16[4,2,32,256]{3,2,1,0:T(8,128)(2,1)S(1)}, bf16[4,2,32,256]{3,2,1,0:T(8,128)(2,1)S(1)}, u32[]{:S(2)}, u32[]{:S(2)}) collective-permute-start(bf16[4,2,32,256]{3,2,1,0:T(8,128)(2,1)S(1)} %collective-permute-done.refs_6_), channel_id=1, source_target_pairs={{0,4},{1,5},{2,6},{3,7},{4,0},{5,1},{6,2},{7,3},{8,12},{9,13},{10,... | collective-permute-start | bytes 393224 | tf_op jit(solution)/shard_map/ppermute | solution.py:61
  14.9 7.0 %collective-permute-start.7 = (bf16[4,2,32,256]{3,2,1,0:T(8,128)(2,1)S(1)}, bf16[4,2,32,256]{3,2,1,0:T(8,128)(2,1)S(1)}, u32[]{:S(2)}, u32[]{:S(2)}) collective-permute-start(bf16[4,2,32,256]{3,2,1,0:T(8,128)(2,1)S(1)} %collective-permute-done.refs_6_), channel_id=1, source_target_pairs={{0,6},{1,7},{2,4},{3,5},{4,2},{5,3},{6,0},{7,1},{8,14},{9,15},{10,... | collective-permute-start | bytes 393224 | tf_op jit(solution)/shard_map/ppermute | solution.py:61

commit v6 on v5

--- a/solution.py
+++ b/solution.py
@@ -233,8 +233,9 @@
         for term in range(2):
             now = [x.astype(jnp.bfloat16) for x in value]
             value = [x - y.astype(jnp.float32) for x, y in zip(value, now)]
-            out_ref[t, term, 0] = jnp.concatenate([now[0], -now[1]], axis=1)
-            out_ref[t, term, 1] = jnp.concatenate([now[1], now[0]], axis=1)
+            at = slice(term * 2 * order, (term + 1) * 2 * order)
+            out_ref[t, 0, :, at] = jnp.concatenate([now[0], -now[1]], axis=1)
+            out_ref[t, 1, :, at] = jnp.concatenate([now[1], now[0]], axis=1)
 
 
 def last_kernel(nop, rows, order, *refs):
@@ -245,10 +246,11 @@
     if len(refs) > 2:
         piece_ref, loop_ref = refs[1:3]
         piece = jnp.concatenate([piece_ref[:, part].reshape(width, order) for part in range(2)], axis=1)
-        met = loop_ref[...].reshape(-1, 2 * order)
-        found = lax.dot_general(met, piece, (((1,), (1,)), ((), ())), preferred_element_type=jnp.float32)
-        found = found.reshape(times, 2, 2, width, width)
-        tables = [found[t, 0, part] + found[t, 1, part] for t in range(times) for part in range(2)]
+        met = loop_ref[...].reshape(-1, 4 * order)
+        twice = jnp.concatenate([piece, piece], axis=1)
+        found = lax.dot_general(met, twice, (((1,), (1,)), ((), ())), preferred_element_type=jnp.float32)
+        found = found.reshape(times, 2, width, width)
+        tables = [found[t, part] for t in range(times) for part in range(2)]
         left_over = left_over + diagonal_sums(tables, nop, rows)
     height = left_over.shape[0]
     terms = []
@@ -282,7 +284,7 @@
     times, order = product.shape[0], back.shape[2]
     return pl.pallas_call(
         functools.partial(loop_kernel, masks, nop, rows),
-        out_shape=jax.ShapeDtypeStruct((times, 2, 2, nop * rows, 2 * order), jnp.bfloat16),
+        out_shape=jax.ShapeDtypeStruct((times, 2, nop * rows, 4 * order), jnp.bfloat16),
         in_specs=[WHOLE, WHOLE, pl.BlockSpec(memory_space=pl.ANY)],
         out_specs=WHOLE,
         compiler_params=pltpu.CompilerParams(vmem_limit_bytes=VMEM_LIMIT),

time: 23.2 us -> 23.2 us (level)
  no operation moved by 1% of the time
where the time goes in v6:
time: 23.2 us; the launch traced here: 23 us
  starting transfers between devices  11.1 us (48%)
  Pallas kernels  8.39 us (36%)
  waiting for transfers between devices  3.36 us (14%)
    ppermute x7, starting transfers between devices, swap(): return lax.ppermute(array, ('ta', 'sa'), pairs)  10.7 us
    ppermute x7, waiting for transfers between devices, swap(): return lax.ppermute(array, ('ta', 'sa'), pairs)  3.36 us
    pallas_call x1, Pallas kernels, sink_products(): pl.pallas_call(sink_kernel, out_shape=jax.ShapeDtypeStruct((times, 2, 2 *...  2.97 us
    pallas_call x2, Pallas kernels, traces(): pl.pallas_call(functools.partial(trace_kernel, tuple(pieces), known, sums...  2.71 us
    pallas_call x1, Pallas kernels, finish(): pl.pallas_call(functools.partial(last_kernel, nop, rows, order), out_shap...  1.18 us
    pallas_call x1, Pallas kernels, chosen_source_rows(): pl.pallas_call(source_kernel, out_shape=[pltpu.VMEM((nop, bank.shape[3],...  1.05 us
    pallas_call x1, Pallas kernels, loops(): pl.pallas_call(functools.partial(loop_kernel, masks, nop, rows), out_shap...  0.48 us
  transfers between devices with their start and end apart: 8, of which 4 were waited for; matrix products, arithmetic and copies ran while one was open for 0% of the time, Pallas kernels for 31%

profile of v6, /device:TPU:0, one launch (start us, length us, event | category | flops | bytes accessed | tf_op | source)
XLA Modules:
  0.0 23.0 jit_solution(15398959403964711730)
XLA Ops:
  0.0 0.5 %collective-permute-start.1 = (bf16[2,9,128,2,256]{4,3,2,1,0:T(2,128)(2,1)}, bf16[2,9,128,2,256]{4,3,2,1,0:T(2,128)(2,1)S(1)}, u32[]{:S(2)}, u32[]{:S(2)}) collective-permute-start(bf16[2,9,128,2,256]{4,3,2,1,0:T(2,128)(2,1)} %own_ref.1), channel_id=1, source_target_pairs={{0,1},{1,0},{2,3},{3,2},{4,5},{5,4},{6,7},{7,6},{8,9},{9,8},{10,11... | collective-permute-start | bytes 7077896 | tf_op jit(solution)/shard_map/ppermute | solution.py:302
  0.5 1.1 %source_rows.1 = (bf16[4,2,32,256]{3,2,1,0:T(8,128)(2,1)S(1)}, s32[4]{0:T(128)S(4)}) custom-call(s32[4]{0:T(128)} %mom_ref.1, s32[4]{0:T(128)} %disp_ref.1, bf16[1,9,32,2,256]{4,3,2,1,0:T(2,128)(2,1)} %bank_ref.1), custom_call_target="tpu_custom_call" | custom-call | tf_op jit(solution)/shard_map/source_rows/pallas_call | solution.py:35
  1.5 3.7 %collective-permute-start = (bf16[4,2,32,256]{3,2,1,0:T(8,128)(2,1)S(1)}, bf16[4,2,32,256]{3,2,1,0:T(8,128)(2,1)S(1)}, u32[]{:S(2)}, u32[]{:S(2)}) collective-permute-start(bf16[4,2,32,256]{3,2,1,0:T(8,128)(2,1)S(1)} %get-tuple-element.9.refs_2_), channel_id=1, source_target_pairs={{0,8},{1,9},{2,10},{3,11},{4,12},{5,13},{6,14},{7,15},{8,0},{9,1},... | collective-permute-start | bytes 393224 | tf_op jit(solution)/shard_map/ppermute | solution.py:61
  5.2 2.5 %collective-permute-start.4 = (bf16[4,2,32,256]{3,2,1,0:T(8,128)(2,1)S(1)}, bf16[4,2,32,256]{3,2,1,0:T(8,128)(2,1)S(1)}, u32[]{:S(2)}, u32[]{:S(2)}) collective-permute-start(bf16[4,2,32,256]{3,2,1,0:T(8,128)(2,1)S(1)} %get-tuple-element.9.refs_2_), channel_id=1, source_target_pairs={{0,6},{1,5},{2,4},{3,7},{4,2},{5,1},{6,0},{7,3},{8,14},{9,13},{10,... | collective-permute-start | bytes 393224 | tf_op jit(solution)/shard_map/ppermute | solution.py:61
  7.7 0.4 %collective-permute-start.5 = (bf16[4,2,32,256]{3,2,1,0:T(8,128)(2,1)S(1)}, bf16[4,2,32,256]{3,2,1,0:T(8,128)(2,1)S(1)}, u32[]{:S(2)}, u32[]{:S(2)}) collective-permute-start(bf16[4,2,32,256]{3,2,1,0:T(8,128)(2,1)S(1)} %get-tuple-element.9.refs_2_), channel_id=1, source_target_pairs={{0,4},{1,3},{2,6},{3,1},{4,0},{5,7},{6,2},{7,5},{8,12},{9,11},{10,... | collective-permute-start | bytes 393224 | tf_op jit(solution)/shard_map/ppermute | solution.py:61
  8.1 0.5 %collective-permute-start.6 = (bf16[4,2,32,256]{3,2,1,0:T(8,128)(2,1)S(1)}, bf16[4,2,32,256]{3,2,1,0:T(8,128)(2,1)S(1)}, u32[]{:S(2)}, u32[]{:S(2)}) collective-permute-start(bf16[4,2,32,256]{3,2,1,0:T(8,128)(2,1)S(1)} %get-tuple-element.9.refs_2_), channel_id=1, source_target_pairs={{0,2},{1,7},{2,0},{3,5},{4,6},{5,3},{6,4},{7,1},{8,10},{9,15},{10,... | collective-permute-start | bytes 393224 | tf_op jit(solution)/shard_map/ppermute | solution.py:61
  8.7 0.0 collective-permute-done.1.other_ref
  8.7 3.0 %sink_product.1.refs_0_.product_ref = bf16[2,2,512,512]{3,2,1,0:T(8,128)(2,1)S(1)} custom-call(s32[4]{0:T(128)S(4)} %get-tuple-element.10.entry_ref, bf16[2,1,256,2,256]{4,3,2,1,0:T(2,128)(2,1)} %forward_ref.1, bf16[2,9,128,2,256]{4,3,2,1,0:T(2,128)(2,1)} %own_ref.1, bf16[2,9,128,2,256]{4,3,2,1,0:T(2,128)(2,1)S(1)} %collective-permute-done.1.other_ref), custom_call_target="tpu_custom_call" | custom-call | flops 1073741824 | bytes 5242880 | tf_op jit(solution)/shard_map/sink_product/pallas_call | solution.py:103
  11.6 0.6 %collective-permute-done.refs_6_ = bf16[4,2,32,256]{3,2,1,0:T(8,128)(2,1)S(1)} collective-permute-done((bf16[4,2,32,256]{3,2,1,0:T(8,128)(2,1)S(1)}, bf16[4,2,32,256]{3,2,1,0:T(8,128)(2,1)S(1)}, u32[]{:S(2)}, u32[]{:S(2)}) %collective-permute-start) | collective-permute-done | bytes 131104 | tf_op jit(solution)/shard_map/ppermute | solution.py:61
  12.2 1.5 %collective-permute-start.2 = (bf16[4,2,32,256]{3,2,1,0:T(8,128)(2,1)S(1)}, bf16[4,2,32,256]{3,2,1,0:T(8,128)(2,1)S(1)}, u32[]{:S(2)}, u32[]{:S(2)}) collective-permute-start(bf16[4,2,32,256]{3,2,1,0:T(8,128)(2,1)S(1)} %collective-permute-done.refs_6_), channel_id=1, source_target_pairs={{0,2},{1,3},{2,0},{3,1},{4,6},{5,7},{6,4},{7,5},{8,10},{9,11},{10,... | collective-permute-start | bytes 393224 | tf_op jit(solution)/shard_map/ppermute | solution.py:61
  13.8 1.0 %collective-permute-start.3 = (bf16[4,2,32,256]{3,2,1,0:T(8,128)(2,1)S(1)}, bf16[4,2,32,256]{3,2,1,0:T(8,128)(2,1)S(1)}, u32[]{:S(2)}, u32[]{:S(2)}) collective-permute-start(bf16[4,2,32,256]{3,2,1,0:T(8,128)(2,1)S(1)} %collective-permute-done.refs_6_), channel_id=1, source_target_pairs={{0,4},{1,5},{2,6},{3,7},{4,0},{5,1},{6,2},{7,3},{8,12},{9,13},{10,... | collective-permute-start | bytes 393224 | tf_op jit(solution)/shard_map/ppermute | solution.py:61
  14.8 0.0 copy-done
  14.8 0.1 copy.7
  14.9 0.0 collective-permute-done.4.refs_3_
  14.9 1.0 %collective-permute-start.7 = (bf16[4,2,32,256]{3,2,1,0:T(8,128)(2,1)S(1)}, bf16[4,2,32,256]{3,2,1,0:T(8,128)(2,1)S(1)}, u32[]{:S(2)}, u32[]{:S(2)}) collective-permute-start(bf16[4,2,32,256]{3,2,1,0:T(8,128)(2,1)S(1)} %collective-permute-done.refs_6_), channel_id=1, source_target_pairs={{0,6},{1,7},{2,4},{3,5},{4,2},{5,3},{6,0},{7,1},{8,14},{9,15},{10,... | collective-permute-start | bytes 393224 | tf_op jit(solution)/shard_map/ppermute | solution.py:61
  15.9 0.0 collective-permute-done.5.refs_4_
  15.9 0.0 collective-permute-done.6.refs_5_
  15.9 1.8 %traces.1.refs_4_.after_ref = f32[2,256,256]{2,1,0:T(8,128)S(1)} custom-call(bf16[2,2,512,512]{3,2,1,0:T(8,128)(2,1)S(1)} %sink_product.1.refs_0_.product_ref, bf16[2,512,256]{2,1,0:T(8,128)(2,1)S(1)} %bitcast.7, bf16[4,2,32,256]{3,2,1,0:T(8,128)(2,1)S(1)} %get-tuple-element.9.refs_2_, bf16[4,2,32,256]{3,2,1,0:T(8,128)(2,1)S(1)} %collective-permute-done.4.refs_3_, ...), custom_call_target="tpu_custom_call" | custom-call | flops 1342177280 | bytes 4194304 | tf_op jit(solution)/shard_map/traces/pallas_call | solution.py:212
  17.7 0.5 %loops.1.refs_2_ = bf16[2,2,128,1024]{3,2,1,0:T(8,128)(2,1)S(1)} custom-call(bf16[2,2,512,512]{3,2,1,0:T(8,128)(2,1)S(1)} %sink_product.1.refs_0_.product_ref, bf16[2,512,256]{2,1,0:T(8,128)(2,1)S(1)} %bitcast.8, f32[2,256,256]{2,1,0:T(8,128)S(1)} %traces.1.refs_4_.after_ref), custom_call_target="tpu_custom_call" | custom-call | tf_op jit(solution)/shard_map/loops/pallas_call | solution.py:285
  18.1 0.1 collective-permute-done.2.refs_2_
  18.2 1.8 %collective-permute-done.3.refs_3_ = bf16[4,2,32,256]{3,2,1,0:T(8,128)(2,1)S(1)} collective-permute-done((bf16[4,2,32,256]{3,2,1,0:T(8,128)(2,1)S(1)}, bf16[4,2,32,256]{3,2,1,0:T(8,128)(2,1)S(1)}, u32[]{:S(2)}, u32[]{:S(2)}) %collective-permute-start.3) | collective-permute-done | bytes 131104 | tf_op jit(solution)/shard_map/ppermute | solution.py:61
  20.0 1.0 %trace_sums.1.refs_0_ = f32[16,128]{1,0:T(8,128)S(1)} custom-call(bf16[2,2,512,512]{3,2,1,0:T(8,128)(2,1)S(1)} %sink_product.1.refs_0_.product_ref, bf16[2,512,256]{2,1,0:T(8,128)(2,1)S(1)} %bitcast.9, bf16[4,2,32,256]{3,2,1,0:T(8,128)(2,1)S(1)} %collective-permute-done.2.refs_2_, bf16[4,2,32,256]{3,2,1,0:T(8,128)(2,1)S(1)} %collective-permute-done.3.refs_3_, ...), custom_call_target="tpu_custom_call" | custom-call | flops 536870912 | bytes 4194304 | tf_op jit(solution)/shard_map/trace_sums/pallas_call | solution.py:212
  20.9 0.9 %collective-permute-done.7.refs_1_ = bf16[4,2,32,256]{3,2,1,0:T(8,128)(2,1)S(1)} collective-permute-done((bf16[4,2,32,256]{3,2,1,0:T(8,128)(2,1)S(1)}, bf16[4,2,32,256]{3,2,1,0:T(8,128)(2,1)S(1)}, u32[]{:S(2)}, u32[]{:S(2)}) %collective-permute-start.7) | collective-permute-done | bytes 131104 | tf_op jit(solution)/shard_map/ppermute | solution.py:61
  21.8 1.2 %traces_last.1 = f32[2,2,4,4]{3,2,1,0:T(4,128)} custom-call(f32[16,128]{1,0:T(8,128)S(1)} %trace_sums.1.refs_0_, bf16[4,2,32,256]{3,2,1,0:T(8,128)(2,1)S(1)} %collective-permute-done.7.refs_1_, bf16[2,2,128,1024]{3,2,1,0:T(8,128)(2,1)S(1)} %loops.1.refs_2_), custom_call_target="tpu_custom_call" | custom-call | tf_op jit(solution)/shard_map/traces_last/pallas_call | solution.py:273
  (1 shorter events, 0.0 us)
Async XLA Ops:
  0.0 8.7 %collective-permute-start.1 = (bf16[2,9,128,2,256]{4,3,2,1,0:T(2,128)(2,1)}, bf16[2,9,128,2,256]{4,3,2,1,0:T(2,128)(2,1)S(1)}, u32[]{:S(2)}, u32[]{:S(2)}) collective-permute-start(bf16[2,9,128,2,256]{4,3,2,1,0:T(2,128)(2,1)} %own_ref.1), channel_id=1, source_target_pairs={{0,1},{1,0},{2,3},{3,2},{4,5},{5,4},{6,7},{7,6},{8,9},{9,8},{10,11... | collective-permute-start | bytes 7077896 | tf_op jit(solution)/shard_map/ppermute | solution.py:302
  1.5 10.7 %collective-permute-start = (bf16[4,2,32,256]{3,2,1,0:T(8,128)(2,1)S(1)}, bf16[4,2,32,256]{3,2,1,0:T(8,128)(2,1)S(1)}, u32[]{:S(2)}, u32[]{:S(2)}) collective-permute-start(bf16[4,2,32,256]{3,2,1,0:T(8,128)(2,1)S(1)} %get-tuple-element.9.refs_2_), channel_id=1, source_target_pairs={{0,8},{1,9},{2,10},{3,11},{4,12},{5,13},{6,14},{7,15},{8,0},{9,1},... | collective-permute-start | bytes 393224 | tf_op jit(solution)/shard_map/ppermute | solution.py:61
  5.2 9.7 %collective-permute-start.4 = (bf16[4,2,32,256]{3,2,1,0:T(8,128)(2,1)S(1)}, bf16[4,2,32,256]{3,2,1,0:T(8,128)(2,1)S(1)}, u32[]{:S(2)}, u32[]{:S(2)}) collective-permute-start(bf16[4,2,32,256]{3,2,1,0:T(8,128)(2,1)S(1)} %get-tuple-element.9.refs_2_), channel_id=1, source_target_pairs={{0,6},{1,5},{2,4},{3,7},{4,2},{5,1},{6,0},{7,3},{8,14},{9,13},{10,... | collective-permute-start | bytes 393224 | tf_op jit(solution)/shard_map/ppermute | solution.py:61
  7.7 8.2 %collective-permute-start.5 = (bf16[4,2,32,256]{3,2,1,0:T(8,128)(2,1)S(1)}, bf16[4,2,32,256]{3,2,1,0:T(8,128)(2,1)S(1)}, u32[]{:S(2)}, u32[]{:S(2)}) collective-permute-start(bf16[4,2,32,256]{3,2,1,0:T(8,128)(2,1)S(1)} %get-tuple-element.9.refs_2_), channel_id=1, source_target_pairs={{0,4},{1,3},{2,6},{3,1},{4,0},{5,7},{6,2},{7,5},{8,12},{9,11},{10,... | collective-permute-start | bytes 393224 | tf_op jit(solution)/shard_map/ppermute | solution.py:61
  8.1 7.8 %collective-permute-start.6 = (bf16[4,2,32,256]{3,2,1,0:T(8,128)(2,1)S(1)}, bf16[4,2,32,256]{3,2,1,0:T(8,128)(2,1)S(1)}, u32[]{:S(2)}, u32[]{:S(2)}) collective-permute-start(bf16[4,2,32,256]{3,2,1,0:T(8,128)(2,1)S(1)} %get-tuple-element.9.refs_2_), channel_id=1, source_target_pairs={{0,2},{1,7},{2,0},{3,5},{4,6},{5,3},{6,4},{7,1},{8,10},{9,15},{10,... | collective-permute-start | bytes 393224 | tf_op jit(solution)/shard_map/ppermute | solution.py:61
  8.7 6.1 %copy-start = (bf16[1,2,256,2,256]{4,3,2,1,0:T(2,128)(2,1)S(1)}, bf16[1,2,256,2,256]{4,3,2,1,0:T(2,128)(2,1)}, u32[]{:S(2)}) copy-start(bf16[1,2,256,2,256]{4,3,2,1,0:T(2,128)(2,1)} %param.7) | copy-start | bytes 1572868
  12.2 6.0 %collective-permute-start.2 = (bf16[4,2,32,256]{3,2,1,0:T(8,128)(2,1)S(1)}, bf16[4,2,32,256]{3,2,1,0:T(8,128)(2,1)S(1)}, u32[]{:S(2)}, u32[]{:S(2)}) collective-permute-start(bf16[4,2,32,256]{3,2,1,0:T(8,128)(2,1)S(1)} %collective-permute-done.refs_6_), channel_id=1, source_target_pairs={{0,2},{1,3},{2,0},{3,1},{4,6},{5,7},{6,4},{7,5},{8,10},{9,11},{10,... | collective-permute-start | bytes 393224 | tf_op jit(solution)/shard_map/ppermute | solution.py:61
  13.8 6.2 %collective-permute-start.3 = (bf16[4,2,32,256]{3,2,1,0:T(8,128)(2,1)S(1)}, bf16[4,2,32,256]{3,2,1,0:T(8,128)(2,1)S(1)}, u32[]{:S(2)}, u32[]{:S(2)}) collective-permute-start(bf16[4,2,32,256]{3,2,1,0:T(8,128)(2,1)S(1)} %collective-permute-done.refs_6_), channel_id=1, source_target_pairs={{0,4},{1,5},{2,6},{3,7},{4,0},{5,1},{6,2},{7,3},{8,12},{9,13},{10,... | collective-permute-start | bytes 393224 | tf_op jit(solution)/shard_map/ppermute | solution.py:61
  14.9 7.0 %collective-permute-start.7 = (bf16[4,2,32,256]{3,2,1,0:T(8,128)(2,1)S(1)}, bf16[4,2,32,256]{3,2,1,0:T(8,128)(2,1)S(1)}, u32[]{:S(2)}, u32[]{:S(2)}) collective-permute-start(bf16[4,2,32,256]{3,2,1,0:T(8,128)(2,1)S(1)} %collective-permute-done.refs_6_), channel_id=1, source_target_pairs={{0,6},{1,7},{2,4},{3,5},{4,2},{5,3},{6,0},{7,1},{8,14},{9,15},{10,... | collective-permute-start | bytes 393224 | tf_op jit(solution)/shard_map/ppermute | solution.py:61

commit v7 on v5

--- a/solution.py
+++ b/solution.py
@@ -315,7 +315,7 @@
         early = {(0, 0): source} | {m: swap(source, m, n_times) for m in zip(*orders)}
         early[far_mask, far_mask] = far
         far, product = lax.optimization_barrier((far, product))
-        late = {(far_mask ^ m[0], far_mask ^ m[1]): swap(far, m, n_times) for m in zip(near, near)}
+        late = {(far_mask ^ m[0], far_mask ^ m[1]): swap(far, m, n_times) for m in zip(near, near[1:] + near[:1])}
         first = traces(product, back, early, nop, rows)
         last_masks = list(late)[-1]
         end = late.pop(last_masks)

time: 23.2 us -> 23.2 us (level)
  no operation moved by 1% of the time
where the time goes in v7:
time: 23.2 us; the launch traced here: 23 us
  starting transfers between devices  11.1 us (48%)
  Pallas kernels  8.39 us (36%)
  waiting for transfers between devices  3.35 us (14%)
    ppermute x7, starting transfers between devices, swap(): return lax.ppermute(array, ('ta', 'sa'), pairs)  10.7 us
    ppermute x7, waiting for transfers between devices, swap(): return lax.ppermute(array, ('ta', 'sa'), pairs)  3.35 us
    pallas_call x1, Pallas kernels, sink_products(): pl.pallas_call(sink_kernel, out_shape=jax.ShapeDtypeStruct((times, 2, 2 *...  2.97 us
    pallas_call x2, Pallas kernels, traces(): pl.pallas_call(functools.partial(trace_kernel, tuple(pieces), known, sums...  2.71 us
    pallas_call x1, Pallas kernels, finish(): pl.pallas_call(functools.partial(last_kernel, nop, rows, order), out_shap...  1.18 us
    pallas_call x1, Pallas kernels, chosen_source_rows(): pl.pallas_call(source_kernel, out_shape=[pltpu.VMEM((nop, bank.shape[3],...  1.05 us
    pallas_call x1, Pallas kernels, loops(): pl.pallas_call(functools.partial(loop_kernel, masks, nop, rows), out_shap...  0.48 us
  transfers between devices with their start and end apart: 8, of which 4 were waited for; matrix products, arithmetic and copies ran while one was open for 0% of the time, Pallas kernels for 31%

profile of v7, /device:TPU:0, one launch (start us, length us, event | category | flops | bytes accessed | tf_op | source)
XLA Modules:
  0.0 23.0 jit_solution(16988668072958031553)
XLA Ops:
  0.0 0.5 %collective-permute-start.1 = (bf16[2,9,128,2,256]{4,3,2,1,0:T(2,128)(2,1)}, bf16[2,9,128,2,256]{4,3,2,1,0:T(2,128)(2,1)S(1)}, u32[]{:S(2)}, u32[]{:S(2)}) collective-permute-start(bf16[2,9,128,2,256]{4,3,2,1,0:T(2,128)(2,1)} %own_ref.1), channel_id=1, source_target_pairs={{0,1},{1,0},{2,3},{3,2},{4,5},{5,4},{6,7},{7,6},{8,9},{9,8},{10,11... | collective-permute-start | bytes 7077896 | tf_op jit(solution)/shard_map/ppermute | solution.py:300
  0.5 1.1 %source_rows.1 = (bf16[4,2,32,256]{3,2,1,0:T(8,128)(2,1)S(1)}, s32[4]{0:T(128)S(4)}) custom-call(s32[4]{0:T(128)} %mom_ref.1, s32[4]{0:T(128)} %disp_ref.1, bf16[1,9,32,2,256]{4,3,2,1,0:T(2,128)(2,1)} %bank_ref.1), custom_call_target="tpu_custom_call" | custom-call | tf_op jit(solution)/shard_map/source_rows/pallas_call | solution.py:35
  1.5 3.7 %collective-permute-start = (bf16[4,2,32,256]{3,2,1,0:T(8,128)(2,1)S(1)}, bf16[4,2,32,256]{3,2,1,0:T(8,128)(2,1)S(1)}, u32[]{:S(2)}, u32[]{:S(2)}) collective-permute-start(bf16[4,2,32,256]{3,2,1,0:T(8,128)(2,1)S(1)} %get-tuple-element.9.refs_2_), channel_id=1, source_target_pairs={{0,8},{1,9},{2,10},{3,11},{4,12},{5,13},{6,14},{7,15},{8,0},{9,1},... | collective-permute-start | bytes 393224 | tf_op jit(solution)/shard_map/ppermute | solution.py:61
  5.2 2.5 %collective-permute-start.4 = (bf16[4,2,32,256]{3,2,1,0:T(8,128)(2,1)S(1)}, bf16[4,2,32,256]{3,2,1,0:T(8,128)(2,1)S(1)}, u32[]{:S(2)}, u32[]{:S(2)}) collective-permute-start(bf16[4,2,32,256]{3,2,1,0:T(8,128)(2,1)S(1)} %get-tuple-element.9.refs_2_), channel_id=1, source_target_pairs={{0,6},{1,5},{2,4},{3,7},{4,2},{5,1},{6,0},{7,3},{8,14},{9,13},{10,... | collective-permute-start | bytes 393224 | tf_op jit(solution)/shard_map/ppermute | solution.py:61
  7.7 0.4 %collective-permute-start.5 = (bf16[4,2,32,256]{3,2,1,0:T(8,128)(2,1)S(1)}, bf16[4,2,32,256]{3,2,1,0:T(8,128)(2,1)S(1)}, u32[]{:S(2)}, u32[]{:S(2)}) collective-permute-start(bf16[4,2,32,256]{3,2,1,0:T(8,128)(2,1)S(1)} %get-tuple-element.9.refs_2_), channel_id=1, source_target_pairs={{0,4},{1,3},{2,6},{3,1},{4,0},{5,7},{6,2},{7,5},{8,12},{9,11},{10,... | collective-permute-start | bytes 393224 | tf_op jit(solution)/shard_map/ppermute | solution.py:61
  8.1 0.5 %collective-permute-start.6 = (bf16[4,2,32,256]{3,2,1,0:T(8,128)(2,1)S(1)}, bf16[4,2,32,256]{3,2,1,0:T(8,128)(2,1)S(1)}, u32[]{:S(2)}, u32[]{:S(2)}) collective-permute-start(bf16[4,2,32,256]{3,2,1,0:T(8,128)(2,1)S(1)} %get-tuple-element.9.refs_2_), channel_id=1, source_target_pairs={{0,2},{1,7},{2,0},{3,5},{4,6},{5,3},{6,4},{7,1},{8,10},{9,15},{10,... | collective-permute-start | bytes 393224 | tf_op jit(solution)/shard_map/ppermute | solution.py:61
  8.7 0.0 collective-permute-done.1.other_ref
  8.7 3.0 %sink_product.1.refs_0_.product_ref = bf16[2,2,512,512]{3,2,1,0:T(8,128)(2,1)S(1)} custom-call(s32[4]{0:T(128)S(4)} %get-tuple-element.10.entry_ref, bf16[2,1,256,2,256]{4,3,2,1,0:T(2,128)(2,1)} %forward_ref.1, bf16[2,9,128,2,256]{4,3,2,1,0:T(2,128)(2,1)} %own_ref.1, bf16[2,9,128,2,256]{4,3,2,1,0:T(2,128)(2,1)S(1)} %collective-permute-done.1.other_ref), custom_call_target="tpu_custom_call" | custom-call | flops 1073741824 | bytes 5242880 | tf_op jit(solution)/shard_map/sink_product/pallas_call | solution.py:103
  11.6 0.6 %collective-permute-done.refs_6_ = bf16[4,2,32,256]{3,2,1,0:T(8,128)(2,1)S(1)} collective-permute-done((bf16[4,2,32,256]{3,2,1,0:T(8,128)(2,1)S(1)}, bf16[4,2,32,256]{3,2,1,0:T(8,128)(2,1)S(1)}, u32[]{:S(2)}, u32[]{:S(2)}) %collective-permute-start) | collective-permute-done | bytes 131104 | tf_op jit(solution)/shard_map/ppermute | solution.py:61
  12.2 1.5 %collective-permute-start.2 = (bf16[4,2,32,256]{3,2,1,0:T(8,128)(2,1)S(1)}, bf16[4,2,32,256]{3,2,1,0:T(8,128)(2,1)S(1)}, u32[]{:S(2)}, u32[]{:S(2)}) collective-permute-start(bf16[4,2,32,256]{3,2,1,0:T(8,128)(2,1)S(1)} %collective-permute-done.refs_6_), channel_id=1, source_target_pairs={{0,2},{1,5},{2,0},{3,7},{4,6},{5,1},{6,4},{7,3},{8,10},{9,13},{10,... | collective-permute-start | bytes 393224 | tf_op jit(solution)/shard_map/ppermute | solution.py:61
  13.8 1.0 %collective-permute-start.3 = (bf16[4,2,32,256]{3,2,1,0:T(8,128)(2,1)S(1)}, bf16[4,2,32,256]{3,2,1,0:T(8,128)(2,1)S(1)}, u32[]{:S(2)}, u32[]{:S(2)}) collective-permute-start(bf16[4,2,32,256]{3,2,1,0:T(8,128)(2,1)S(1)} %collective-permute-done.refs_6_), channel_id=1, source_target_pairs={{0,4},{1,7},{2,6},{3,5},{4,0},{5,3},{6,2},{7,1},{8,12},{9,15},{10,... | collective-permute-start | bytes 393224 | tf_op jit(solution)/shard_map/ppermute | solution.py:61
  14.8 0.0 copy-done
  14.8 0.1 copy.7
  14.9 0.0 collective-permute-done.4.refs_3_
  14.9 1.0 %collective-permute-start.7 = (bf16[4,2,32,256]{3,2,1,0:T(8,128)(2,1)S(1)}, bf16[4,2,32,256]{3,2,1,0:T(8,128)(2,1)S(1)}, u32[]{:S(2)}, u32[]{:S(2)}) collective-permute-start(bf16[4,2,32,256]{3,2,1,0:T(8,128)(2,1)S(1)} %collective-permute-done.refs_6_), channel_id=1, source_target_pairs={{0,6},{1,3},{2,4},{3,1},{4,2},{5,7},{6,0},{7,5},{8,14},{9,11},{10,... | collective-permute-start | bytes 393224 | tf_op jit(solution)/shard_map/ppermute | solution.py:61
  15.9 0.4 %collective-permute-done.5.refs_4_ = bf16[4,2,32,256]{3,2,1,0:T(8,128)(2,1)S(1)} collective-permute-done((bf16[4,2,32,256]{3,2,1,0:T(8,128)(2,1)S(1)}, bf16[4,2,32,256]{3,2,1,0:T(8,128)(2,1)S(1)}, u32[]{:S(2)}, u32[]{:S(2)}) %collective-permute-start.5) | collective-permute-done | bytes 131104 | tf_op jit(solution)/shard_map/ppermute | solution.py:61
  16.3 0.0 collective-permute-done.6.refs_5_
  16.3 1.8 %traces.1.refs_4_.after_ref = f32[2,256,256]{2,1,0:T(8,128)S(1)} custom-call(bf16[2,2,512,512]{3,2,1,0:T(8,128)(2,1)S(1)} %sink_product.1.refs_0_.product_ref, bf16[2,512,256]{2,1,0:T(8,128)(2,1)S(1)} %bitcast.7, bf16[4,2,32,256]{3,2,1,0:T(8,128)(2,1)S(1)} %get-tuple-element.9.refs_2_, bf16[4,2,32,256]{3,2,1,0:T(8,128)(2,1)S(1)} %collective-permute-done.4.refs_3_, ...), custom_call_target="tpu_custom_call" | custom-call | flops 1342177280 | bytes 4194304 | tf_op jit(solution)/shard_map/traces/pallas_call | solution.py:212
  18.1 0.5 %loops.1.refs_2_ = bf16[2,2,2,128,512]{4,3,2,1,0:T(8,128)(2,1)S(1)} custom-call(bf16[2,2,512,512]{3,2,1,0:T(8,128)(2,1)S(1)} %sink_product.1.refs_0_.product_ref, bf16[2,512,256]{2,1,0:T(8,128)(2,1)S(1)} %bitcast.8, f32[2,256,256]{2,1,0:T(8,128)S(1)} %traces.1.refs_4_.after_ref), custom_call_target="tpu_custom_call" | custom-call | tf_op jit(solution)/shard_map/loops/pallas_call | solution.py:283
  18.6 0.0 collective-permute-done.2.refs_2_
  18.6 1.2 %collective-permute-done.3.refs_3_ = bf16[4,2,32,256]{3,2,1,0:T(8,128)(2,1)S(1)} collective-permute-done((bf16[4,2,32,256]{3,2,1,0:T(8,128)(2,1)S(1)}, bf16[4,2,32,256]{3,2,1,0:T(8,128)(2,1)S(1)}, u32[]{:S(2)}, u32[]{:S(2)}) %collective-permute-start.3) | collective-permute-done | bytes 131104 | tf_op jit(solution)/shard_map/ppermute | solution.py:61
  19.8 1.0 %trace_sums.1.refs_0_ = f32[16,128]{1,0:T(8,128)S(1)} custom-call(bf16[2,2,512,512]{3,2,1,0:T(8,128)(2,1)S(1)} %sink_product.1.refs_0_.product_ref, bf16[2,512,256]{2,1,0:T(8,128)(2,1)S(1)} %bitcast.9, bf16[4,2,32,256]{3,2,1,0:T(8,128)(2,1)S(1)} %collective-permute-done.2.refs_2_, bf16[4,2,32,256]{3,2,1,0:T(8,128)(2,1)S(1)} %collective-permute-done.3.refs_3_, ...), custom_call_target="tpu_custom_call" | custom-call | flops 536870912 | bytes 4194304 | tf_op jit(solution)/shard_map/trace_sums/pallas_call | solution.py:212
  20.7 1.1 %collective-permute-done.7.refs_1_ = bf16[4,2,32,256]{3,2,1,0:T(8,128)(2,1)S(1)} collective-permute-done((bf16[4,2,32,256]{3,2,1,0:T(8,128)(2,1)S(1)}, bf16[4,2,32,256]{3,2,1,0:T(8,128)(2,1)S(1)}, u32[]{:S(2)}, u32[]{:S(2)}) %collective-permute-start.7) | collective-permute-done | bytes 131104 | tf_op jit(solution)/shard_map/ppermute | solution.py:61
  21.8 1.2 %traces_last.1 = f32[2,2,4,4]{3,2,1,0:T(4,128)} custom-call(f32[16,128]{1,0:T(8,128)S(1)} %trace_sums.1.refs_0_, bf16[4,2,32,256]{3,2,1,0:T(8,128)(2,1)S(1)} %collective-permute-done.7.refs_1_, bf16[2,2,2,128,512]{4,3,2,1,0:T(8,128)(2,1)S(1)} %loops.1.refs_2_), custom_call_target="tpu_custom_call" | custom-call | tf_op jit(solution)/shard_map/traces_last/pallas_call | solution.py:271
  (1 shorter events, 0.0 us)
Async XLA Ops:
  0.0 8.7 %collective-permute-start.1 = (bf16[2,9,128,2,256]{4,3,2,1,0:T(2,128)(2,1)}, bf16[2,9,128,2,256]{4,3,2,1,0:T(2,128)(2,1)S(1)}, u32[]{:S(2)}, u32[]{:S(2)}) collective-permute-start(bf16[2,9,128,2,256]{4,3,2,1,0:T(2,128)(2,1)} %own_ref.1), channel_id=1, source_target_pairs={{0,1},{1,0},{2,3},{3,2},{4,5},{5,4},{6,7},{7,6},{8,9},{9,8},{10,11... | collective-permute-start | bytes 7077896 | tf_op jit(solution)/shard_map/ppermute | solution.py:300
  1.5 10.7 %collective-permute-start = (bf16[4,2,32,256]{3,2,1,0:T(8,128)(2,1)S(1)}, bf16[4,2,32,256]{3,2,1,0:T(8,128)(2,1)S(1)}, u32[]{:S(2)}, u32[]{:S(2)}) collective-permute-start(bf16[4,2,32,256]{3,2,1,0:T(8,128)(2,1)S(1)} %get-tuple-element.9.refs_2_), channel_id=1, source_target_pairs={{0,8},{1,9},{2,10},{3,11},{4,12},{5,13},{6,14},{7,15},{8,0},{9,1},... | collective-permute-start | bytes 393224 | tf_op jit(solution)/shard_map/ppermute | solution.py:61
  5.2 9.7 %collective-permute-start.4 = (bf16[4,2,32,256]{3,2,1,0:T(8,128)(2,1)S(1)}, bf16[4,2,32,256]{3,2,1,0:T(8,128)(2,1)S(1)}, u32[]{:S(2)}, u32[]{:S(2)}) collective-permute-start(bf16[4,2,32,256]{3,2,1,0:T(8,128)(2,1)S(1)} %get-tuple-element.9.refs_2_), channel_id=1, source_target_pairs={{0,6},{1,5},{2,4},{3,7},{4,2},{5,1},{6,0},{7,3},{8,14},{9,13},{10,... | collective-permute-start | bytes 393224 | tf_op jit(solution)/shard_map/ppermute | solution.py:61
  7.7 8.7 %collective-permute-start.5 = (bf16[4,2,32,256]{3,2,1,0:T(8,128)(2,1)S(1)}, bf16[4,2,32,256]{3,2,1,0:T(8,128)(2,1)S(1)}, u32[]{:S(2)}, u32[]{:S(2)}) collective-permute-start(bf16[4,2,32,256]{3,2,1,0:T(8,128)(2,1)S(1)} %get-tuple-element.9.refs_2_), channel_id=1, source_target_pairs={{0,4},{1,3},{2,6},{3,1},{4,0},{5,7},{6,2},{7,5},{8,12},{9,11},{10,... | collective-permute-start | bytes 393224 | tf_op jit(solution)/shard_map/ppermute | solution.py:61
  8.1 8.2 %collective-permute-start.6 = (bf16[4,2,32,256]{3,2,1,0:T(8,128)(2,1)S(1)}, bf16[4,2,32,256]{3,2,1,0:T(8,128)(2,1)S(1)}, u32[]{:S(2)}, u32[]{:S(2)}) collective-permute-start(bf16[4,2,32,256]{3,2,1,0:T(8,128)(2,1)S(1)} %get-tuple-element.9.refs_2_), channel_id=1, source_target_pairs={{0,2},{1,7},{2,0},{3,5},{4,6},{5,3},{6,4},{7,1},{8,10},{9,15},{10,... | collective-permute-start | bytes 393224 | tf_op jit(solution)/shard_map/ppermute | solution.py:61
  8.7 6.1 %copy-start = (bf16[1,2,256,2,256]{4,3,2,1,0:T(2,128)(2,1)S(1)}, bf16[1,2,256,2,256]{4,3,2,1,0:T(2,128)(2,1)}, u32[]{:S(2)}) copy-start(bf16[1,2,256,2,256]{4,3,2,1,0:T(2,128)(2,1)} %param.7) | copy-start | bytes 1572868
  12.2 6.3 %collective-permute-start.2 = (bf16[4,2,32,256]{3,2,1,0:T(8,128)(2,1)S(1)}, bf16[4,2,32,256]{3,2,1,0:T(8,128)(2,1)S(1)}, u32[]{:S(2)}, u32[]{:S(2)}) collective-permute-start(bf16[4,2,32,256]{3,2,1,0:T(8,128)(2,1)S(1)} %collective-permute-done.refs_6_), channel_id=1, source_target_pairs={{0,2},{1,5},{2,0},{3,7},{4,6},{5,1},{6,4},{7,3},{8,10},{9,13},{10,... | collective-permute-start | bytes 393224 | tf_op jit(solution)/shard_map/ppermute | solution.py:61
  13.8 6.0 %collective-permute-start.3 = (bf16[4,2,32,256]{3,2,1,0:T(8,128)(2,1)S(1)}, bf16[4,2,32,256]{3,2,1,0:T(8,128)(2,1)S(1)}, u32[]{:S(2)}, u32[]{:S(2)}) collective-permute-start(bf16[4,2,32,256]{3,2,1,0:T(8,128)(2,1)S(1)} %collective-permute-done.refs_6_), channel_id=1, source_target_pairs={{0,4},{1,7},{2,6},{3,5},{4,0},{5,3},{6,2},{7,1},{8,12},{9,15},{10,... | collective-permute-start | bytes 393224 | tf_op jit(solution)/shard_map/ppermute | solution.py:61
  14.9 7.0 %collective-permute-start.7 = (bf16[4,2,32,256]{3,2,1,0:T(8,128)(2,1)S(1)}, bf16[4,2,32,256]{3,2,1,0:T(8,128)(2,1)S(1)}, u32[]{:S(2)}, u32[]{:S(2)}) collective-permute-start(bf16[4,2,32,256]{3,2,1,0:T(8,128)(2,1)S(1)} %collective-permute-done.refs_6_), channel_id=1, source_target_pairs={{0,6},{1,3},{2,4},{3,1},{4,2},{5,7},{6,0},{7,5},{8,14},{9,11},{10,... | collective-permute-start | bytes 393224 | tf_op jit(solution)/shard_map/ppermute | solution.py:61
